TPU v7x, 128 devices: a whole 4x4x4 slice. The times are simulated.
128 devices in a mesh: prow: 8 (over x, core), pcol: 16 (over y, z).
Axes of the slice: x: 4, y: 4, z: 4, core: 2. Of those that a mesh axis runs over, the one named last changes fastest.
Arguments:
- z_block: float32 [131072, 2048], P('prow', 'pcol'), may hold values from -6 to 6
- v_panels: bfloat16 [2, 131072, 512], P(None, 'prow', 'pcol'), may hold values from -0.015625 to 0.015625
- t_panels: float32 [2, 512, 512], replicated, as said below
Outputs:
- eigen_out: float32 [131072, 2048], P('prow', 'pcol')
Inputs may be any that keep to these rules, and one draw needn't show every extreme that they name: Each panel of t_panels is upper triangular with a positive diagonal.
All inputs are finite; a program needn't handle non-finite values.
Results may differ from a plain program's by a relative error of at most 0.0045.
Values may be sent and summed in bfloat16 or wider, within the bound.
No kernel may reach another device: no remote copies, remote signals or barrier semaphores. Data moves between devices by JAX's collectives and lax.ppermute only.
A program may use at most 128 MiB of HBM per device.

v0:
```python
import jax
import jax.numpy as jnp
from jax import lax
from jax.sharding import PartitionSpec as P


def local(z_block, v_panels, t_panels):
    vectors = z_block
    for which_panel in range(2):
        reflectors = lax.all_gather(v_panels[which_panel], "pcol", axis=1, tiled=True)
        rounded = vectors.astype(jnp.bfloat16)
        partial_value = lax.dot_general(
            reflectors, rounded, (((0,), (0,)), ((), ())), preferred_element_type=jnp.float32
        )
        factor = t_panels[which_panel].T
        summed = lax.psum(partial_value, "prow")
        coeffs = jnp.dot(factor, summed, precision=lax.Precision.HIGHEST).astype(jnp.bfloat16)
        vectors = vectors - jnp.dot(reflectors, coeffs, preferred_element_type=jnp.float32)
    return vectors


def solution(mesh):
    return jax.shard_map(
        local,
        mesh=mesh,
        in_specs=(P("prow", "pcol"), P(None, "prow", "pcol"), P()),
        out_specs=P("prow", "pcol"),
        check_vma=False,
    )
```

profile of v0, /device:TPU:0, one launch (start us, length us, event | category | flops | bytes accessed | tf_op | source)
XLA Modules:
  0.0 412.2 jit_solution(4683304289632662624)
XLA Ops:
  6.5 0.0 all-gather.5.cloned.1.call-start
  6.5 3.0 fusion.19
  9.5 0.0 all-gather.5.cloned.1.call-update
  9.6 0.0 all-reduce.3.cloned.1.call-start
  9.6 114.0 %all-gather.5.cloned.1.call-done = bf16[1,16384,512]{1,2,0:T(8,128)(2,1)} async-done(((bf16[1,16384,32]{1,2,0:T(8,128)(2,1)}), bf16[1,16384,512]{1,2,0:T(8,128)(2,1)}) %all-gather.5.cloned.1.call-update) | async-done | bytes 16777232 | tf_op jit(solution)/shard_map/all_gather | solution.py:10
  123.6 13.3 %fusion.6 = f32[512,128]{1,0:T(8,128)} fusion(bf16[1,16384,512]{1,2,0:T(8,128)(2,1)} %all-gather.5.cloned.1.call-done, f32[16384,128]{1,0:T(8,128)} %param.3), kind=kOutput, calls=%fused_computation.8 | convolution fusion | flops 2149580800 | bytes 25427968 | tf_op jit(solution)/shard_map/dot_general | solution.py:12
  137.0 0.0 all-reduce.3.cloned.1.call-update
  137.0 0.0 all-gather.7.cloned.1.call-start
  137.1 0.7 all-gather.7.cloned.1.call-update
  137.7 0.0 copy-start
  137.8 0.2 all-reduce.5.cloned.1.call-start
  138.0 9.1 %copy.4 = f32[16384,128]{0,1:T(8,128)} copy(f32[16384,128]{1,0:T(8,128)} %param.3) | data formatting | bytes 16777216 | tf_op args[0]
  147.1 49.3 %all-reduce.3.cloned.1.call-done = f32[512,128]{1,0:T(8,128)} async-done(((f32[512,128]{1,0:T(8,128)}), f32[512,128]{1,0:T(8,128)}) %all-reduce.3.cloned.1.call-update) | async-done | bytes 262160 | tf_op jit(solution)/shard_map/psum | solution.py:16
  196.4 0.0 copy-done
  196.5 1.7 convolution_convert_fusion.1
  198.2 14.0 %fusion = f32[16384,128]{0,1:T(8,128)} fusion(f32[16384,128]{0,1:T(8,128)} %copy.4, bf16[128,512]{1,0:T(8,128)(2,1)S(1)} %convolution_convert_fusion.1, bf16[1,16384,512]{1,2,0:T(8,128)(2,1)} %all-gather.5.cloned.1.call-done), kind=kOutput, calls=%fused_computation.2 | convolution fusion | flops 2149580800 | bytes 33685504 | tf_op jit(solution)/shard_map/dot_general | solution.py:18
  212.1 97.3 %all-gather.7.cloned.1.call-done = bf16[1,16384,512]{1,2,0:T(8,128)(2,1)} async-done(((bf16[1,16384,32]{1,2,0:T(8,128)(2,1)}), bf16[1,16384,512]{1,2,0:T(8,128)(2,1)}) %all-gather.7.cloned.1.call-update) | async-done | bytes 16777232 | tf_op jit(solution)/shard_map/all_gather | solution.py:10
  309.5 12.3 %fusion.10 = f32[512,128]{0,1:T(8,128)} fusion(bf16[1,16384,512]{1,2,0:T(8,128)(2,1)} %all-gather.7.cloned.1.call-done, f32[16384,128]{0,1:T(8,128)} %fusion), kind=kOutput, calls=%fused_computation.12 | convolution fusion | flops 2149580800 | bytes 25427968 | tf_op jit(solution)/shard_map/dot_general | solution.py:12
  321.7 0.0 all-reduce.5.cloned.1.call-update
  321.8 59.5 %all-reduce.5.cloned.1.call-done = f32[512,128]{0,1:T(8,128)} async-done(((f32[512,128]{0,1:T(8,128)}), f32[512,128]{0,1:T(8,128)}) %all-reduce.5.cloned.1.call-update) | async-done | bytes 262160 | tf_op jit(solution)/shard_map/psum | solution.py:16
  381.2 1.7 convolution_convert_fusion
  382.9 13.8 %fusion.1 = f32[16384,128]{0,1:T(8,128)} fusion(f32[16384,128]{0,1:T(8,128)} %fusion, bf16[128,512]{1,0:T(8,128)(2,1)S(1)} %convolution_convert_fusion, bf16[1,16384,512]{1,2,0:T(8,128)(2,1)} %all-gather.7.cloned.1.call-done), kind=kOutput, calls=%fused_computation.3 | convolution fusion | flops 2149580800 | bytes 33685504 | tf_op jit(solution)/shard_map/dot_general | solution.py:18
  396.7 9.0 %copy.5 = f32[16384,128]{1,0:T(8,128)} copy(f32[16384,128]{0,1:T(8,128)} %fusion.1) | data formatting | bytes 16777216 | tf_op jit(solution)/shard_map/sub | solution.py:18
Async XLA Ops:
  6.5 117.1 %all-gather.5.cloned.1.call-start = ((), (), s32[]{:S(2)}) async-start(), calls=%async_computation.2 | async-start | bytes 17825792 | tf_op jit(solution)/shard_map/all_gather | solution.py:10
  9.6 186.9 %all-reduce.3.cloned.1.call-start = ((), (), s32[]{:S(2)}) async-start(), calls=%async_computation | async-start | bytes 524288 | tf_op jit(solution)/shard_map/psum | solution.py:16
  137.0 172.4 %all-gather.7.cloned.1.call-start = ((), (), s32[]{:S(2)}) async-start(), calls=%async_computation.3 | async-start | bytes 17825792 | tf_op jit(solution)/shard_map/all_gather | solution.py:10
  137.7 58.7 %copy-start = (f32[2,512,512]{2,1,0:T(8,128)S(1)}, f32[2,512,512]{2,1,0:T(8,128)}, u32[]{:S(2)}) copy-start(f32[2,512,512]{2,1,0:T(8,128)} %param.5) | copy-start | bytes 6291460
  137.8 243.5 %all-reduce.5.cloned.1.call-start = ((), (), s32[]{:S(2)}) async-start(), calls=%async_computation.1 | async-start | bytes 524288 | tf_op jit(solution)/shard_map/psum | solution.py:16
Sparse Core Ops, SparseCore 0:
  9.7 113.9 all-gather.4
  137.1 59.2 all-reduce.2
  198.8 110.5 all-gather.6
  321.9 59.2 all-reduce.4
where the time goes:
time: 413 us; the launch traced here: 412 us
  waiting for transfers between devices  321 us (78%)
  matrix products  56.7 us (14%)
  local copies, waits for them, and re-layouts  21.1 us (5%)
  between operations  13.2 us (3%)
    all_gather x2, waiting for transfers between devices, local(): lax.all_gather(v_panels[which_panel], 'pcol', axis=1, tiled=True)  211 us
    psum x2, waiting for transfers between devices, local(): summed = lax.psum(partial_value, 'prow')  109 us
    dot_general x2, matrix products, local(): jnp.dot(reflectors, coeffs, preferred_element_type=jnp.float32)  27.7 us
    dot_general x2, matrix products, local(): lax.dot_general(reflectors, rounded, (((0,), (0,)), ((), ())), preferred_...  25.6 us
    unnamed x3, local copies, waits for them, and re-layouts  9.13 us
    sub x1, local copies, waits for them, and re-layouts, local(): vectors - jnp.dot(reflectors, coeffs, preferred_element_type=jnp.float32)  8.98 us
  transfers between devices with their start and end apart: 4, of which 4 were waited for; matrix products, arithmetic and copies ran while one was open for 6% of the time, Pallas kernels for 0%

commit v1 on v0

v1 whole, which is shorter than its diff:
```python
import functools

import jax
import jax.numpy as jnp
from jax import lax
from jax.experimental import pallas as pl
from jax.experimental.pallas import tpu as pltpu
from jax.sharding import PartitionSpec as P

RING = 4
BF16, F32 = jnp.bfloat16, jnp.float32
AXES = ("prow", "pcol")


def device(x, core, y, z):
    return (x * 2 + core) * RING * RING + y * RING + z


def permutation(target):
    pairs = []
    for x in range(RING):
        for core in range(2):
            for y in range(RING):
                for z in range(RING):
                    pairs.append((device(x, core, y, z), device(*target(x, core, y, z))))
    return pairs


def along_u(s):
    return permutation(lambda x, c, y, z: (x, c, (y + s) % RING, z) if c == 0 else (x, c, y, (z + s) % RING))


def along_w(s):
    return permutation(lambda x, c, y, z: (x, c, y, (z + s) % RING) if c == 0 else (x, c, (y + s) % RING, z))


def along_x(s):
    return permutation(lambda x, c, y, z: ((x + s) % RING, c, y, z))


def other_core():
    return permutation(lambda x, c, y, z: (x, 1 - c, y, z))


def send(value, pairs):
    return lax.ppermute(value, AXES, pairs)


def params(mib=48):
    return pltpu.CompilerParams(vmem_limit_bytes=mib * 2**20)


def cost(flops, nbytes):
    return pl.CostEstimate(flops=flops, bytes_accessed=nbytes, transcendentals=0)


def stack_kernel(place, *refs):
    out = refs[-1]
    width = refs[0].shape[0]
    for s in range(RING):
        at = lax.rem(place[0] - s + RING, RING)
        out[pl.ds(pl.multiple_of(at * width, width), width), :] = refs[s][...]


def stack(place, blocks):
    width, rows = blocks[0].shape
    tile = rows // 4
    return pl.pallas_call(
        stack_kernel,
        grid_spec=pltpu.PrefetchScalarGridSpec(
            num_scalar_prefetch=1,
            grid=(rows // tile,),
            in_specs=[pl.BlockSpec((width, tile), lambda i, place: (0, i))] * RING,
            out_specs=pl.BlockSpec((RING * width, tile), lambda i, place: (0, i)),
        ),
        out_shape=jax.ShapeDtypeStruct((RING * width, rows), BF16),
        compiler_params=params(),
        cost_estimate=cost(0, 4 * RING * width * rows),
        name="stack_reflectors",
    )(place, *blocks)


def transpose_kernel(*refs):
    out = refs[-1]
    width = refs[0].shape[0]
    for t in range(RING):
        out[:, t * width:(t + 1) * width] = refs[t][...].T


def transpose(blocks):
    width, rows = blocks[0].shape
    tile = 512
    return pl.pallas_call(
        transpose_kernel,
        grid=(rows // tile,),
        in_specs=[pl.BlockSpec((width, tile), lambda i: (0, i))] * RING,
        out_specs=pl.BlockSpec((tile, RING * width), lambda i: (i, 0)),
        out_shape=jax.ShapeDtypeStruct((rows, RING * width), BF16),
        compiler_params=params(),
        cost_estimate=cost(0, 4 * RING * width * rows),
        name="transpose_reflectors",
    )(*blocks)


def first_sums_kernel(*refs):
    v, z, outs, total = refs[:4], refs[4:8], refs[8:12], refs[12]
    step = pl.program_id(0)

    @pl.when(step == 0)
    def _():
        total[...] = jnp.zeros_like(total)

    left = jnp.concatenate([r[...] for r in v], axis=0)
    right = jnp.concatenate([r[...] for r in z], axis=1)
    total[...] += jnp.dot(left, right, preferred_element_type=F32)

    @pl.when(step == pl.num_programs(0) - 1)
    def _():
        for s in range(RING):
            outs[s][...] = total[:, s * 128:(s + 1) * 128].astype(outs[s].dtype)


def second_sums_kernel(*refs):
    v, z, flat, coeffs, outs, total = refs[:4], refs[4:8], refs[8], refs[9:13], refs[13:17], refs[17]
    step = pl.program_id(0)

    @pl.when(step == 0)
    def _():
        total[...] = jnp.zeros_like(total)

    left = jnp.concatenate([r[...] for r in v], axis=0)
    old = jnp.concatenate([r[...] for r in z], axis=1).astype(F32)
    w = jnp.concatenate([r[...] for r in coeffs], axis=1)
    right = (old - jnp.dot(flat[...], w, preferred_element_type=F32)).astype(BF16)
    total[...] += jnp.dot(left, right, preferred_element_type=F32)

    @pl.when(step == pl.num_programs(0) - 1)
    def _():
        for s in range(RING):
            outs[s][...] = total[:, s * 128:(s + 1) * 128].astype(outs[s].dtype)


def sums(v, z, flat=None, coeffs=None):
    width, rows = v[0].shape
    columns = z[0].shape[1]
    nb = RING * width
    tile = 512
    in_specs = [pl.BlockSpec((width, tile), lambda i: (0, i))] * RING
    in_specs += [pl.BlockSpec((tile, columns), lambda i: (i, 0))] * RING
    args = list(v) + list(z)
    if flat is not None:
        in_specs += [pl.BlockSpec((tile, nb), lambda i: (i, 0))]
        in_specs += [pl.BlockSpec((nb, columns), lambda i: (0, 0))] * RING
        args += [flat] + list(coeffs)
    return pl.pallas_call(
        first_sums_kernel if flat is None else second_sums_kernel,
        grid=(rows // tile,),
        in_specs=in_specs,
        out_specs=[pl.BlockSpec((nb, columns), lambda i: (0, 0))] * RING,
        out_shape=[jax.ShapeDtypeStruct((nb, columns), F32 if s == 0 else BF16) for s in range(RING)],
        scratch_shapes=[pltpu.VMEM((nb, RING * columns), F32)],
        compiler_params=params(),
        cost_estimate=cost(2 * nb * rows * RING * columns * (1 if flat is None else 2), 4 * nb * rows),
        name="panel_sums",
    )(*args)


def add_cores_kernel(place, mine, theirs, out):
    u, w = place[0], place[1]
    width = mine.shape[0] // (RING * RING)
    for t in range(RING):
        for k in range(RING):
            at = lax.rem(u - k + RING, RING) * RING + lax.rem(w - t + RING, RING)
            rows = slice((t * RING + k) * width, (t * RING + k + 1) * width)
            out[rows, :] = mine[rows, :] + theirs[pl.ds(pl.multiple_of(at * width, width), width), :]


def add_cores(place, mine, theirs):
    vmem = pl.BlockSpec(memory_space=pltpu.VMEM)
    return pl.pallas_call(
        add_cores_kernel,
        in_specs=[pl.BlockSpec(memory_space=pltpu.SMEM), vmem, vmem],
        out_specs=vmem,
        out_shape=jax.ShapeDtypeStruct(mine.shape, F32),
        compiler_params=params(),
        cost_estimate=cost(mine.size, 12 * mine.size),
        name="add_cores",
    )(place, mine, theirs)


def coefficients_kernel(factor, a, b, c, d, out):
    total = a[...] + b[...].astype(F32) + c[...].astype(F32) + d[...].astype(F32)
    out[...] = jnp.dot(
        factor[...], total, preferred_element_type=F32, precision=lax.Precision.HIGHEST
    ).astype(BF16)


def coefficients(factor, parts):
    vmem = pl.BlockSpec(memory_space=pltpu.VMEM)
    return pl.pallas_call(
        coefficients_kernel,
        in_specs=[vmem] * 5,
        out_specs=vmem,
        out_shape=jax.ShapeDtypeStruct(parts[0].shape, BF16),
        compiler_params=params(),
        cost_estimate=cost(12 * factor.size * parts[0].shape[1], 4 * factor.size),
        name="coefficients",
    )(factor, *parts)


def update_kernel(*refs):
    first, second, w0, w1, outs = refs[0], refs[1], refs[2:6], refs[6:10], refs[10:14]
    w0 = jnp.concatenate([r[...] for r in w0], axis=1)
    w1 = jnp.concatenate([r[...] for r in w1], axis=1)
    moved = jnp.dot(first[...], w0, preferred_element_type=F32)
    moved += jnp.dot(second[...], w1, preferred_element_type=F32)
    for s in range(RING):
        outs[s][...] = moved[:, s * 128:(s + 1) * 128].astype(BF16)


def update(first, second, w0, w1):
    rows, nb = first.shape
    columns = w0[0].shape[1]
    tile = 512
    flat = pl.BlockSpec((tile, nb), lambda i: (i, 0))
    small = pl.BlockSpec((nb, columns), lambda i: (0, 0))
    return pl.pallas_call(
        update_kernel,
        grid=(rows // tile,),
        in_specs=[flat, flat] + [small] * (2 * RING),
        out_specs=[pl.BlockSpec((tile, columns), lambda i: (i, 0))] * RING,
        out_shape=[jax.ShapeDtypeStruct((rows, columns), BF16)] * RING,
        compiler_params=params(),
        cost_estimate=cost(4 * nb * rows * RING * columns, 4 * nb * rows),
        name="update",
    )(first, second, *w0, *w1)


def subtract_kernel(place, z, *refs):
    out = refs[-1]
    for s in range(RING):
        @pl.when(pl.program_id(0) == s)
        def _(s=s):
            out[...] = z[...] - refs[s][...].astype(F32)


def subtract(place, z, moved):
    rows, columns = moved[0].shape
    tile = 2048
    steps = rows // tile

    def whole(s, i, place):
        return (lax.rem(place[0] + s, RING) * steps + i, 0)

    def part(k):
        return lambda s, i, place: (jnp.where(s < k, 0, jnp.where(s == k, i, steps - 1)), 0)

    return pl.pallas_call(
        subtract_kernel,
        grid_spec=pltpu.PrefetchScalarGridSpec(
            num_scalar_prefetch=1,
            grid=(RING, steps),
            in_specs=[pl.BlockSpec((tile, columns), whole)]
            + [pl.BlockSpec((tile, columns), part(k)) for k in range(RING)],
            out_specs=pl.BlockSpec((tile, columns), whole),
        ),
        out_shape=jax.ShapeDtypeStruct(z.shape, F32),
        compiler_params=params(),
        cost_estimate=cost(z.size, 10 * z.size),
        name="subtract",
    )(place, z, *moved)


def rows_kernel(order, source, out):
    out[...] = source[...]


def take_blocks(order, source):
    nb = source.shape[1]
    width = nb // (RING * RING)
    return pl.pallas_call(
        rows_kernel,
        grid_spec=pltpu.PrefetchScalarGridSpec(
            num_scalar_prefetch=1,
            grid=(RING * RING,),
            in_specs=[pl.BlockSpec((2, width, nb), lambda i, order: (0, order[i], 0))],
            out_specs=pl.BlockSpec((2, width, nb), lambda i, order: (0, i, 0)),
        ),
        out_shape=jax.ShapeDtypeStruct(source.shape, F32),
        compiler_params=params(),
        cost_estimate=cost(0, 8 * source.size),
        name="take_blocks",
    )(order, source)


def local(z_block, v_panels, t_panels):
    prow, pcol = lax.axis_index("prow"), lax.axis_index("pcol")
    core, y, z = prow % 2, pcol // RING, pcol % RING
    u, w = jnp.where(core == 0, y, z), jnp.where(core == 0, z, y)
    place = jnp.stack([u, w]).astype(jnp.int32)
    rows = z_block.shape[0] // RING
    width = v_panels.shape[2]

    def chunk(s):
        return ((u + s) % RING) * rows

    def gather(panel):
        flat = v_panels[panel].T
        mine = [lax.dynamic_slice(flat, (0, chunk(s)), (width, rows)) for s in range(RING)]
        mine = [mine[0]] + [send(mine[s], along_u(s)) for s in range(1, RING)]
        block = stack(place, mine)
        return [block] + [send(block, along_w(t)) for t in range(1, RING)]

    step, kept = jnp.arange(RING * RING) // RING, jnp.arange(RING * RING) % RING
    gone = (w - step) % RING
    order = jnp.where(core == 0, kept * RING + gone, gone * RING + kept).astype(jnp.int32)
    factors = take_blocks(order, jnp.swapaxes(take_blocks(order, t_panels), 1, 2))

    def reduce(parts, factor):
        parts = [parts[0]] + [send(parts[s], along_u(-s)) for s in range(1, RING)]
        total = parts[0]
        for part in parts[1:]:
            total = total + part.astype(F32)
        total = add_cores(place, total, send(total, other_core()))
        rounded = total.astype(BF16)
        coeffs = coefficients(factor, [total] + [send(rounded, along_x(s)) for s in range(1, RING)])
        return [coeffs] + [send(coeffs, along_u(s)) for s in range(1, RING)]

    first = gather(0)
    dealt = [lax.dynamic_slice(z_block, (chunk(s), 0), (rows, z_block.shape[1])).astype(BF16) for s in range(RING)]
    dealt = [dealt[0]] + [send(dealt[s], along_u(s)) for s in range(1, RING)]
    second = gather(1)
    first_flat, second_flat = transpose(first), transpose(second)

    w0 = reduce(sums(first, dealt), factors[0])
    w1 = reduce(sums(second, dealt, first_flat, w0), factors[1])
    moved = update(first_flat, second_flat, w0, w1)
    moved = [moved[0]] + [send(moved[s], along_u(-s)) for s in range(1, RING)]
    return subtract(place, z_block, moved)


def solution(mesh):
    return jax.shard_map(
        local,
        mesh=mesh,
        in_specs=(P("prow", "pcol"), P(None, "prow", "pcol"), P()),
        out_specs=P("prow", "pcol"),
        check_vma=False,
    )
```

time: 413 us -> 230 us (0.56)
  waiting for transfers between devices: 321 us -> 77.6 us
  starting transfers between devices: 0.3 us -> 82.4 us
  matrix products: 56.7 us -> 0 us
  Pallas kernels: 0 us -> 56.5 us
  between operations: 13.2 us -> 0.33 us
  local copies, waits for them, and re-layouts: 21.1 us -> 11.4 us
    all_gather x2 -> x0, waiting for transfers between devices: 211 us -> none  [local(): lax.all_gather(v_panels[which_panel], 'pcol', axis=1, tiled=True)]
    psum x2 -> x0, waiting for transfers between devices: 109 us -> none  [local(): summed = lax.psum(partial_value, 'prow')]
    ppermute x0 -> x38, starting transfers between devices: none -> 82.4 us  [send(): return lax.ppermute(value, AXES, pairs)]
    ppermute x0 -> x38, waiting for transfers between devices: none -> 77.6 us  [send(): return lax.ppermute(value, AXES, pairs)]
    dot_general x6 -> x0, matrix products: 56.7 us -> none  [the longest x2 27.7 us: local(): jnp.dot(reflectors, coeffs, preferred_element_type=jnp.float32)]
    pallas_call x0 -> x14, Pallas kernels: none -> 56.5 us  [the longest x2 17.4 us: sums(): pl.pallas_call(first_sums_kernel if flat is None else second_sums_kernel,...]
    sub x1 -> x0, local copies, waits for them, and re-layouts: 8.98 us -> none  [local(): vectors - jnp.dot(reflectors, coeffs, preferred_element_type=jnp.float32)]
    unnamed x3 -> x22, local copies, waits for them, and re-layouts: 9.13 us -> 1.35 us
  transfers between devices with their start and end apart: 4 -> 38, of which waited for: 4 -> 17; matrix products, arithmetic and copies ran while one was open for 6% -> 2% of each run, Pallas kernels for 0% -> 12%
where the time goes in v1:
time: 230 us; the launch traced here: 229 us
  starting transfers between devices  82.4 us (36%)
  waiting for transfers between devices  77.6 us (34%)
  Pallas kernels  56.5 us (25%)
  local copies, waits for them, and re-layouts  11.4 us (5%)
    ppermute x38, starting transfers between devices, send(): return lax.ppermute(value, AXES, pairs)  82.4 us
    ppermute x38, waiting for transfers between devices, send(): return lax.ppermute(value, AXES, pairs)  77.6 us
    pallas_call x2, Pallas kernels, sums(): pl.pallas_call(first_sums_kernel if flat is None else second_sums_kernel,...  17.4 us
    pallas_call x2, Pallas kernels, transpose(): pl.pallas_call(transpose_kernel, grid=(rows // tile,), in_specs=[pl.Block...  11.6 us
    pallas_call x1, Pallas kernels, subtract(): pl.pallas_call(subtract_kernel, grid_spec=pltpu.PrefetchScalarGridSpec(nu...  9.63 us
    pallas_call x1, Pallas kernels, update(): pl.pallas_call(update_kernel, grid=(rows // tile,), in_specs=[flat, flat]...  8.68 us
    convert_element_type x1, local copies, waits for them, and re-layouts, local(): lax.dynamic_slice(z_block, (chunk(s), 0), (rows, z_block.shape[1]))  5.46 us
  transfers between devices with their start and end apart: 38, of which 17 were waited for; matrix products, arithmetic and copies ran while one was open for 2% of the time, Pallas kernels for 12%

profile of v1, /device:TPU:0, one launch (start us, length us, event | category | flops | bytes accessed | tf_op | source)
XLA Modules:
  0.0 229.0 jit_solution(7682009928175885235)
XLA Ops:
  0.0 5.5 %dynamic-slice_convert_fusion = (bf16[4096,128]{1,0:T(8,128)(2,1)}, bf16[4096,128]{1,0:T(8,128)(2,1)}, bf16[4096,128]{1,0:T(8,128)(2,1)}, bf16[4096,128]{1,0:T(8,128)(2,1)S(1)}) fusion(f32[16384,128]{1,0:T(8,128)} %z.1, s32[]{:T(128)S(6)} %select_n.110, s32[]{:T(128)S(6)} %select_n.108, s32[]{:T(128)S(6)} %select_n.106, s32[]{:T(128)S(6)} %select_n.104), kind=kLoop, calls=%fused_computation | loop fusion | bytes 8388624 | tf_op jit(solution)/shard_map/convert_element_type | solution.py:330
  11.5 2.4 %collective-permute-start.2 = (bf16[32,4096]{1,0:T(8,128)(2,1)S(1)}, bf16[32,4096]{1,0:T(8,128)(2,1)S(1)}, u32[]{:S(2)}, u32[]{:S(2)}) collective-permute-start(bf16[32,4096]{1,0:T(8,128)(2,1)S(1)} %get-tuple-element.41), channel_id=1, source_target_pairs={{0,12},{1,13},{2,14},{3,15},{4,0},{5,1},{6,2},{7,3},{8,4},{9,5},{1... | collective-permute-start | bytes 786440 | tf_op jit(solution)/shard_map/ppermute | solution.py:46
  14.6 9.9 %collective-permute-done.refs_1_ = bf16[32,4096]{1,0:T(8,128)(2,1)S(1)} collective-permute-done((bf16[32,4096]{1,0:T(8,128)(2,1)S(1)}, bf16[32,4096]{1,0:T(8,128)(2,1)S(1)}, u32[]{:S(2)}, u32[]{:S(2)}) %collective-permute-start) | collective-permute-done | bytes 262176 | tf_op jit(solution)/shard_map/ppermute | solution.py:46
  26.4 2.2 collective-permute-done.1.refs_2_
  29.5 2.0 collective-permute-start.3
  31.5 3.6 %collective-permute-start.4 = (bf16[128,4096]{1,0:T(8,128)(2,1)S(1)}, bf16[128,4096]{1,0:T(8,128)(2,1)S(1)}, u32[]{:S(2)}, u32[]{:S(2)}) collective-permute-start(bf16[128,4096]{1,0:T(8,128)(2,1)S(1)} %stack_reflectors.2.refs_0_), channel_id=1, source_target_pairs={{0,2},{1,3},{2,0},{3,1},{4,6},{5,7},{6,4},{7,5},{8,10},{9,11},{10,... | collective-permute-start | bytes 3145736 | tf_op jit(solution)/shard_map/ppermute | solution.py:46
  37.4 7.6 %collective-permute-done.13.refs_6_ = bf16[4096,128]{1,0:T(8,128)(2,1)} collective-permute-done((bf16[4096,128]{1,0:T(8,128)(2,1)}, bf16[4096,128]{1,0:T(8,128)(2,1)}, u32[]{:S(2)}, u32[]{:S(2)}) %collective-permute-start.13) | collective-permute-done | bytes 1048608 | tf_op jit(solution)/shard_map/ppermute | solution.py:46
  45.0 14.4 %collective-permute-done.14.refs_7_ = bf16[4096,128]{1,0:T(8,128)(2,1)S(1)} collective-permute-done((bf16[4096,128]{1,0:T(8,128)(2,1)}, bf16[4096,128]{1,0:T(8,128)(2,1)S(1)}, u32[]{:S(2)}, u32[]{:S(2)}) %collective-permute-start.14) | collective-permute-done | bytes 1048608 | tf_op jit(solution)/shard_map/ppermute | solution.py:46
  59.4 9.9 %collective-permute-start.7 = (bf16[32,4096]{1,0:T(8,128)(2,1)S(1)}, bf16[32,4096]{1,0:T(8,128)(2,1)S(1)}, u32[]{:S(2)}, u32[]{:S(2)}) collective-permute-start(bf16[32,4096]{1,0:T(8,128)(2,1)S(1)} %get-tuple-element.38), channel_id=1, source_target_pairs={{0,8},{1,9},{2,10},{3,11},{4,12},{5,13},{6,14},{7,15},{8,0},{9,1},... | collective-permute-start | bytes 786440 | tf_op jit(solution)/shard_map/ppermute | solution.py:46
  69.4 3.0 %collective-permute-start.8 = (bf16[32,4096]{1,0:T(8,128)(2,1)S(1)}, bf16[32,4096]{1,0:T(8,128)(2,1)S(1)}, u32[]{:S(2)}, u32[]{:S(2)}) collective-permute-start(bf16[32,4096]{1,0:T(8,128)(2,1)S(1)} %get-tuple-element.37), channel_id=1, source_target_pairs={{0,12},{1,13},{2,14},{3,15},{4,0},{5,1},{6,2},{7,3},{8,4},{9,5},{1... | collective-permute-start | bytes 786440 | tf_op jit(solution)/shard_map/ppermute | solution.py:46
  72.4 7.4 %panel_sums.2 = (f32[512,128]{1,0:T(8,128)S(1)}, bf16[512,128]{1,0:T(8,128)(2,1)S(1)}, bf16[512,128]{1,0:T(8,128)(2,1)S(1)}, bf16[512,128]{1,0:T(8,128)(2,1)S(1)}) custom-call(bf16[128,4096]{1,0:T(8,128)(2,1)S(1)} %stack_reflectors.2.refs_0_, bf16[128,4096]{1,0:T(8,128)(2,1)S(1)} %collective-permute-done.3.refs_1_, ...), custom_call_target="tpu_custom_call" | custom-call | flops 2147483648 | bytes 8388608 | tf_op jit(solution)/shard_map/panel_sums/pallas_call | solution.py:155
  79.8 5.2 %collective-permute-start.15 = (bf16[512,128]{1,0:T(8,128)(2,1)S(1)}, bf16[512,128]{1,0:T(8,128)(2,1)S(1)}, u32[]{:S(2)}, u32[]{:S(2)}) collective-permute-start(bf16[512,128]{1,0:T(8,128)(2,1)S(1)} %get-tuple-element.18), channel_id=1, source_target_pairs={{0,12},{1,13},{2,14},{3,15},{4,0},{5,1},{6,2},{7,3},{8,4},{9,5},{1... | collective-permute-start | bytes 393224 | tf_op jit(solution)/shard_map/ppermute | solution.py:46
  86.0 2.2 stack_reflectors.3.refs_0_
  88.3 5.4 %collective-permute-start.10 = (bf16[128,4096]{1,0:T(8,128)(2,1)}, bf16[128,4096]{1,0:T(8,128)(2,1)}, u32[]{:S(2)}, u32[]{:S(2)}) collective-permute-start(bf16[128,4096]{1,0:T(8,128)(2,1)} %stack_reflectors.3.refs_0_), channel_id=1, source_target_pairs={{0,2},{1,3},{2,0},{3,1},{4,6},{5,7},{6,4},{7,5},{8,10},{9,11},{10,... | collective-permute-start | bytes 3145736 | tf_op jit(solution)/shard_map/ppermute | solution.py:46
  93.7 3.1 %collective-permute-start.11 = (bf16[128,4096]{1,0:T(8,128)(2,1)}, bf16[128,4096]{1,0:T(8,128)(2,1)}, u32[]{:S(2)}, u32[]{:S(2)}) collective-permute-start(bf16[128,4096]{1,0:T(8,128)(2,1)} %stack_reflectors.3.refs_0_), channel_id=1, source_target_pairs={{0,3},{1,0},{2,1},{3,2},{4,7},{5,4},{6,5},{7,6},{8,11},{9,8},{10,9... | collective-permute-start | bytes 3145736 | tf_op jit(solution)/shard_map/ppermute | solution.py:46
  96.8 10.1 %collective-permute-start.9 = (bf16[128,4096]{1,0:T(8,128)(2,1)}, bf16[128,4096]{1,0:T(8,128)(2,1)}, u32[]{:S(2)}, u32[]{:S(2)}) collective-permute-start(bf16[128,4096]{1,0:T(8,128)(2,1)} %stack_reflectors.3.refs_0_), channel_id=1, source_target_pairs={{0,1},{1,2},{2,3},{3,0},{4,5},{5,6},{6,7},{7,4},{8,9},{9,10},{10,1... | collective-permute-start | bytes 3145736 | tf_op jit(solution)/shard_map/ppermute | solution.py:46
  114.1 1.9 copy.4
  117.3 2.8 %collective-permute-start.20 = (bf16[512,128]{1,0:T(8,128)(2,1)}, bf16[512,128]{1,0:T(8,128)(2,1)S(1)}, u32[]{:S(2)}, u32[]{:S(2)}) collective-permute-start(bf16[512,128]{1,0:T(8,128)(2,1)} %convert_element_type.43), channel_id=1, source_target_pairs={{0,64},{1,65},{2,66},{3,67},{4,68},{5,69},{6,70},{7,71},{8,72},{9,... | collective-permute-start | bytes 393224 | tf_op jit(solution)/shard_map/ppermute | solution.py:46
  121.8 2.6 %collective-permute-done.20.c = bf16[512,128]{1,0:T(8,128)(2,1)S(1)} collective-permute-done((bf16[512,128]{1,0:T(8,128)(2,1)}, bf16[512,128]{1,0:T(8,128)(2,1)S(1)}, u32[]{:S(2)}, u32[]{:S(2)}) %collective-permute-start.20) | collective-permute-done | bytes 131104 | tf_op jit(solution)/shard_map/ppermute | solution.py:46
  127.5 5.1 %collective-permute-start.23 = (bf16[512,128]{1,0:T(8,128)(2,1)S(1)}, bf16[512,128]{1,0:T(8,128)(2,1)S(1)}, u32[]{:S(2)}, u32[]{:S(2)}) collective-permute-start(bf16[512,128]{1,0:T(8,128)(2,1)S(1)} %coefficients.2.refs_9_.refs_2_), channel_id=1, source_target_pairs={{0,8},{1,9},{2,10},{3,11},{4,12},{5,13},{6,14},{7,15},{8,0},{9,1},... | collective-permute-start | bytes 393224 | tf_op jit(solution)/shard_map/ppermute | solution.py:46
  132.6 4.4 %transpose_reflectors.2.refs_8_.refs_0_ = bf16[4096,512]{1,0:T(8,128)(2,1)} custom-call(bf16[128,4096]{1,0:T(8,128)(2,1)S(1)} %stack_reflectors.2.refs_0_, bf16[128,4096]{1,0:T(8,128)(2,1)S(1)} %copy-done.3, bf16[128,4096]{1,0:T(8,128)(2,1)S(1)} %copy-done.5, bf16[128,4096]{1,0:T(8,128)(2,1)S(1)} %copy-done.7), custom_call_target="tpu_custom_call" | custom-call | bytes 8388608 | tf_op jit(solution)/shard_map/transpose_reflectors/pallas_call | solution.py:93
  137.6 10.1 %panel_sums.3 = (f32[512,128]{1,0:T(8,128)S(1)}, bf16[512,128]{1,0:T(8,128)(2,1)S(1)}, bf16[512,128]{1,0:T(8,128)(2,1)S(1)}, bf16[512,128]{1,0:T(8,128)(2,1)S(1)}) custom-call(bf16[128,4096]{1,0:T(8,128)(2,1)} %stack_reflectors.3.refs_0_, bf16[128,4096]{1,0:T(8,128)(2,1)} %collective-permute-done.9.refs_1_, ...), custom_call_target="tpu_custom_call" | custom-call | flops 4294967296 | bytes 8388608 | tf_op jit(solution)/shard_map/panel_sums/pallas_call | solution.py:155
  149.2 2.0 collective-permute-start.26
  152.7 3.0 %collective-permute-done.26 = bf16[512,128]{1,0:T(8,128)(2,1)S(1)} collective-permute-done((bf16[512,128]{1,0:T(8,128)(2,1)S(1)}, bf16[512,128]{1,0:T(8,128)(2,1)S(1)}, u32[]{:S(2)}, u32[]{:S(2)}) %collective-permute-start.26) | collective-permute-done | bytes 131104 | tf_op jit(solution)/shard_map/ppermute | solution.py:46
  161.5 2.4 %collective-permute-start.30 = (bf16[512,128]{1,0:T(8,128)(2,1)S(1)}, bf16[512,128]{1,0:T(8,128)(2,1)S(1)}, u32[]{:S(2)}, u32[]{:S(2)}) collective-permute-start(bf16[512,128]{1,0:T(8,128)(2,1)S(1)} %convert_element_type.47), channel_id=1, source_target_pairs={{0,64},{1,65},{2,66},{3,67},{4,68},{5,69},{6,70},{7,71},{8,72},{9,... | collective-permute-start | bytes 393224 | tf_op jit(solution)/shard_map/ppermute | solution.py:46
  166.5 3.7 %collective-permute-done.30.c = bf16[512,128]{1,0:T(8,128)(2,1)S(1)} collective-permute-done((bf16[512,128]{1,0:T(8,128)(2,1)S(1)}, bf16[512,128]{1,0:T(8,128)(2,1)S(1)}, u32[]{:S(2)}, u32[]{:S(2)}) %collective-permute-start.30) | collective-permute-done | bytes 131104 | tf_op jit(solution)/shard_map/ppermute | solution.py:46
  173.2 2.5 %collective-permute-start.34 = (bf16[512,128]{1,0:T(8,128)(2,1)S(1)}, bf16[512,128]{1,0:T(8,128)(2,1)S(1)}, u32[]{:S(2)}, u32[]{:S(2)}) collective-permute-start(bf16[512,128]{1,0:T(8,128)(2,1)S(1)} %coefficients.3.refs_6_), channel_id=1, source_target_pairs={{0,12},{1,13},{2,14},{3,15},{4,0},{5,1},{6,2},{7,3},{8,4},{9,5},{1... | collective-permute-start | bytes 393224 | tf_op jit(solution)/shard_map/ppermute | solution.py:46
  175.7 7.3 %transpose_reflectors.3.refs_1_ = bf16[4096,512]{1,0:T(8,128)(2,1)} custom-call(bf16[128,4096]{1,0:T(8,128)(2,1)} %stack_reflectors.3.refs_0_, bf16[128,4096]{1,0:T(8,128)(2,1)} %collective-permute-done.9.refs_1_, bf16[128,4096]{1,0:T(8,128)(2,1)} %collective-permute-done.10.refs_2_, bf16[128,4096]{1,0:T(8,128)(2,1)} %collective-permute-done.11.refs_3_), custom_call_target="tpu_custom_call" | custom-call | bytes 8388608 | tf_op jit(solution)/shard_map/transpose_reflectors/pallas_call | solution.py:93
  183.0 8.7 %update.1 = (bf16[4096,128]{1,0:T(8,128)(2,1)S(1)}, bf16[4096,128]{1,0:T(8,128)(2,1)S(1)}, bf16[4096,128]{1,0:T(8,128)(2,1)S(1)}, bf16[4096,128]{1,0:T(8,128)(2,1)S(1)}) custom-call(bf16[4096,512]{1,0:T(8,128)(2,1)} %transpose_reflectors.2.refs_8_.refs_0_, bf16[4096,512]{1,0:T(8,128)(2,1)} %transpose_reflectors.3.refs_1_, ...), custom_call_target="tpu_custom_call" | custom-call | flops 4294967296 | bytes 8388608 | tf_op jit(solution)/shard_map/update/pallas_call | solution.py:227
  195.0 11.5 %collective-permute-done.35.refs_1_ = bf16[4096,128]{1,0:T(8,128)(2,1)S(1)} collective-permute-done((bf16[4096,128]{1,0:T(8,128)(2,1)S(1)}, bf16[4096,128]{1,0:T(8,128)(2,1)S(1)}, u32[]{:S(2)}, u32[]{:S(2)}) %collective-permute-start.35) | collective-permute-done | bytes 1048608 | tf_op jit(solution)/shard_map/ppermute | solution.py:46
  208.3 11.1 %collective-permute-done.37.refs_3_ = bf16[4096,128]{1,0:T(8,128)(2,1)S(1)} collective-permute-done((bf16[4096,128]{1,0:T(8,128)(2,1)S(1)}, bf16[4096,128]{1,0:T(8,128)(2,1)S(1)}, u32[]{:S(2)}, u32[]{:S(2)}) %collective-permute-start.37) | collective-permute-done | bytes 1048608 | tf_op jit(solution)/shard_map/ppermute | solution.py:46
  219.4 9.6 %subtract.1 = f32[16384,128]{1,0:T(8,128)} custom-call(s32[2]{0:T(128)S(1)} %pad_add_fusion.place, f32[16384,128]{1,0:T(8,128)} %z.1, bf16[4096,128]{1,0:T(8,128)(2,1)S(1)} %get-tuple-element.25.refs_0_, bf16[4096,128]{1,0:T(8,128)(2,1)S(1)} %collective-permute-done.35.refs_1_, bf16[4096,128]{1,0:T(8,128)(2,1)S(1)} %collective-permute-done.36.refs_2_, ...), custom_call_target="tpu_custom_call" | custom-call | flops 2097152 | bytes 20971520 | tf_op jit(solution)/shard_map/subtract/pallas_call | solution.py:258
  (92 shorter events, 45.8 us)
Async XLA Ops:
  5.5 29.6 %collective-permute-start.12 = (bf16[4096,128]{1,0:T(8,128)(2,1)}, bf16[4096,128]{1,0:T(8,128)(2,1)}, u32[]{:S(2)}, u32[]{:S(2)}) collective-permute-start(bf16[4096,128]{1,0:T(8,128)(2,1)} %get-tuple-element.31), channel_id=1, source_target_pairs={{0,4},{1,5},{2,6},{3,7},{4,8},{5,9},{6,10},{7,11},{8,12},{9,13},{1... | collective-permute-start | bytes 3145736 | tf_op jit(solution)/shard_map/ppermute | solution.py:46
  8.3 16.2 %collective-permute-start = (bf16[32,4096]{1,0:T(8,128)(2,1)S(1)}, bf16[32,4096]{1,0:T(8,128)(2,1)S(1)}, u32[]{:S(2)}, u32[]{:S(2)}) collective-permute-start(bf16[32,4096]{1,0:T(8,128)(2,1)S(1)} %get-tuple-element.43), channel_id=1, source_target_pairs={{0,4},{1,5},{2,6},{3,7},{4,8},{5,9},{6,10},{7,11},{8,12},{9,13},{1... | collective-permute-start | bytes 786440 | tf_op jit(solution)/shard_map/ppermute | solution.py:46
  10.0 18.7 %collective-permute-start.1 = (bf16[32,4096]{1,0:T(8,128)(2,1)S(1)}, bf16[32,4096]{1,0:T(8,128)(2,1)S(1)}, u32[]{:S(2)}, u32[]{:S(2)}) collective-permute-start(bf16[32,4096]{1,0:T(8,128)(2,1)S(1)} %get-tuple-element.42), channel_id=1, source_target_pairs={{0,8},{1,9},{2,10},{3,11},{4,12},{5,13},{6,14},{7,15},{8,0},{9,1},... | collective-permute-start | bytes 786440 | tf_op jit(solution)/shard_map/ppermute | solution.py:46
  11.5 17.1 %collective-permute-start.2 = (bf16[32,4096]{1,0:T(8,128)(2,1)S(1)}, bf16[32,4096]{1,0:T(8,128)(2,1)S(1)}, u32[]{:S(2)}, u32[]{:S(2)}) collective-permute-start(bf16[32,4096]{1,0:T(8,128)(2,1)S(1)} %get-tuple-element.41), channel_id=1, source_target_pairs={{0,12},{1,13},{2,14},{3,15},{4,0},{5,1},{6,2},{7,3},{8,4},{9,5},{1... | collective-permute-start | bytes 786440 | tf_op jit(solution)/shard_map/ppermute | solution.py:46
  13.9 31.1 %collective-permute-start.13 = (bf16[4096,128]{1,0:T(8,128)(2,1)}, bf16[4096,128]{1,0:T(8,128)(2,1)}, u32[]{:S(2)}, u32[]{:S(2)}) collective-permute-start(bf16[4096,128]{1,0:T(8,128)(2,1)} %get-tuple-element.30), channel_id=1, source_target_pairs={{0,8},{1,9},{2,10},{3,11},{4,12},{5,13},{6,14},{7,15},{8,0},{9,1},... | collective-permute-start | bytes 3145736 | tf_op jit(solution)/shard_map/ppermute | solution.py:46
  24.5 35.0 %collective-permute-start.14 = (bf16[4096,128]{1,0:T(8,128)(2,1)}, bf16[4096,128]{1,0:T(8,128)(2,1)S(1)}, u32[]{:S(2)}, u32[]{:S(2)}) collective-permute-start(bf16[4096,128]{1,0:T(8,128)(2,1)} %get-tuple-element.29), channel_id=1, source_target_pairs={{0,12},{1,13},{2,14},{3,15},{4,0},{5,1},{6,2},{7,3},{8,4},{9,5},{1... | collective-permute-start | bytes 3145736 | tf_op jit(solution)/shard_map/ppermute | solution.py:46
  29.5 39.9 %collective-permute-start.3 = (bf16[128,4096]{1,0:T(8,128)(2,1)S(1)}, bf16[128,4096]{1,0:T(8,128)(2,1)S(1)}, u32[]{:S(2)}, u32[]{:S(2)}) collective-permute-start(bf16[128,4096]{1,0:T(8,128)(2,1)S(1)} %stack_reflectors.2.refs_0_), channel_id=1, source_target_pairs={{0,1},{1,2},{2,3},{3,0},{4,5},{5,6},{6,7},{7,4},{8,9},{9,10},{10,1... | collective-permute-start | bytes 3145736 | tf_op jit(solution)/shard_map/ppermute | solution.py:46
  31.5 40.9 %collective-permute-start.4 = (bf16[128,4096]{1,0:T(8,128)(2,1)S(1)}, bf16[128,4096]{1,0:T(8,128)(2,1)S(1)}, u32[]{:S(2)}, u32[]{:S(2)}) collective-permute-start(bf16[128,4096]{1,0:T(8,128)(2,1)S(1)} %stack_reflectors.2.refs_0_), channel_id=1, source_target_pairs={{0,2},{1,3},{2,0},{3,1},{4,6},{5,7},{6,4},{7,5},{8,10},{9,11},{10,... | collective-permute-start | bytes 3145736 | tf_op jit(solution)/shard_map/ppermute | solution.py:46
  35.1 37.3 %collective-permute-start.5 = (bf16[128,4096]{1,0:T(8,128)(2,1)S(1)}, bf16[128,4096]{1,0:T(8,128)(2,1)S(1)}, u32[]{:S(2)}, u32[]{:S(2)}) collective-permute-start(bf16[128,4096]{1,0:T(8,128)(2,1)S(1)} %stack_reflectors.2.refs_0_), channel_id=1, source_target_pairs={{0,3},{1,0},{2,1},{3,2},{4,7},{5,4},{6,5},{7,6},{8,11},{9,8},{10,9... | collective-permute-start | bytes 3145736 | tf_op jit(solution)/shard_map/ppermute | solution.py:46
  45.0 40.1 %collective-permute-start.6 = (bf16[32,4096]{1,0:T(8,128)(2,1)S(1)}, bf16[32,4096]{1,0:T(8,128)(2,1)S(1)}, u32[]{:S(2)}, u32[]{:S(2)}) collective-permute-start(bf16[32,4096]{1,0:T(8,128)(2,1)S(1)} %get-tuple-element.39), channel_id=1, source_target_pairs={{0,4},{1,5},{2,6},{3,7},{4,8},{5,9},{6,10},{7,11},{8,12},{9,13},{1... | collective-permute-start | bytes 786440 | tf_op jit(solution)/shard_map/ppermute | solution.py:46
  59.4 26.6 %collective-permute-start.7 = (bf16[32,4096]{1,0:T(8,128)(2,1)S(1)}, bf16[32,4096]{1,0:T(8,128)(2,1)S(1)}, u32[]{:S(2)}, u32[]{:S(2)}) collective-permute-start(bf16[32,4096]{1,0:T(8,128)(2,1)S(1)} %get-tuple-element.38), channel_id=1, source_target_pairs={{0,8},{1,9},{2,10},{3,11},{4,12},{5,13},{6,14},{7,15},{8,0},{9,1},... | collective-permute-start | bytes 786440 | tf_op jit(solution)/shard_map/ppermute | solution.py:46
  69.4 16.6 %collective-permute-start.8 = (bf16[32,4096]{1,0:T(8,128)(2,1)S(1)}, bf16[32,4096]{1,0:T(8,128)(2,1)S(1)}, u32[]{:S(2)}, u32[]{:S(2)}) collective-permute-start(bf16[32,4096]{1,0:T(8,128)(2,1)S(1)} %get-tuple-element.37), channel_id=1, source_target_pairs={{0,12},{1,13},{2,14},{3,15},{4,0},{5,1},{6,2},{7,3},{8,4},{9,5},{1... | collective-permute-start | bytes 786440 | tf_op jit(solution)/shard_map/ppermute | solution.py:46
  79.8 17.0 %collective-permute-start.15 = (bf16[512,128]{1,0:T(8,128)(2,1)S(1)}, bf16[512,128]{1,0:T(8,128)(2,1)S(1)}, u32[]{:S(2)}, u32[]{:S(2)}) collective-permute-start(bf16[512,128]{1,0:T(8,128)(2,1)S(1)} %get-tuple-element.18), channel_id=1, source_target_pairs={{0,12},{1,13},{2,14},{3,15},{4,0},{5,1},{6,2},{7,3},{8,4},{9,5},{1... | collective-permute-start | bytes 393224 | tf_op jit(solution)/shard_map/ppermute | solution.py:46
  85.1 21.9 %collective-permute-start.16 = (bf16[512,128]{1,0:T(8,128)(2,1)S(1)}, bf16[512,128]{1,0:T(8,128)(2,1)S(1)}, u32[]{:S(2)}, u32[]{:S(2)}) collective-permute-start(bf16[512,128]{1,0:T(8,128)(2,1)S(1)} %get-tuple-element.19), channel_id=1, source_target_pairs={{0,8},{1,9},{2,10},{3,11},{4,12},{5,13},{6,14},{7,15},{8,0},{9,1},... | collective-permute-start | bytes 393224 | tf_op jit(solution)/shard_map/ppermute | solution.py:46
  85.1 21.9 %collective-permute-start.17 = (bf16[512,128]{1,0:T(8,128)(2,1)S(1)}, bf16[512,128]{1,0:T(8,128)(2,1)S(1)}, u32[]{:S(2)}, u32[]{:S(2)}) collective-permute-start(bf16[512,128]{1,0:T(8,128)(2,1)S(1)} %get-tuple-element.20), channel_id=1, source_target_pairs={{0,4},{1,5},{2,6},{3,7},{4,8},{5,9},{6,10},{7,11},{8,12},{9,13},{1... | collective-permute-start | bytes 393224 | tf_op jit(solution)/shard_map/ppermute | solution.py:46
  88.3 44.3 %collective-permute-start.10 = (bf16[128,4096]{1,0:T(8,128)(2,1)}, bf16[128,4096]{1,0:T(8,128)(2,1)}, u32[]{:S(2)}, u32[]{:S(2)}) collective-permute-start(bf16[128,4096]{1,0:T(8,128)(2,1)} %stack_reflectors.3.refs_0_), channel_id=1, source_target_pairs={{0,2},{1,3},{2,0},{3,1},{4,6},{5,7},{6,4},{7,5},{8,10},{9,11},{10,... | collective-permute-start | bytes 3145736 | tf_op jit(solution)/shard_map/ppermute | solution.py:46
  93.7 43.3 %collective-permute-start.11 = (bf16[128,4096]{1,0:T(8,128)(2,1)}, bf16[128,4096]{1,0:T(8,128)(2,1)}, u32[]{:S(2)}, u32[]{:S(2)}) collective-permute-start(bf16[128,4096]{1,0:T(8,128)(2,1)} %stack_reflectors.3.refs_0_), channel_id=1, source_target_pairs={{0,3},{1,0},{2,1},{3,2},{4,7},{5,4},{6,5},{7,6},{8,11},{9,8},{10,9... | collective-permute-start | bytes 3145736 | tf_op jit(solution)/shard_map/ppermute | solution.py:46
  96.8 40.2 %collective-permute-start.9 = (bf16[128,4096]{1,0:T(8,128)(2,1)}, bf16[128,4096]{1,0:T(8,128)(2,1)}, u32[]{:S(2)}, u32[]{:S(2)}) collective-permute-start(bf16[128,4096]{1,0:T(8,128)(2,1)} %stack_reflectors.3.refs_0_), channel_id=1, source_target_pairs={{0,1},{1,2},{2,3},{3,0},{4,5},{5,6},{6,7},{7,4},{8,9},{9,10},{10,1... | collective-permute-start | bytes 3145736 | tf_op jit(solution)/shard_map/ppermute | solution.py:46
  109.9 10.3 %collective-permute-start.19 = (bf16[512,128]{1,0:T(8,128)(2,1)}, bf16[512,128]{1,0:T(8,128)(2,1)S(1)}, u32[]{:S(2)}, u32[]{:S(2)}) collective-permute-start(bf16[512,128]{1,0:T(8,128)(2,1)} %convert_element_type.43), channel_id=1, source_target_pairs={{0,32},{1,33},{2,34},{3,35},{4,36},{5,37},{6,38},{7,39},{8,40},{9,... | collective-permute-start | bytes 393224 | tf_op jit(solution)/shard_map/ppermute | solution.py:46
  117.3 7.1 %collective-permute-start.20 = (bf16[512,128]{1,0:T(8,128)(2,1)}, bf16[512,128]{1,0:T(8,128)(2,1)S(1)}, u32[]{:S(2)}, u32[]{:S(2)}) collective-permute-start(bf16[512,128]{1,0:T(8,128)(2,1)} %convert_element_type.43), channel_id=1, source_target_pairs={{0,64},{1,65},{2,66},{3,67},{4,68},{5,69},{6,70},{7,71},{8,72},{9,... | collective-permute-start | bytes 393224 | tf_op jit(solution)/shard_map/ppermute | solution.py:46
  127.4 9.6 %collective-permute-start.22 = (bf16[512,128]{1,0:T(8,128)(2,1)S(1)}, bf16[512,128]{1,0:T(8,128)(2,1)S(1)}, u32[]{:S(2)}, u32[]{:S(2)}) collective-permute-start(bf16[512,128]{1,0:T(8,128)(2,1)S(1)} %coefficients.2.refs_9_.refs_2_), channel_id=1, source_target_pairs={{0,4},{1,5},{2,6},{3,7},{4,8},{5,9},{6,10},{7,11},{8,12},{9,13},{1... | collective-permute-start | bytes 393224 | tf_op jit(solution)/shard_map/ppermute | solution.py:46
  127.5 9.6 %collective-permute-start.23 = (bf16[512,128]{1,0:T(8,128)(2,1)S(1)}, bf16[512,128]{1,0:T(8,128)(2,1)S(1)}, u32[]{:S(2)}, u32[]{:S(2)}) collective-permute-start(bf16[512,128]{1,0:T(8,128)(2,1)S(1)} %coefficients.2.refs_9_.refs_2_), channel_id=1, source_target_pairs={{0,8},{1,9},{2,10},{3,11},{4,12},{5,13},{6,14},{7,15},{8,0},{9,1},... | collective-permute-start | bytes 393224 | tf_op jit(solution)/shard_map/ppermute | solution.py:46
  149.2 6.5 %collective-permute-start.26 = (bf16[512,128]{1,0:T(8,128)(2,1)S(1)}, bf16[512,128]{1,0:T(8,128)(2,1)S(1)}, u32[]{:S(2)}, u32[]{:S(2)}) collective-permute-start(bf16[512,128]{1,0:T(8,128)(2,1)S(1)} %get-tuple-element.23), channel_id=1, source_target_pairs={{0,8},{1,9},{2,10},{3,11},{4,12},{5,13},{6,14},{7,15},{8,0},{9,1},... | collective-permute-start | bytes 393224 | tf_op jit(solution)/shard_map/ppermute | solution.py:46
  159.7 6.8 %collective-permute-start.29 = (bf16[512,128]{1,0:T(8,128)(2,1)S(1)}, bf16[512,128]{1,0:T(8,128)(2,1)S(1)}, u32[]{:S(2)}, u32[]{:S(2)}) collective-permute-start(bf16[512,128]{1,0:T(8,128)(2,1)S(1)} %convert_element_type.47), channel_id=1, source_target_pairs={{0,32},{1,33},{2,34},{3,35},{4,36},{5,37},{6,38},{7,39},{8,40},{9,... | collective-permute-start | bytes 393224 | tf_op jit(solution)/shard_map/ppermute | solution.py:46
  161.5 8.7 %collective-permute-start.30 = (bf16[512,128]{1,0:T(8,128)(2,1)S(1)}, bf16[512,128]{1,0:T(8,128)(2,1)S(1)}, u32[]{:S(2)}, u32[]{:S(2)}) collective-permute-start(bf16[512,128]{1,0:T(8,128)(2,1)S(1)} %convert_element_type.47), channel_id=1, source_target_pairs={{0,64},{1,65},{2,66},{3,67},{4,68},{5,69},{6,70},{7,71},{8,72},{9,... | collective-permute-start | bytes 393224 | tf_op jit(solution)/shard_map/ppermute | solution.py:46
  163.9 6.3 %collective-permute-start.31 = (bf16[512,128]{1,0:T(8,128)(2,1)S(1)}, bf16[512,128]{1,0:T(8,128)(2,1)S(1)}, u32[]{:S(2)}, u32[]{:S(2)}) collective-permute-start(bf16[512,128]{1,0:T(8,128)(2,1)S(1)} %convert_element_type.47), channel_id=1, source_target_pairs={{0,96},{1,97},{2,98},{3,99},{4,100},{5,101},{6,102},{7,103},{8,104... | collective-permute-start | bytes 393224 | tf_op jit(solution)/shard_map/ppermute | solution.py:46
  171.3 11.7 %collective-permute-start.32 = (bf16[512,128]{1,0:T(8,128)(2,1)S(1)}, bf16[512,128]{1,0:T(8,128)(2,1)S(1)}, u32[]{:S(2)}, u32[]{:S(2)}) collective-permute-start(bf16[512,128]{1,0:T(8,128)(2,1)S(1)} %coefficients.3.refs_6_), channel_id=1, source_target_pairs={{0,4},{1,5},{2,6},{3,7},{4,8},{5,9},{6,10},{7,11},{8,12},{9,13},{1... | collective-permute-start | bytes 393224 | tf_op jit(solution)/shard_map/ppermute | solution.py:46
  171.6 11.4 %collective-permute-start.33 = (bf16[512,128]{1,0:T(8,128)(2,1)S(1)}, bf16[512,128]{1,0:T(8,128)(2,1)S(1)}, u32[]{:S(2)}, u32[]{:S(2)}) collective-permute-start(bf16[512,128]{1,0:T(8,128)(2,1)S(1)} %coefficients.3.refs_6_), channel_id=1, source_target_pairs={{0,8},{1,9},{2,10},{3,11},{4,12},{5,13},{6,14},{7,15},{8,0},{9,1},... | collective-permute-start | bytes 393224 | tf_op jit(solution)/shard_map/ppermute | solution.py:46
  173.2 9.8 %collective-permute-start.34 = (bf16[512,128]{1,0:T(8,128)(2,1)S(1)}, bf16[512,128]{1,0:T(8,128)(2,1)S(1)}, u32[]{:S(2)}, u32[]{:S(2)}) collective-permute-start(bf16[512,128]{1,0:T(8,128)(2,1)S(1)} %coefficients.3.refs_6_), channel_id=1, source_target_pairs={{0,12},{1,13},{2,14},{3,15},{4,0},{5,1},{6,2},{7,3},{8,4},{9,5},{1... | collective-permute-start | bytes 393224 | tf_op jit(solution)/shard_map/ppermute | solution.py:46
  191.7 14.9 %collective-permute-start.35 = (bf16[4096,128]{1,0:T(8,128)(2,1)S(1)}, bf16[4096,128]{1,0:T(8,128)(2,1)S(1)}, u32[]{:S(2)}, u32[]{:S(2)}) collective-permute-start(bf16[4096,128]{1,0:T(8,128)(2,1)S(1)} %get-tuple-element.26), channel_id=1, source_target_pairs={{0,12},{1,13},{2,14},{3,15},{4,0},{5,1},{6,2},{7,3},{8,4},{9,5},{1... | collective-permute-start | bytes 3145736 | tf_op jit(solution)/shard_map/ppermute | solution.py:46
  191.8 16.5 %collective-permute-start.36 = (bf16[4096,128]{1,0:T(8,128)(2,1)S(1)}, bf16[4096,128]{1,0:T(8,128)(2,1)S(1)}, u32[]{:S(2)}, u32[]{:S(2)}) collective-permute-start(bf16[4096,128]{1,0:T(8,128)(2,1)S(1)} %get-tuple-element.27), channel_id=1, source_target_pairs={{0,8},{1,9},{2,10},{3,11},{4,12},{5,13},{6,14},{7,15},{8,0},{9,1},... | collective-permute-start | bytes 3145736 | tf_op jit(solution)/shard_map/ppermute | solution.py:46
  193.7 25.7 %collective-permute-start.37 = (bf16[4096,128]{1,0:T(8,128)(2,1)S(1)}, bf16[4096,128]{1,0:T(8,128)(2,1)S(1)}, u32[]{:S(2)}, u32[]{:S(2)}) collective-permute-start(bf16[4096,128]{1,0:T(8,128)(2,1)S(1)} %get-tuple-element.28), channel_id=1, source_target_pairs={{0,4},{1,5},{2,6},{3,7},{4,8},{5,9},{6,10},{7,11},{8,12},{9,13},{1... | collective-permute-start | bytes 3145736 | tf_op jit(solution)/shard_map/ppermute | solution.py:46
  (17 other events, 210.4 us)

commit v2 on v0

v2 whole, which is shorter than its diff:
```python
import functools

import jax
import jax.numpy as jnp
from jax import lax
from jax.experimental import pallas as pl
from jax.experimental.pallas import tpu as pltpu
from jax.sharding import PartitionSpec as P

RING = 4
BF16, F32 = jnp.bfloat16, jnp.float32
AXES = ("prow", "pcol")


def device(x, core, y, z):
    return (x * 2 + core) * RING * RING + y * RING + z


def permutation(target):
    pairs = []
    for x in range(RING):
        for core in range(2):
            for y in range(RING):
                for z in range(RING):
                    pairs.append((device(x, core, y, z), device(*target(x, core, y, z))))
    return pairs


def along_u(s):
    return permutation(lambda x, c, y, z: (x, c, (y + s) % RING, z) if c == 0 else (x, c, y, (z + s) % RING))


def along_w(s):
    return permutation(lambda x, c, y, z: (x, c, y, (z + s) % RING) if c == 0 else (x, c, (y + s) % RING, z))


def along_x(s):
    return permutation(lambda x, c, y, z: ((x + s) % RING, c, y, z))


def other_core():
    return permutation(lambda x, c, y, z: (x, 1 - c, y, z))


def send(value, pairs):
    return lax.ppermute(value, AXES, pairs)


def params(mib=16):
    return pltpu.CompilerParams(vmem_limit_bytes=mib * 2**20)


def cost(flops, nbytes):
    return pl.CostEstimate(flops=flops, bytes_accessed=nbytes, transcendentals=0)


def home(place, t, k):
    gone = lax.rem(place[1] - t + RING, RING)
    return jnp.where(place[2] == 0, k * RING + gone, gone * RING + k)


def block_rows(at, width):
    return pl.ds(pl.multiple_of(at * width, width), width)


def stack_kernel(place, *refs):
    blocks, outs = refs[:RING], refs[RING:]
    width = blocks[0].shape[0] // 2
    for s in range(RING):
        rows = block_rows(lax.rem(place[0] - s + RING, RING), width)
        for panel in range(2):
            outs[panel][rows, :] = blocks[s][panel * width:(panel + 1) * width, :]


def stack(place, blocks):
    height, rows = blocks[0].shape
    tile = rows // 4
    out = jax.ShapeDtypeStruct((RING * height // 2, rows), BF16)
    return pl.pallas_call(
        stack_kernel,
        grid_spec=pltpu.PrefetchScalarGridSpec(
            num_scalar_prefetch=1,
            grid=(rows // tile,),
            in_specs=[pl.BlockSpec((height, tile), lambda i, place: (0, i))] * RING,
            out_specs=[pl.BlockSpec((RING * height // 2, tile), lambda i, place: (0, i))] * 2,
        ),
        out_shape=[out, out],
        compiler_params=params(8),
        cost_estimate=cost(0, 4 * RING * height * rows),
        name="stack_reflectors",
    )(place, *blocks)


def transpose_kernel(*refs):
    out = refs[-1]
    at = 0
    for r in refs[:-1]:
        out[:, at:at + r.shape[0]] = r[...].T
        at += r.shape[0]


def transpose(blocks):
    rows = blocks[0].shape[1]
    nb = sum(b.shape[0] for b in blocks)
    tile = 1024
    return pl.pallas_call(
        transpose_kernel,
        grid=(rows // tile,),
        in_specs=[pl.BlockSpec((b.shape[0], tile), lambda i: (0, i)) for b in blocks],
        out_specs=pl.BlockSpec((tile, nb), lambda i: (i, 0)),
        out_shape=jax.ShapeDtypeStruct((rows, nb), BF16),
        compiler_params=params(8),
        cost_estimate=cost(0, 4 * nb * rows),
        name="transpose_reflectors",
    )(*blocks)


def put_home(place, total, outs, width):
    for s in range(RING):
        for t in range(RING):
            for k in range(RING):
                at = t * RING + k
                outs[s][block_rows(home(place, t, k), width), :] = total[
                    at * width:(at + 1) * width, s * 128:(s + 1) * 128
                ].astype(outs[s].dtype)


def take_home(place, sources, width, out):
    for s, source in enumerate(sources):
        for t in range(RING):
            for k in range(RING):
                at = t * RING + k
                out[at * width:(at + 1) * width, s * 128:(s + 1) * 128] = source[block_rows(home(place, t, k), width), :]


def first_sums_kernel(count, width, place, *refs):
    v, z = refs[:count], refs[count:count + RING]
    outs, total = refs[count + RING:count + 2 * RING], refs[-1]
    step = pl.program_id(0)
    left = jnp.concatenate([r[...] for r in v], axis=0)
    right = jnp.concatenate([r[...] for r in z], axis=1)
    part = jnp.dot(left, right, preferred_element_type=F32)

    @pl.when(step == 0)
    def _():
        total[...] = part

    @pl.when(step > 0)
    def _():
        total[...] += part

    @pl.when(step == pl.num_programs(0) - 1)
    def _():
        put_home(place, total, outs, width)


def second_sums_kernel(count, width, place, *refs):
    v, z, flat = refs[:count], refs[count:count + RING], refs[count + RING]
    coeffs, outs = refs[count + RING + 1:count + 2 * RING + 1], refs[count + 2 * RING + 1:count + 3 * RING + 1]
    total, w = refs[-2:]
    step = pl.program_id(0)

    @pl.when(step == 0)
    def _():
        take_home(place, coeffs, width, w)

    left = jnp.concatenate([r[...] for r in v], axis=0)
    old = jnp.concatenate([r[...] for r in z], axis=1).astype(F32)
    right = (old - jnp.dot(flat[...], w[...], preferred_element_type=F32)).astype(BF16)
    part = jnp.dot(left, right, preferred_element_type=F32)

    @pl.when(step == 0)
    def _():
        total[...] = part

    @pl.when(step > 0)
    def _():
        total[...] += part

    @pl.when(step == pl.num_programs(0) - 1)
    def _():
        put_home(place, total, outs, width)


SUMS_TILE = 1024


def sums(place, v, z, flat=None, coeffs=None, tile=None):
    tile = tile or SUMS_TILE
    rows = v[0].shape[1]
    columns = z[0].shape[1]
    nb = sum(b.shape[0] for b in v)
    width = nb // (RING * RING)
    in_specs = [pl.BlockSpec((b.shape[0], tile), lambda i, place: (0, i)) for b in v]
    in_specs += [pl.BlockSpec((tile, columns), lambda i, place: (i, 0))] * RING
    args = list(v) + list(z)
    scratch = [pltpu.VMEM((nb, RING * columns), F32)]
    if flat is not None:
        in_specs += [pl.BlockSpec((tile, nb), lambda i, place: (i, 0))]
        in_specs += [pl.BlockSpec((nb, columns), lambda i, place: (0, 0))] * RING
        args += [flat] + list(coeffs)
        scratch += [pltpu.VMEM((nb, RING * columns), BF16)]
    return pl.pallas_call(
        functools.partial(first_sums_kernel if flat is None else second_sums_kernel, len(v), width),
        grid_spec=pltpu.PrefetchScalarGridSpec(
            num_scalar_prefetch=1,
            grid=(rows // tile,),
            in_specs=in_specs,
            out_specs=[pl.BlockSpec((nb, columns), lambda i, place: (0, 0))] * RING,
            scratch_shapes=scratch,
        ),
        out_shape=[jax.ShapeDtypeStruct((nb, columns), F32 if s == 0 else BF16) for s in range(RING)],
        compiler_params=params(20),
        cost_estimate=cost(2 * nb * rows * RING * columns * (1 if flat is None else 2), 4 * nb * rows),
        name="panel_sums",
    )(place, *args)


def coefficients_kernel(factor, a, b, c, d, out):
    total = a[...] + b[...].astype(F32) + c[...].astype(F32) + d[...].astype(F32)
    out[...] = jnp.dot(
        factor[...], total, preferred_element_type=F32, precision=lax.Precision.HIGHEST
    ).astype(BF16)


def coefficients(factor, parts):
    vmem = pl.BlockSpec(memory_space=pltpu.VMEM)
    return pl.pallas_call(
        coefficients_kernel,
        in_specs=[vmem] * 5,
        out_specs=vmem,
        out_shape=jax.ShapeDtypeStruct(parts[0].shape, BF16),
        compiler_params=params(8),
        cost_estimate=cost(12 * factor.size * parts[0].shape[1], 4 * factor.size),
        name="coefficients",
    )(factor, *parts)


def update_kernel(count, width, place, first, second, *refs):
    w0, w1, outs, w = refs[:count], refs[count:2 * count], refs[2 * count:3 * count], refs[-1]
    nb = first.shape[1]

    @pl.when(pl.program_id(0) == 0)
    def _():
        take_home(place, w0, width, w.at[:nb])
        take_home(place, w1, width, w.at[nb:])

    moved = jnp.dot(first[...], w[:nb, :], preferred_element_type=F32)
    moved += jnp.dot(second[...], w[nb:, :], preferred_element_type=F32)
    for s in range(count):
        outs[s][...] = moved[:, s * 128:(s + 1) * 128].astype(BF16)


UPDATE_TILE = 1024


def update(place, first, second, w0, w1, tile=None):
    tile = tile or UPDATE_TILE
    rows, nb = first.shape
    columns = w0[0].shape[1]
    count = len(w0)
    flat = pl.BlockSpec((tile, nb), lambda i, place: (i, 0))
    small = pl.BlockSpec((nb, columns), lambda i, place: (0, 0))
    return pl.pallas_call(
        functools.partial(update_kernel, count, nb // (RING * RING)),
        grid_spec=pltpu.PrefetchScalarGridSpec(
            num_scalar_prefetch=1,
            grid=(rows // tile,),
            in_specs=[flat, flat] + [small] * (2 * count),
            out_specs=[pl.BlockSpec((tile, columns), lambda i, place: (i, 0))] * count,
            scratch_shapes=[pltpu.VMEM((2 * nb, count * columns), BF16)],
        ),
        out_shape=[jax.ShapeDtypeStruct((rows, columns), BF16)] * count,
        compiler_params=params(),
        cost_estimate=cost(4 * nb * rows * count * columns, 4 * nb * rows),
        name="update",
    )(place, first, second, *w0, *w1)


def subtract_kernel(s, place, z, moved, *refs):
    refs[-1][...] = z[...] - moved[...].astype(F32)


SUB_TILE = 2048


def subtract(place, z, moved, s, out, tile=None):
    tile = tile or SUB_TILE
    rows, columns = moved.shape
    steps = rows // tile

    def whole(i, place):
        return (lax.rem(place[0] + s, RING) * steps + i, 0)

    in_specs = [pl.BlockSpec((tile, columns), whole), pl.BlockSpec((tile, columns), lambda i, place: (i, 0))]
    args = [z, moved]
    if out is not None:
        in_specs.append(pl.BlockSpec(memory_space=pl.ANY))
        args.append(out)
    return pl.pallas_call(
        functools.partial(subtract_kernel, s),
        grid_spec=pltpu.PrefetchScalarGridSpec(
            num_scalar_prefetch=1,
            grid=(steps,),
            in_specs=in_specs,
            out_specs=pl.BlockSpec((tile, columns), whole),
        ),
        out_shape=jax.ShapeDtypeStruct(z.shape, F32),
        input_output_aliases={} if out is None else {3: 0},
        compiler_params=params(8),
        cost_estimate=cost(rows * columns, 10 * rows * columns),
        name="subtract",
    )(place, *args)


def local(z_block, v_panels, t_panels):
    prow, pcol = lax.axis_index("prow"), lax.axis_index("pcol")
    core, y, z = prow % 2, pcol // RING, pcol % RING
    u, w = jnp.where(core == 0, y, z), jnp.where(core == 0, z, y)
    place = jnp.stack([u, w, core]).astype(jnp.int32)
    rows = z_block.shape[0] // RING
    width = v_panels.shape[2]
    factors = jnp.swapaxes(t_panels, 1, 2)

    def chunk(s):
        return ((u + s) % RING) * rows

    def gather(block):
        half = block.shape[0] // 2
        ahead, behind = send(block, along_w(1)), send(block, along_w(-1))
        far_low = send(ahead[:half], along_w(1))
        far_high = send(behind[half:], along_w(-1))
        return [block, ahead, far_low, far_high, behind]

    flat = jnp.swapaxes(v_panels, 1, 2).reshape(2 * width, RING * rows)
    mine = [lax.dynamic_slice(flat, (0, chunk(s)), (2 * width, rows)) for s in range(RING)]
    z_in, mine = lax.optimization_barrier((z_block, mine))
    blocks = stack(place, [mine[0]] + [send(mine[s], along_u(s)) for s in range(1, RING)])

    dealt = [lax.dynamic_slice(z_in, (chunk(s), 0), (rows, z_block.shape[1])).astype(BF16) for s in range(RING)]
    dealt = [dealt[0]] + [send(dealt[s], along_u(s)) for s in range(1, RING)]
    first = gather(blocks[0])
    first, dealt, block, factors = lax.optimization_barrier((first, dealt, blocks[1], factors))
    near = [send(block, along_w(1)), send(block, along_w(-1))]

    def reduce(parts, factor, early, late):
        parts = [parts[0]] + [send(parts[s], along_u(-s)) for s in range(1, RING)]
        total = parts[0]
        for part in parts[1:]:
            total = total + part.astype(F32)
        total = total + send(total, other_core())
        rounded = total.astype(BF16)
        rounded, early = lax.optimization_barrier((rounded, early))
        parts = [total] + [send(rounded, along_x(s)) for s in range(1, RING)]
        parts, late = lax.optimization_barrier((parts, late))
        coeffs = coefficients(factor, parts)
        return [coeffs] + [send(coeffs, along_u(s)) for s in range(1, RING)], early, late

    w0, near, first_flat = reduce(sums(place, first, dealt), factors[0], near, transpose(first))
    second = [block, near[0], send(block, along_w(2)), near[1]]
    w1, _, second_flat = reduce(sums(place, second, dealt, first_flat, w0), factors[1], (), transpose(second))

    def moved(shifts):
        parts = update(place, first_flat, second_flat, [w0[s] for s in shifts], [w1[s] for s in shifts])
        return [part if s == 0 else send(part, along_u(-s)) for s, part in zip(shifts, parts)]

    right, left = moved((1, 3))
    far, own = moved((2, 0))
    out = subtract(place, z_block, own, 0, None)
    out = subtract(place, z_block, right, 1, out)
    out = subtract(place, z_block, left, 3, out)
    return subtract(place, z_block, far, 2, out)


def solution(mesh):
    return jax.shard_map(
        local,
        mesh=mesh,
        in_specs=(P("prow", "pcol"), P(None, "prow", "pcol"), P()),
        out_specs=P("prow", "pcol"),
        check_vma=False,
    )
```

time: 413 us -> 196 us (0.47)
  waiting for transfers between devices: 321 us -> 92.4 us
  matrix products: 56.7 us -> 0 us
  starting transfers between devices: 0.3 us -> 48.2 us
  Pallas kernels: 0 us -> 37.6 us
  between operations: 13.2 us -> 0.22 us
  local copies, waits for them, and re-layouts: 21.1 us -> 13.9 us
    all_gather x2 -> x0, waiting for transfers between devices: 211 us -> none  [local(): lax.all_gather(v_panels[which_panel], 'pcol', axis=1, tiled=True)]
    psum x2 -> x0, waiting for transfers between devices: 109 us -> none  [local(): summed = lax.psum(partial_value, 'prow')]
    ppermute x0 -> x36, waiting for transfers between devices: none -> 92.4 us  [send(): return lax.ppermute(value, AXES, pairs)]
    dot_general x6 -> x0, matrix products: 56.7 us -> none  [the longest x2 27.7 us: local(): jnp.dot(reflectors, coeffs, preferred_element_type=jnp.float32)]
    ppermute x0 -> x36, starting transfers between devices: none -> 48.2 us  [send(): return lax.ppermute(value, AXES, pairs)]
    pallas_call x0 -> x13, Pallas kernels: none -> 37.6 us  [the longest x2 13.7 us: sums(): pl.pallas_call(functools.partial(first_sums_kernel if flat is None else s...]
    sub x1 -> x0, local copies, waits for them, and re-layouts: 8.98 us -> none  [local(): vectors - jnp.dot(reflectors, coeffs, preferred_element_type=jnp.float32)]
    convert_element_type x0 -> x1, local copies, waits for them, and re-layouts: none -> 5.38 us  [local(): lax.dynamic_slice(z_in, (chunk(s), 0), (rows, z_block.shape[1]))]
  transfers between devices with their start and end apart: 4 -> 36, of which waited for: 4 -> 27; matrix products, arithmetic and copies ran while one was open for 6% -> 5% of each run, Pallas kernels for 0% -> 13%
where the time goes in v2:
time: 196 us; the launch traced here: 193 us
  waiting for transfers between devices  92.4 us (47%)
  starting transfers between devices  48.2 us (25%)
  Pallas kernels  37.6 us (19%)
  local copies, waits for them, and re-layouts  13.9 us (7%)
    ppermute x36, waiting for transfers between devices, send(): return lax.ppermute(value, AXES, pairs)  92.4 us
    ppermute x36, starting transfers between devices, send(): return lax.ppermute(value, AXES, pairs)  48.2 us
    pallas_call x2, Pallas kernels, sums(): pl.pallas_call(functools.partial(first_sums_kernel if flat is None else s...  13.7 us
    pallas_call x4, Pallas kernels, subtract(): pl.pallas_call(functools.partial(subtract_kernel, s), grid_spec=pltpu.Pre...  7.89 us
    pallas_call x2, Pallas kernels, update(): pl.pallas_call(functools.partial(update_kernel, count, nb // (RING * RING...  7.27 us
    pallas_call x2, Pallas kernels, transpose(): pl.pallas_call(transpose_kernel, grid=(rows // tile,), in_specs=[pl.Block...  5.44 us
    convert_element_type x1, local copies, waits for them, and re-layouts, local(): lax.dynamic_slice(z_in, (chunk(s), 0), (rows, z_block.shape[1]))  5.38 us
    unnamed x15, local copies, waits for them, and re-layouts  4.13 us
  transfers between devices with their start and end apart: 36, of which 27 were waited for; matrix products, arithmetic and copies ran while one was open for 5% of the time, Pallas kernels for 13%

profile of v2, /device:TPU:0, one launch (start us, length us, event | category | flops | bytes accessed | tf_op | source)
XLA Modules:
  0.0 192.5 jit_solution(14210802624339691278)
XLA Ops:
  0.0 2.5 %constant_dynamic-slice_fusion = (bf16[64,4096]{1,0:T(8,128)(2,1)S(1)}, bf16[64,4096]{1,0:T(8,128)(2,1)S(1)}, bf16[64,4096]{1,0:T(8,128)(2,1)}, bf16[64,4096]{1,0:T(8,128)(2,1)S(1)}) fusion(bf16[64,16384]{1,0:T(8,128)(2,1)} %bitcast.14, s32[]{:T(128)S(6)} %select_n.73, s32[]{:T(128)S(6)} %select_n.71, s32[]{:T(128)S(6)} %select_n.69, s32[]{:T(128)S(6)} %select_n.67), kind=kLoop, calls=%fused_computation.8 | loop fusion | bytes 4194320 | tf_op jit(solution)/shard_map/dynamic_slice | solution.py:336
  4.1 2.9 %collective-permute-start.1 = (bf16[64,4096]{1,0:T(8,128)(2,1)S(1)}, bf16[64,4096]{1,0:T(8,128)(2,1)S(1)}, u32[]{:S(2)}, u32[]{:S(2)}) collective-permute-start(bf16[64,4096]{1,0:T(8,128)(2,1)S(1)} %get-tuple-element.50), channel_id=1, source_target_pairs={{0,8},{1,9},{2,10},{3,11},{4,12},{5,13},{6,14},{7,15},{8,0},{9,1},... | collective-permute-start | bytes 1572872 | tf_op jit(solution)/shard_map/ppermute | solution.py:46
  8.5 4.6 %collective-permute-done.refs_1_ = bf16[64,4096]{1,0:T(8,128)(2,1)S(1)} collective-permute-done((bf16[64,4096]{1,0:T(8,128)(2,1)}, bf16[64,4096]{1,0:T(8,128)(2,1)S(1)}, u32[]{:S(2)}, u32[]{:S(2)}) %collective-permute-start) | collective-permute-done | bytes 524320 | tf_op jit(solution)/shard_map/ppermute | solution.py:46
  13.1 6.9 %collective-permute-done.1.refs_2_ = bf16[64,4096]{1,0:T(8,128)(2,1)S(1)} collective-permute-done((bf16[64,4096]{1,0:T(8,128)(2,1)S(1)}, bf16[64,4096]{1,0:T(8,128)(2,1)S(1)}, u32[]{:S(2)}, u32[]{:S(2)}) %collective-permute-start.1) | collective-permute-done | bytes 524320 | tf_op jit(solution)/shard_map/ppermute | solution.py:46
  21.2 4.1 %collective-permute-start.5 = (bf16[128,4096]{1,0:T(8,128)(2,1)S(1)}, bf16[128,4096]{1,0:T(8,128)(2,1)S(1)}, u32[]{:S(2)}, u32[]{:S(2)}) collective-permute-start(bf16[128,4096]{1,0:T(8,128)(2,1)S(1)} %get-tuple-element.55.refs_0_), channel_id=1, source_target_pairs={{0,3},{1,0},{2,1},{3,2},{4,7},{5,4},{6,5},{7,6},{8,11},{9,8},{10,9... | collective-permute-start | bytes 3145736 | tf_op jit(solution)/shard_map/ppermute | solution.py:46
  25.3 5.4 %dynamic-slice_convert_fusion = (bf16[4096,128]{1,0:T(8,128)(2,1)}, bf16[4096,128]{1,0:T(8,128)(2,1)}, bf16[4096,128]{1,0:T(8,128)(2,1)}, bf16[4096,128]{1,0:T(8,128)(2,1)S(1)}) fusion(f32[16384,128]{1,0:T(8,128)} %z.7, s32[]{:T(128)S(6)} %select_n.73, s32[]{:T(128)S(6)} %select_n.71, s32[]{:T(128)S(6)} %select_n.69, s32[]{:T(128)S(6)} %select_n.67), kind=kLoop, calls=%fused_computation | loop fusion | bytes 8388624 | tf_op jit(solution)/shard_map/convert_element_type | solution.py:340
  30.7 2.1 %collective-permute-start.9 = (bf16[4096,128]{1,0:T(8,128)(2,1)}, bf16[4096,128]{1,0:T(8,128)(2,1)}, u32[]{:S(2)}, u32[]{:S(2)}) collective-permute-start(bf16[4096,128]{1,0:T(8,128)(2,1)} %get-tuple-element.95), channel_id=1, source_target_pairs={{0,12},{1,13},{2,14},{3,15},{4,0},{5,1},{6,2},{7,3},{8,4},{9,5},{1... | collective-permute-start | bytes 3145736 | tf_op jit(solution)/shard_map/ppermute | solution.py:46
  34.7 8.8 %collective-permute-done.5.refs_4_ = bf16[128,4096]{1,0:T(8,128)(2,1)S(1)} collective-permute-done((bf16[128,4096]{1,0:T(8,128)(2,1)S(1)}, bf16[128,4096]{1,0:T(8,128)(2,1)S(1)}, u32[]{:S(2)}, u32[]{:S(2)}) %collective-permute-start.5) | collective-permute-done | bytes 1048608 | tf_op jit(solution)/shard_map/ppermute | solution.py:46
  44.4 3.7 %collective-permute-start.6 = (bf16[64,4096]{1,0:T(8,128)(2,1)}, bf16[64,4096]{1,0:T(8,128)(2,1)}, u32[]{:S(2)}, u32[]{:S(2)}) collective-permute-start(bf16[64,4096]{1,0:T(8,128)(2,1)} %slice.17), channel_id=1, source_target_pairs={{0,3},{1,0},{2,1},{3,2},{4,7},{5,4},{6,5},{7,6},{8,11},{9,8},{10,9... | collective-permute-start | bytes 1572872 | tf_op jit(solution)/shard_map/ppermute | solution.py:46
  48.1 10.0 %collective-permute-done.3.refs_1_ = bf16[128,4096]{1,0:T(8,128)(2,1)S(1)} collective-permute-done((bf16[128,4096]{1,0:T(8,128)(2,1)S(1)}, bf16[128,4096]{1,0:T(8,128)(2,1)S(1)}, u32[]{:S(2)}, u32[]{:S(2)}) %collective-permute-start.3) | collective-permute-done | bytes 1048608 | tf_op jit(solution)/shard_map/ppermute | solution.py:46
  59.0 2.9 %copy.7 = f32[2,512,512]{1,2,0:T(8,128)} copy(f32[2,512,512]{2,1,0:T(8,128)} %param.5) | data formatting | bytes 4194304 | tf_op args[2]
  62.6 4.3 %collective-permute-done.7.refs_6_.refs_5_ = bf16[4096,128]{1,0:T(8,128)(2,1)} collective-permute-done((bf16[4096,128]{1,0:T(8,128)(2,1)}, bf16[4096,128]{1,0:T(8,128)(2,1)}, u32[]{:S(2)}, u32[]{:S(2)}) %collective-permute-start.7) | collective-permute-done | bytes 1048608 | tf_op jit(solution)/shard_map/ppermute | solution.py:46
  66.9 2.9 %collective-permute-done.4.refs_2_ = bf16[64,4096]{1,0:T(8,128)(2,1)} collective-permute-done((bf16[64,4096]{1,0:T(8,128)(2,1)}, bf16[64,4096]{1,0:T(8,128)(2,1)}, u32[]{:S(2)}, u32[]{:S(2)}) %collective-permute-start.4) | collective-permute-done | bytes 524320 | tf_op jit(solution)/shard_map/ppermute | solution.py:46
  73.0 6.0 %panel_sums.2 = (f32[512,128]{1,0:T(8,128)S(1)}, bf16[512,128]{1,0:T(8,128)(2,1)S(1)}, bf16[512,128]{1,0:T(8,128)(2,1)S(1)}, bf16[512,128]{1,0:T(8,128)(2,1)S(1)}) custom-call(s32[3]{0:T(128)S(1)} %pad_add_fusion.place, bf16[128,4096]{1,0:T(8,128)(2,1)S(1)} %copy-done.1, bf16[128,4096]{1,0:T(8,128)(2,1)S(1)} %collective-permute-done.3.refs_1_, ...), custom_call_target="tpu_custom_call" | custom-call | flops 2147483648 | bytes 8388608 | tf_op jit(solution)/shard_map/panel_sums/pallas_call | solution.py:203
  80.9 2.9 %collective-permute-start.11 = (bf16[512,128]{1,0:T(8,128)(2,1)S(1)}, bf16[512,128]{1,0:T(8,128)(2,1)S(1)}, u32[]{:S(2)}, u32[]{:S(2)}) collective-permute-start(bf16[512,128]{1,0:T(8,128)(2,1)S(1)} %get-tuple-element.66), channel_id=1, source_target_pairs={{0,8},{1,9},{2,10},{3,11},{4,12},{5,13},{6,14},{7,15},{8,0},{9,1},... | collective-permute-start | bytes 393224 | tf_op jit(solution)/shard_map/ppermute | solution.py:46
  84.7 4.0 %collective-permute-done.11 = bf16[512,128]{1,0:T(8,128)(2,1)S(1)} collective-permute-done((bf16[512,128]{1,0:T(8,128)(2,1)S(1)}, bf16[512,128]{1,0:T(8,128)(2,1)S(1)}, u32[]{:S(2)}, u32[]{:S(2)}) %collective-permute-start.11) | collective-permute-done | bytes 131104 | tf_op jit(solution)/shard_map/ppermute | solution.py:46
  88.7 2.8 %collective-permute-done.12 = bf16[512,128]{1,0:T(8,128)(2,1)S(1)} collective-permute-done((bf16[512,128]{1,0:T(8,128)(2,1)S(1)}, bf16[512,128]{1,0:T(8,128)(2,1)S(1)}, u32[]{:S(2)}, u32[]{:S(2)}) %collective-permute-start.12) | collective-permute-done | bytes 131104 | tf_op jit(solution)/shard_map/ppermute | solution.py:46
  93.3 2.8 %collective-permute-start.18 = (bf16[512,128]{1,0:T(8,128)(2,1)S(1)}, bf16[512,128]{1,0:T(8,128)(2,1)S(1)}, u32[]{:S(2)}, u32[]{:S(2)}) collective-permute-start(bf16[512,128]{1,0:T(8,128)(2,1)S(1)} %get-tuple-element.69), channel_id=1, source_target_pairs={{0,96},{1,97},{2,98},{3,99},{4,100},{5,101},{6,102},{7,103},{8,104... | collective-permute-start | bytes 393224 | tf_op jit(solution)/shard_map/ppermute | solution.py:46
  98.0 3.8 %transpose_reflectors.2.refs_8_.first = bf16[4096,512]{1,0:T(8,128)(2,1)S(1)} custom-call(bf16[128,4096]{1,0:T(8,128)(2,1)S(1)} %copy-done.1, bf16[128,4096]{1,0:T(8,128)(2,1)S(1)} %collective-permute-done.3.refs_1_, bf16[64,4096]{1,0:T(8,128)(2,1)} %collective-permute-done.4.refs_2_, bf16[64,4096]{1,0:T(8,128)(2,1)} %collective-permute-done.6.refs_3_, ...), custom_call_target="tpu_custom_call" | custom-call | bytes 8388608 | tf_op jit(solution)/shard_map/transpose_reflectors/pallas_call | solution.py:106
  107.4 3.1 %collective-permute-start.21 = (bf16[512,128]{1,0:T(8,128)(2,1)S(1)}, bf16[512,128]{1,0:T(8,128)(2,1)S(1)}, u32[]{:S(2)}, u32[]{:S(2)}) collective-permute-start(bf16[512,128]{1,0:T(8,128)(2,1)S(1)} %coefficients.2.refs_9_.refs_1_), channel_id=1, source_target_pairs={{0,8},{1,9},{2,10},{3,11},{4,12},{5,13},{6,14},{7,15},{8,0},{9,1},... | collective-permute-start | bytes 393224 | tf_op jit(solution)/shard_map/ppermute | solution.py:46
  113.9 2.8 %collective-permute-done.20.refs_10_.refs_0_ = bf16[512,128]{1,0:T(8,128)(2,1)S(1)} collective-permute-done((bf16[512,128]{1,0:T(8,128)(2,1)S(1)}, bf16[512,128]{1,0:T(8,128)(2,1)S(1)}, u32[]{:S(2)}, u32[]{:S(2)}) %collective-permute-start.20) | collective-permute-done | bytes 131104 | tf_op jit(solution)/shard_map/ppermute | solution.py:46
  116.7 7.6 %panel_sums.3 = (f32[512,128]{1,0:T(8,128)S(1)}, bf16[512,128]{1,0:T(8,128)(2,1)S(1)}, bf16[512,128]{1,0:T(8,128)(2,1)S(1)}, bf16[512,128]{1,0:T(8,128)(2,1)S(1)}) custom-call(s32[3]{0:T(128)S(1)} %pad_add_fusion.place, bf16[128,4096]{1,0:T(8,128)(2,1)S(1)} %copy-done.3, bf16[128,4096]{1,0:T(8,128)(2,1)S(1)} %collective-permute-done.14.refs_1_, ...), custom_call_target="tpu_custom_call" | custom-call | flops 4294967296 | bytes 8388608 | tf_op jit(solution)/shard_map/panel_sums/pallas_call | solution.py:203
  124.6 2.1 %collective-permute-start.24 = (bf16[512,128]{1,0:T(8,128)(2,1)S(1)}, bf16[512,128]{1,0:T(8,128)(2,1)S(1)}, u32[]{:S(2)}, u32[]{:S(2)}) collective-permute-start(bf16[512,128]{1,0:T(8,128)(2,1)S(1)} %get-tuple-element.80), channel_id=1, source_target_pairs={{0,8},{1,9},{2,10},{3,11},{4,12},{5,13},{6,14},{7,15},{8,0},{9,1},... | collective-permute-start | bytes 393224 | tf_op jit(solution)/shard_map/ppermute | solution.py:46
  126.8 2.5 %collective-permute-done.23 = bf16[512,128]{1,0:T(8,128)(2,1)S(1)} collective-permute-done((bf16[512,128]{1,0:T(8,128)(2,1)S(1)}, bf16[512,128]{1,0:T(8,128)(2,1)S(1)}, u32[]{:S(2)}, u32[]{:S(2)}) %collective-permute-start.23) | collective-permute-done | bytes 131104 | tf_op jit(solution)/shard_map/ppermute | solution.py:46
  133.0 4.3 %collective-permute-start.26 = (f32[512,128]{1,0:T(8,128)S(1)}, f32[512,128]{1,0:T(8,128)S(1)}, u32[]{:S(2)}, u32[]{:S(2)}) collective-permute-start(f32[512,128]{1,0:T(8,128)S(1)} %convert_add_fusion), channel_id=1, source_target_pairs={{0,16},{1,17},{2,18},{3,19},{4,20},{5,21},{6,22},{7,23},{8,24},{9,... | collective-permute-start | bytes 786440 | tf_op jit(solution)/shard_map/ppermute | solution.py:46
  142.2 2.6 %collective-permute-done.29.d = bf16[512,128]{1,0:T(8,128)(2,1)S(1)} collective-permute-done((bf16[512,128]{1,0:T(8,128)(2,1)S(1)}, bf16[512,128]{1,0:T(8,128)(2,1)S(1)}, u32[]{:S(2)}, u32[]{:S(2)}) %collective-permute-start.29) | collective-permute-done | bytes 131104 | tf_op jit(solution)/shard_map/ppermute | solution.py:46
  146.4 2.3 %collective-permute-done.27.b = bf16[512,128]{1,0:T(8,128)(2,1)S(1)} collective-permute-done((bf16[512,128]{1,0:T(8,128)(2,1)S(1)}, bf16[512,128]{1,0:T(8,128)(2,1)S(1)}, u32[]{:S(2)}, u32[]{:S(2)}) %collective-permute-start.27) | collective-permute-done | bytes 131104 | tf_op jit(solution)/shard_map/ppermute | solution.py:46
  151.8 2.9 %collective-permute-done.33.refs_3_ = bf16[512,128]{1,0:T(8,128)(2,1)S(1)} collective-permute-done((bf16[512,128]{1,0:T(8,128)(2,1)S(1)}, bf16[512,128]{1,0:T(8,128)(2,1)S(1)}, u32[]{:S(2)}, u32[]{:S(2)}) %collective-permute-start.33) | collective-permute-done | bytes 131104 | tf_op jit(solution)/shard_map/ppermute | solution.py:46
  156.1 3.6 %update.3 = (bf16[4096,128]{1,0:T(8,128)(2,1)S(1)}, bf16[4096,128]{1,0:T(8,128)(2,1)S(1)}) custom-call(s32[3]{0:T(128)S(1)} %pad_add_fusion.place, bf16[4096,512]{1,0:T(8,128)(2,1)S(1)} %transpose_reflectors.2.refs_8_.first, bf16[4096,512]{1,0:T(8,128)(2,1)S(1)} %transpose_reflectors.3.second, bf16[512,128]{1,0:T(8,128)(2,1)S(1)} %collective-permute-done.20.refs_10_.refs_0_, ...), custom_call_target="tpu_custom_call" | custom-call | flops 2147483648 | bytes 8388608 | tf_op jit(solution)/shard_map/update/pallas_call | solution.py:264
  160.5 2.5 %collective-permute-start.35 = (bf16[4096,128]{1,0:T(8,128)(2,1)S(1)}, bf16[4096,128]{1,0:T(8,128)(2,1)S(1)}, u32[]{:S(2)}, u32[]{:S(2)}) collective-permute-start(bf16[4096,128]{1,0:T(8,128)(2,1)S(1)} %get-tuple-element.89), channel_id=1, source_target_pairs={{0,12},{1,13},{2,14},{3,15},{4,0},{5,1},{6,2},{7,3},{8,4},{9,5},{1... | collective-permute-start | bytes 3145736 | tf_op jit(solution)/shard_map/ppermute | solution.py:46
  163.0 3.6 %update.2 = (bf16[4096,128]{1,0:T(8,128)(2,1)S(1)}, bf16[4096,128]{1,0:T(8,128)(2,1)S(1)}) custom-call(s32[3]{0:T(128)S(1)} %pad_add_fusion.place, bf16[4096,512]{1,0:T(8,128)(2,1)S(1)} %transpose_reflectors.2.refs_8_.first, bf16[4096,512]{1,0:T(8,128)(2,1)S(1)} %transpose_reflectors.3.second, bf16[512,128]{1,0:T(8,128)(2,1)S(1)} %collective-permute-done.21.refs_11_.refs_0_, ...), custom_call_target="tpu_custom_call" | custom-call | flops 2147483648 | bytes 8388608 | tf_op jit(solution)/shard_map/update/pallas_call | solution.py:264
  168.8 17.8 %collective-permute-done.35.moved = bf16[4096,128]{1,0:T(8,128)(2,1)S(1)} collective-permute-done((bf16[4096,128]{1,0:T(8,128)(2,1)S(1)}, bf16[4096,128]{1,0:T(8,128)(2,1)S(1)}, u32[]{:S(2)}, u32[]{:S(2)}) %collective-permute-start.35) | collective-permute-done | bytes 1048608 | tf_op jit(solution)/shard_map/ppermute | solution.py:46
  (79 shorter events, 51.0 us)
Async XLA Ops:
  2.5 10.6 %collective-permute-start = (bf16[64,4096]{1,0:T(8,128)(2,1)}, bf16[64,4096]{1,0:T(8,128)(2,1)S(1)}, u32[]{:S(2)}, u32[]{:S(2)}) collective-permute-start(bf16[64,4096]{1,0:T(8,128)(2,1)} %get-tuple-element.49), channel_id=1, source_target_pairs={{0,4},{1,5},{2,6},{3,7},{4,8},{5,9},{6,10},{7,11},{8,12},{9,13},{1... | collective-permute-start | bytes 1572872 | tf_op jit(solution)/shard_map/ppermute | solution.py:46
  4.1 15.9 %collective-permute-start.1 = (bf16[64,4096]{1,0:T(8,128)(2,1)S(1)}, bf16[64,4096]{1,0:T(8,128)(2,1)S(1)}, u32[]{:S(2)}, u32[]{:S(2)}) collective-permute-start(bf16[64,4096]{1,0:T(8,128)(2,1)S(1)} %get-tuple-element.50), channel_id=1, source_target_pairs={{0,8},{1,9},{2,10},{3,11},{4,12},{5,13},{6,14},{7,15},{8,0},{9,1},... | collective-permute-start | bytes 1572872 | tf_op jit(solution)/shard_map/ppermute | solution.py:46
  7.0 13.0 %collective-permute-start.2 = (bf16[64,4096]{1,0:T(8,128)(2,1)S(1)}, bf16[64,4096]{1,0:T(8,128)(2,1)S(1)}, u32[]{:S(2)}, u32[]{:S(2)}) collective-permute-start(bf16[64,4096]{1,0:T(8,128)(2,1)S(1)} %get-tuple-element.51), channel_id=1, source_target_pairs={{0,12},{1,13},{2,14},{3,15},{4,0},{5,1},{6,2},{7,3},{8,4},{9,5},{1... | collective-permute-start | bytes 1572872 | tf_op jit(solution)/shard_map/ppermute | solution.py:46
  21.2 22.4 %collective-permute-start.5 = (bf16[128,4096]{1,0:T(8,128)(2,1)S(1)}, bf16[128,4096]{1,0:T(8,128)(2,1)S(1)}, u32[]{:S(2)}, u32[]{:S(2)}) collective-permute-start(bf16[128,4096]{1,0:T(8,128)(2,1)S(1)} %get-tuple-element.55.refs_0_), channel_id=1, source_target_pairs={{0,3},{1,0},{2,1},{3,2},{4,7},{5,4},{6,5},{7,6},{8,11},{9,8},{10,9... | collective-permute-start | bytes 3145736 | tf_op jit(solution)/shard_map/ppermute | solution.py:46
  25.3 32.9 %collective-permute-start.3 = (bf16[128,4096]{1,0:T(8,128)(2,1)S(1)}, bf16[128,4096]{1,0:T(8,128)(2,1)S(1)}, u32[]{:S(2)}, u32[]{:S(2)}) collective-permute-start(bf16[128,4096]{1,0:T(8,128)(2,1)S(1)} %get-tuple-element.55.refs_0_), channel_id=1, source_target_pairs={{0,1},{1,2},{2,3},{3,0},{4,5},{5,6},{6,7},{7,4},{8,9},{9,10},{10,1... | collective-permute-start | bytes 3145736 | tf_op jit(solution)/shard_map/ppermute | solution.py:46
  30.7 31.9 %collective-permute-start.9 = (bf16[4096,128]{1,0:T(8,128)(2,1)}, bf16[4096,128]{1,0:T(8,128)(2,1)}, u32[]{:S(2)}, u32[]{:S(2)}) collective-permute-start(bf16[4096,128]{1,0:T(8,128)(2,1)} %get-tuple-element.95), channel_id=1, source_target_pairs={{0,12},{1,13},{2,14},{3,15},{4,0},{5,1},{6,2},{7,3},{8,4},{9,5},{1... | collective-permute-start | bytes 3145736 | tf_op jit(solution)/shard_map/ppermute | solution.py:46
  32.7 29.9 %collective-permute-start.8 = (bf16[4096,128]{1,0:T(8,128)(2,1)}, bf16[4096,128]{1,0:T(8,128)(2,1)}, u32[]{:S(2)}, u32[]{:S(2)}) collective-permute-start(bf16[4096,128]{1,0:T(8,128)(2,1)} %get-tuple-element.96), channel_id=1, source_target_pairs={{0,8},{1,9},{2,10},{3,11},{4,12},{5,13},{6,14},{7,15},{8,0},{9,1},... | collective-permute-start | bytes 3145736 | tf_op jit(solution)/shard_map/ppermute | solution.py:46
  34.2 32.7 %collective-permute-start.7 = (bf16[4096,128]{1,0:T(8,128)(2,1)}, bf16[4096,128]{1,0:T(8,128)(2,1)}, u32[]{:S(2)}, u32[]{:S(2)}) collective-permute-start(bf16[4096,128]{1,0:T(8,128)(2,1)} %get-tuple-element.97), channel_id=1, source_target_pairs={{0,4},{1,5},{2,6},{3,7},{4,8},{5,9},{6,10},{7,11},{8,12},{9,13},{1... | collective-permute-start | bytes 3145736 | tf_op jit(solution)/shard_map/ppermute | solution.py:46
  44.4 22.4 %collective-permute-start.6 = (bf16[64,4096]{1,0:T(8,128)(2,1)}, bf16[64,4096]{1,0:T(8,128)(2,1)}, u32[]{:S(2)}, u32[]{:S(2)}) collective-permute-start(bf16[64,4096]{1,0:T(8,128)(2,1)} %slice.17), channel_id=1, source_target_pairs={{0,3},{1,0},{2,1},{3,2},{4,7},{5,4},{6,5},{7,6},{8,11},{9,8},{10,9... | collective-permute-start | bytes 1572872 | tf_op jit(solution)/shard_map/ppermute | solution.py:46
  59.0 10.7 %collective-permute-start.4 = (bf16[64,4096]{1,0:T(8,128)(2,1)}, bf16[64,4096]{1,0:T(8,128)(2,1)}, u32[]{:S(2)}, u32[]{:S(2)}) collective-permute-start(bf16[64,4096]{1,0:T(8,128)(2,1)} %slice.16), channel_id=1, source_target_pairs={{0,1},{1,2},{2,3},{3,0},{4,5},{5,6},{6,7},{7,4},{8,9},{9,10},{10,1... | collective-permute-start | bytes 1572872 | tf_op jit(solution)/shard_map/ppermute | solution.py:46
  69.7 23.5 %collective-permute-start.15 = (bf16[128,4096]{1,0:T(8,128)(2,1)}, bf16[128,4096]{1,0:T(8,128)(2,1)S(1)}, u32[]{:S(2)}, u32[]{:S(2)}) collective-permute-start(bf16[128,4096]{1,0:T(8,128)(2,1)} %copy-done.2), channel_id=1, source_target_pairs={{0,3},{1,0},{2,1},{3,2},{4,7},{5,4},{6,5},{7,6},{8,11},{9,8},{10,9... | collective-permute-start | bytes 3145736 | tf_op jit(solution)/shard_map/ppermute | solution.py:46
  69.7 23.5 %collective-permute-start.14 = (bf16[128,4096]{1,0:T(8,128)(2,1)}, bf16[128,4096]{1,0:T(8,128)(2,1)S(1)}, u32[]{:S(2)}, u32[]{:S(2)}) collective-permute-start(bf16[128,4096]{1,0:T(8,128)(2,1)} %copy-done.2), channel_id=1, source_target_pairs={{0,1},{1,2},{2,3},{3,0},{4,5},{5,6},{6,7},{7,4},{8,9},{9,10},{10,1... | collective-permute-start | bytes 3145736 | tf_op jit(solution)/shard_map/ppermute | solution.py:46
  79.0 5.7 %collective-permute-start.10 = (bf16[512,128]{1,0:T(8,128)(2,1)S(1)}, bf16[512,128]{1,0:T(8,128)(2,1)S(1)}, u32[]{:S(2)}, u32[]{:S(2)}) collective-permute-start(bf16[512,128]{1,0:T(8,128)(2,1)S(1)} %get-tuple-element.65), channel_id=1, source_target_pairs={{0,12},{1,13},{2,14},{3,15},{4,0},{5,1},{6,2},{7,3},{8,4},{9,5},{1... | collective-permute-start | bytes 393224 | tf_op jit(solution)/shard_map/ppermute | solution.py:46
  80.9 7.8 %collective-permute-start.11 = (bf16[512,128]{1,0:T(8,128)(2,1)S(1)}, bf16[512,128]{1,0:T(8,128)(2,1)S(1)}, u32[]{:S(2)}, u32[]{:S(2)}) collective-permute-start(bf16[512,128]{1,0:T(8,128)(2,1)S(1)} %get-tuple-element.66), channel_id=1, source_target_pairs={{0,8},{1,9},{2,10},{3,11},{4,12},{5,13},{6,14},{7,15},{8,0},{9,1},... | collective-permute-start | bytes 393224 | tf_op jit(solution)/shard_map/ppermute | solution.py:46
  83.9 7.7 %collective-permute-start.12 = (bf16[512,128]{1,0:T(8,128)(2,1)S(1)}, bf16[512,128]{1,0:T(8,128)(2,1)S(1)}, u32[]{:S(2)}, u32[]{:S(2)}) collective-permute-start(bf16[512,128]{1,0:T(8,128)(2,1)S(1)} %get-tuple-element.67), channel_id=1, source_target_pairs={{0,4},{1,5},{2,6},{3,7},{4,8},{5,9},{6,10},{7,11},{8,12},{9,13},{1... | collective-permute-start | bytes 393224 | tf_op jit(solution)/shard_map/ppermute | solution.py:46
  84.7 26.5 %collective-permute-start.19 = (bf16[128,4096]{1,0:T(8,128)(2,1)S(1)}, bf16[128,4096]{1,0:T(8,128)(2,1)S(1)}, u32[]{:S(2)}, u32[]{:S(2)}) collective-permute-start(bf16[128,4096]{1,0:T(8,128)(2,1)S(1)} %copy-done.3), channel_id=1, source_target_pairs={{0,2},{1,3},{2,0},{3,1},{4,6},{5,7},{6,4},{7,5},{8,10},{9,11},{10,... | collective-permute-start | bytes 3145736 | tf_op jit(solution)/shard_map/ppermute | solution.py:46
  93.3 8.7 %collective-permute-start.18 = (bf16[512,128]{1,0:T(8,128)(2,1)S(1)}, bf16[512,128]{1,0:T(8,128)(2,1)S(1)}, u32[]{:S(2)}, u32[]{:S(2)}) collective-permute-start(bf16[512,128]{1,0:T(8,128)(2,1)S(1)} %get-tuple-element.69), channel_id=1, source_target_pairs={{0,96},{1,97},{2,98},{3,99},{4,100},{5,101},{6,102},{7,103},{8,104... | collective-permute-start | bytes 393224 | tf_op jit(solution)/shard_map/ppermute | solution.py:46
  96.1 7.9 %collective-permute-start.17 = (bf16[512,128]{1,0:T(8,128)(2,1)S(1)}, bf16[512,128]{1,0:T(8,128)(2,1)S(1)}, u32[]{:S(2)}, u32[]{:S(2)}) collective-permute-start(bf16[512,128]{1,0:T(8,128)(2,1)S(1)} %get-tuple-element.69), channel_id=1, source_target_pairs={{0,64},{1,65},{2,66},{3,67},{4,68},{5,69},{6,70},{7,71},{8,72},{9,... | collective-permute-start | bytes 393224 | tf_op jit(solution)/shard_map/ppermute | solution.py:46
  96.9 8.8 %collective-permute-start.16 = (bf16[512,128]{1,0:T(8,128)(2,1)S(1)}, bf16[512,128]{1,0:T(8,128)(2,1)S(1)}, u32[]{:S(2)}, u32[]{:S(2)}) collective-permute-start(bf16[512,128]{1,0:T(8,128)(2,1)S(1)} %get-tuple-element.69), channel_id=1, source_target_pairs={{0,32},{1,33},{2,34},{3,35},{4,36},{5,37},{6,38},{7,39},{8,40},{9,... | collective-permute-start | bytes 393224 | tf_op jit(solution)/shard_map/ppermute | solution.py:46
  107.4 6.5 %collective-permute-start.21 = (bf16[512,128]{1,0:T(8,128)(2,1)S(1)}, bf16[512,128]{1,0:T(8,128)(2,1)S(1)}, u32[]{:S(2)}, u32[]{:S(2)}) collective-permute-start(bf16[512,128]{1,0:T(8,128)(2,1)S(1)} %coefficients.2.refs_9_.refs_1_), channel_id=1, source_target_pairs={{0,8},{1,9},{2,10},{3,11},{4,12},{5,13},{6,14},{7,15},{8,0},{9,1},... | collective-permute-start | bytes 393224 | tf_op jit(solution)/shard_map/ppermute | solution.py:46
  110.5 6.2 %collective-permute-start.20 = (bf16[512,128]{1,0:T(8,128)(2,1)S(1)}, bf16[512,128]{1,0:T(8,128)(2,1)S(1)}, u32[]{:S(2)}, u32[]{:S(2)}) collective-permute-start(bf16[512,128]{1,0:T(8,128)(2,1)S(1)} %coefficients.2.refs_9_.refs_1_), channel_id=1, source_target_pairs={{0,4},{1,5},{2,6},{3,7},{4,8},{5,9},{6,10},{7,11},{8,12},{9,13},{1... | collective-permute-start | bytes 393224 | tf_op jit(solution)/shard_map/ppermute | solution.py:46
  124.6 6.5 %collective-permute-start.24 = (bf16[512,128]{1,0:T(8,128)(2,1)S(1)}, bf16[512,128]{1,0:T(8,128)(2,1)S(1)}, u32[]{:S(2)}, u32[]{:S(2)}) collective-permute-start(bf16[512,128]{1,0:T(8,128)(2,1)S(1)} %get-tuple-element.80), channel_id=1, source_target_pairs={{0,8},{1,9},{2,10},{3,11},{4,12},{5,13},{6,14},{7,15},{8,0},{9,1},... | collective-permute-start | bytes 393224 | tf_op jit(solution)/shard_map/ppermute | solution.py:46
  126.7 6.2 %collective-permute-start.25 = (bf16[512,128]{1,0:T(8,128)(2,1)S(1)}, bf16[512,128]{1,0:T(8,128)(2,1)S(1)}, u32[]{:S(2)}, u32[]{:S(2)}) collective-permute-start(bf16[512,128]{1,0:T(8,128)(2,1)S(1)} %get-tuple-element.81), channel_id=1, source_target_pairs={{0,4},{1,5},{2,6},{3,7},{4,8},{5,9},{6,10},{7,11},{8,12},{9,13},{1... | collective-permute-start | bytes 393224 | tf_op jit(solution)/shard_map/ppermute | solution.py:46
  133.0 5.4 %collective-permute-start.26 = (f32[512,128]{1,0:T(8,128)S(1)}, f32[512,128]{1,0:T(8,128)S(1)}, u32[]{:S(2)}, u32[]{:S(2)}) collective-permute-start(f32[512,128]{1,0:T(8,128)S(1)} %convert_add_fusion), channel_id=1, source_target_pairs={{0,16},{1,17},{2,18},{3,19},{4,20},{5,21},{6,22},{7,23},{8,24},{9,... | collective-permute-start | bytes 786440 | tf_op jit(solution)/shard_map/ppermute | solution.py:46
  138.4 6.4 %collective-permute-start.29 = (bf16[512,128]{1,0:T(8,128)(2,1)S(1)}, bf16[512,128]{1,0:T(8,128)(2,1)S(1)}, u32[]{:S(2)}, u32[]{:S(2)}) collective-permute-start(bf16[512,128]{1,0:T(8,128)(2,1)S(1)} %get-tuple-element.91), channel_id=1, source_target_pairs={{0,96},{1,97},{2,98},{3,99},{4,100},{5,101},{6,102},{7,103},{8,104... | collective-permute-start | bytes 393224 | tf_op jit(solution)/shard_map/ppermute | solution.py:46
  138.5 7.9 %collective-permute-start.28 = (bf16[512,128]{1,0:T(8,128)(2,1)S(1)}, bf16[512,128]{1,0:T(8,128)(2,1)S(1)}, u32[]{:S(2)}, u32[]{:S(2)}) collective-permute-start(bf16[512,128]{1,0:T(8,128)(2,1)S(1)} %get-tuple-element.91), channel_id=1, source_target_pairs={{0,64},{1,65},{2,66},{3,67},{4,68},{5,69},{6,70},{7,71},{8,72},{9,... | collective-permute-start | bytes 393224 | tf_op jit(solution)/shard_map/ppermute | solution.py:46
  139.2 9.5 %collective-permute-start.27 = (bf16[512,128]{1,0:T(8,128)(2,1)S(1)}, bf16[512,128]{1,0:T(8,128)(2,1)S(1)}, u32[]{:S(2)}, u32[]{:S(2)}) collective-permute-start(bf16[512,128]{1,0:T(8,128)(2,1)S(1)} %get-tuple-element.91), channel_id=1, source_target_pairs={{0,32},{1,33},{2,34},{3,35},{4,36},{5,37},{6,38},{7,39},{8,40},{9,... | collective-permute-start | bytes 393224 | tf_op jit(solution)/shard_map/ppermute | solution.py:46
  149.8 6.2 %collective-permute-start.32 = (bf16[512,128]{1,0:T(8,128)(2,1)S(1)}, bf16[512,128]{1,0:T(8,128)(2,1)S(1)}, u32[]{:S(2)}, u32[]{:S(2)}) collective-permute-start(bf16[512,128]{1,0:T(8,128)(2,1)S(1)} %coefficients.3.refs_3_), channel_id=1, source_target_pairs={{0,4},{1,5},{2,6},{3,7},{4,8},{5,9},{6,10},{7,11},{8,12},{9,13},{1... | collective-permute-start | bytes 393224 | tf_op jit(solution)/shard_map/ppermute | solution.py:46
  151.8 11.2 %collective-permute-start.30 = (bf16[512,128]{1,0:T(8,128)(2,1)S(1)}, bf16[512,128]{1,0:T(8,128)(2,1)S(1)}, u32[]{:S(2)}, u32[]{:S(2)}) collective-permute-start(bf16[512,128]{1,0:T(8,128)(2,1)S(1)} %coefficients.3.refs_3_), channel_id=1, source_target_pairs={{0,8},{1,9},{2,10},{3,11},{4,12},{5,13},{6,14},{7,15},{8,0},{9,1},... | collective-permute-start | bytes 393224 | tf_op jit(solution)/shard_map/ppermute | solution.py:46
  159.7 28.9 %collective-permute-start.34 = (bf16[4096,128]{1,0:T(8,128)(2,1)S(1)}, bf16[4096,128]{1,0:T(8,128)(2,1)S(1)}, u32[]{:S(2)}, u32[]{:S(2)}) collective-permute-start(bf16[4096,128]{1,0:T(8,128)(2,1)S(1)} %get-tuple-element.88), channel_id=1, source_target_pairs={{0,4},{1,5},{2,6},{3,7},{4,8},{5,9},{6,10},{7,11},{8,12},{9,13},{1... | collective-permute-start | bytes 3145736 | tf_op jit(solution)/shard_map/ppermute | solution.py:46
  160.5 26.1 %collective-permute-start.35 = (bf16[4096,128]{1,0:T(8,128)(2,1)S(1)}, bf16[4096,128]{1,0:T(8,128)(2,1)S(1)}, u32[]{:S(2)}, u32[]{:S(2)}) collective-permute-start(bf16[4096,128]{1,0:T(8,128)(2,1)S(1)} %get-tuple-element.89), channel_id=1, source_target_pairs={{0,12},{1,13},{2,14},{3,15},{4,0},{5,1},{6,2},{7,3},{8,4},{9,5},{1... | collective-permute-start | bytes 3145736 | tf_op jit(solution)/shard_map/ppermute | solution.py:46
  166.7 23.9 %collective-permute-start.31 = (bf16[4096,128]{1,0:T(8,128)(2,1)S(1)}, bf16[4096,128]{1,0:T(8,128)(2,1)S(1)}, u32[]{:S(2)}, u32[]{:S(2)}) collective-permute-start(bf16[4096,128]{1,0:T(8,128)(2,1)S(1)} %get-tuple-element.87), channel_id=1, source_target_pairs={{0,8},{1,9},{2,10},{3,11},{4,12},{5,13},{6,14},{7,15},{8,0},{9,1},... | collective-permute-start | bytes 3145736 | tf_op jit(solution)/shard_map/ppermute | solution.py:46
  (11 other events, 90.5 us)

commit v3 on v2

v3 whole, which is shorter than its diff:
```python
import functools

import jax
import jax.numpy as jnp
from jax import lax
from jax.experimental import pallas as pl
from jax.experimental.pallas import tpu as pltpu
from jax.sharding import PartitionSpec as P

RING = 4
BF16, F32 = jnp.bfloat16, jnp.float32
AXES = ("prow", "pcol")


def device(x, core, y, z):
    return (x * 2 + core) * RING * RING + y * RING + z


def permutation(target):
    pairs = []
    for x in range(RING):
        for core in range(2):
            for y in range(RING):
                for z in range(RING):
                    pairs.append((device(x, core, y, z), device(*target(x, core, y, z))))
    return pairs


def along_u(s):
    return permutation(lambda x, c, y, z: (x, c, (y + s) % RING, z) if c == 0 else (x, c, y, (z + s) % RING))


def along_w(s):
    return permutation(lambda x, c, y, z: (x, c, y, (z + s) % RING) if c == 0 else (x, c, (y + s) % RING, z))


def along_x(s):
    return permutation(lambda x, c, y, z: ((x + s) % RING, c, y, z))


def other_core():
    return permutation(lambda x, c, y, z: (x, 1 - c, y, z))


def send(value, pairs):
    return lax.ppermute(value, AXES, pairs)


def params(mib=16):
    return pltpu.CompilerParams(vmem_limit_bytes=mib * 2**20)


def cost(flops, nbytes):
    return pl.CostEstimate(flops=flops, bytes_accessed=nbytes, transcendentals=0)


def home(place, t, k):
    gone = lax.rem(place[1] - t + RING, RING)
    return jnp.where(place[2] == 0, k * RING + gone, gone * RING + k)


def block_rows(at, width):
    return pl.ds(pl.multiple_of(at * width, width), width)


def stack_kernel(place, *refs):
    blocks, outs = refs[:RING], refs[RING:]
    width = blocks[0].shape[0] // 2
    for s in range(RING):
        rows = block_rows(lax.rem(place[0] - s + RING, RING), width)
        for panel in range(2):
            outs[panel][rows, :] = blocks[s][panel * width:(panel + 1) * width, :]


def stack(place, blocks):
    height, rows = blocks[0].shape
    tile = rows // 4
    out = jax.ShapeDtypeStruct((RING * height // 2, rows), BF16)
    return pl.pallas_call(
        stack_kernel,
        grid_spec=pltpu.PrefetchScalarGridSpec(
            num_scalar_prefetch=1,
            grid=(rows // tile,),
            in_specs=[pl.BlockSpec((height, tile), lambda i, place: (0, i))] * RING,
            out_specs=[pl.BlockSpec((RING * height // 2, tile), lambda i, place: (0, i))] * 2,
        ),
        out_shape=[out, out],
        compiler_params=params(8),
        cost_estimate=cost(0, 4 * RING * height * rows),
        name="stack_reflectors",
    )(place, *blocks)


def transpose_kernel(*refs):
    out = refs[-1]
    at = 0
    for r in refs[:-1]:
        out[:, at:at + r.shape[0]] = r[...].T
        at += r.shape[0]


def transpose(blocks):
    rows = blocks[0].shape[1]
    nb = sum(b.shape[0] for b in blocks)
    tile = 1024
    return pl.pallas_call(
        transpose_kernel,
        grid=(rows // tile,),
        in_specs=[pl.BlockSpec((b.shape[0], tile), lambda i: (0, i)) for b in blocks],
        out_specs=pl.BlockSpec((tile, nb), lambda i: (i, 0)),
        out_shape=jax.ShapeDtypeStruct((rows, nb), BF16),
        compiler_params=params(8),
        cost_estimate=cost(0, 4 * nb * rows),
        name="transpose_reflectors",
    )(*blocks)


def put_home(place, total, outs, width):
    for s in range(RING):
        for t in range(RING):
            for k in range(RING):
                at = t * RING + k
                outs[s][block_rows(home(place, t, k), width), :] = total[
                    at * width:(at + 1) * width, s * 128:(s + 1) * 128
                ].astype(outs[s].dtype)


def take_home(place, sources, width, out):
    for s, source in enumerate(sources):
        for t in range(RING):
            for k in range(RING):
                at = t * RING + k
                out[at * width:(at + 1) * width, s * 128:(s + 1) * 128] = source[block_rows(home(place, t, k), width), :]


TILE = 1024


def tiles_of(z, tile):
    own, right, far_low, far_high, left = z
    steps = own.shape[0] // tile
    for i in range(steps):
        far = far_low if i < steps // 2 else far_high
        at = (i % (steps // 2)) * tile
        rows = slice(i * tile, (i + 1) * tile)
        yield rows, [own[rows, :], right[rows, :], far[at:at + tile, :], left[rows, :]]


def first_sums_kernel(count, width, place, *refs):
    v, z = refs[:count], refs[count:count + RING + 1]
    outs, total = refs[count + RING + 1:-1], refs[-1]
    for rows, parts in tiles_of(z, TILE):
        left = jnp.concatenate([r[:, rows] for r in v], axis=0)
        part = jnp.dot(left, jnp.concatenate(parts, axis=1), preferred_element_type=F32)
        if rows.start:
            total[...] += part
        else:
            total[...] = part
    put_home(place, total, outs, width)


def second_sums_kernel(count, width, place, *refs):
    v, z, flat = refs[:count], refs[count:count + RING + 1], refs[count + RING + 1]
    coeffs = refs[count + RING + 2:count + 2 * RING + 2]
    outs, total, w = refs[count + 2 * RING + 2:-2], refs[-2], refs[-1]
    take_home(place, coeffs, width, w)
    for rows, parts in tiles_of(z, TILE):
        left = jnp.concatenate([r[:, rows] for r in v], axis=0)
        old = jnp.concatenate(parts, axis=1).astype(F32)
        right = (old - jnp.dot(flat[rows, :], w[...], preferred_element_type=F32)).astype(BF16)
        part = jnp.dot(left, right, preferred_element_type=F32)
        if rows.start:
            total[...] += part
        else:
            total[...] = part
    put_home(place, total, outs, width)


def sums(place, v, z, flat=None, coeffs=()):
    vmem = pl.BlockSpec(memory_space=pltpu.VMEM)
    rows = v[0].shape[1]
    columns = z[0].shape[1]
    nb = sum(b.shape[0] for b in v)
    width = nb // (RING * RING)
    args = list(v) + list(z)
    scratch = [pltpu.VMEM((nb, RING * columns), F32)]
    if flat is not None:
        args += [flat, *coeffs]
        scratch += [pltpu.VMEM((nb, RING * columns), BF16)]
    return pl.pallas_call(
        functools.partial(first_sums_kernel if flat is None else second_sums_kernel, len(v), width),
        in_specs=[pl.BlockSpec(memory_space=pltpu.SMEM)] + [vmem] * len(args),
        out_specs=[vmem] * RING,
        scratch_shapes=scratch,
        out_shape=[jax.ShapeDtypeStruct((nb, columns), F32 if s == 0 else BF16) for s in range(RING)],
        compiler_params=params(SUMS_MIB),
        cost_estimate=cost(2 * nb * rows * RING * columns * (1 if flat is None else 2), 4 * nb * rows),
        name="panel_sums",
    )(place, *args)


SUMS_MIB = 12


def coefficients_kernel(factor, a, b, c, d, out):
    total = a[...] + b[...].astype(F32) + c[...].astype(F32) + d[...].astype(F32)
    out[...] = jnp.dot(
        factor[...], total, preferred_element_type=F32, precision=lax.Precision.HIGHEST
    ).astype(BF16)


def coefficients(factor, parts):
    vmem = pl.BlockSpec(memory_space=pltpu.VMEM)
    return pl.pallas_call(
        coefficients_kernel,
        in_specs=[vmem] * 5,
        out_specs=vmem,
        out_shape=jax.ShapeDtypeStruct(parts[0].shape, BF16),
        compiler_params=params(8),
        cost_estimate=cost(12 * factor.size * parts[0].shape[1], 4 * factor.size),
        name="coefficients",
    )(factor, *parts)


def update_kernel(count, width, place, first, second, *refs):
    w0, w1, outs, w = refs[:count], refs[count:2 * count], refs[2 * count:-1], refs[-1]
    rows, nb = first.shape
    take_home(place, w0, width, w.at[:nb])
    take_home(place, w1, width, w.at[nb:])
    halves = len(outs) // count
    height = rows // halves
    for at in range(0, rows, TILE):
        moved = jnp.dot(first[at:at + TILE, :], w[:nb, :], preferred_element_type=F32)
        moved += jnp.dot(second[at:at + TILE, :], w[nb:, :], preferred_element_type=F32)
        for s in range(count):
            out, start = outs[s * halves + at // height], at % height
            out[start:start + TILE, :] = moved[:, s * 128:(s + 1) * 128].astype(BF16)


def update(place, first, second, w0, w1, halves):
    vmem = pl.BlockSpec(memory_space=pltpu.VMEM)
    rows, nb = first.shape
    columns = w0[0].shape[1]
    count = len(w0)
    return pl.pallas_call(
        functools.partial(update_kernel, count, nb // (RING * RING)),
        in_specs=[pl.BlockSpec(memory_space=pltpu.SMEM)] + [vmem] * (2 + 2 * count),
        out_specs=[vmem] * (count * halves),
        out_shape=[jax.ShapeDtypeStruct((rows // halves, columns), BF16)] * (count * halves),
        scratch_shapes=[pltpu.VMEM((2 * nb, count * columns), BF16)],
        compiler_params=params(UPDATE_MIB),
        cost_estimate=cost(4 * nb * rows * count * columns, 4 * nb * rows),
        name="update",
    )(place, first, second, *w0, *w1)


UPDATE_MIB = 10


def subtract_kernel(s, place, z, moved, *refs):
    refs[-1][...] = z[...] - moved[...].astype(F32)


SUB_TILE = 2048


def subtract(place, z, moved, s, half, out):
    tile = SUB_TILE
    rows, columns = moved.shape
    steps = rows // tile
    chunk = z.shape[0] // RING // tile

    def whole(i, place):
        return (lax.rem(place[0] + s, RING) * chunk + half * chunk // 2 + i, 0)

    in_specs = [pl.BlockSpec((tile, columns), whole), pl.BlockSpec((tile, columns), lambda i, place: (i, 0))]
    args = [z, moved]
    if out is not None:
        in_specs.append(pl.BlockSpec(memory_space=pl.ANY))
        args.append(out)
    return pl.pallas_call(
        functools.partial(subtract_kernel, s),
        grid_spec=pltpu.PrefetchScalarGridSpec(
            num_scalar_prefetch=1,
            grid=(steps,),
            in_specs=in_specs,
            out_specs=pl.BlockSpec((tile, columns), whole),
        ),
        out_shape=jax.ShapeDtypeStruct(z.shape, F32),
        input_output_aliases={} if out is None else {3: 0},
        compiler_params=params(8),
        cost_estimate=cost(rows * columns, 10 * rows * columns),
        name="subtract",
    )(place, *args)


def local(z_block, v_panels, t_panels):
    prow, pcol = lax.axis_index("prow"), lax.axis_index("pcol")
    core, y, z = prow % 2, pcol // RING, pcol % RING
    u, w = jnp.where(core == 0, y, z), jnp.where(core == 0, z, y)
    place = jnp.stack([u, w, core]).astype(jnp.int32)
    rows = z_block.shape[0] // RING
    width = v_panels.shape[2]
    tie = lax.optimization_barrier

    def chunk(s):
        return ((u + s) % RING) * rows

    flat = jnp.swapaxes(v_panels, 1, 2).reshape(2 * width, RING * rows)
    mine = [lax.dynamic_slice(flat, (0, chunk(s)), (2 * width, rows)) for s in range(RING)]
    z_in, t_in, mine = tie((z_block, t_panels, mine))
    blocks = [mine[0]] + [send(mine[s], along_u(s)) for s in range(1, RING)]

    def cut(s, start, size):
        return lax.dynamic_slice(z_in, (chunk(s) + start, 0), (size, z_block.shape[1])).astype(BF16)

    own, right, left = cut(0, 0, rows), cut(1, 0, rows), cut(3, 0, rows)
    far = [cut(2, 0, rows // 2), cut(2, rows // 2, rows // 2)]
    factors = jnp.swapaxes(t_in, 1, 2)
    blocks, own, factors = tie((blocks, own, factors))
    block, later = stack(place, blocks)

    half = block.shape[0] // 2
    ahead, behind = send(block, along_w(1)), send(block, along_w(-1))
    right, left = send(right, along_u(1)), send(left, along_u(-1))
    right, left, far = tie((right, left, far))
    far = [send(far[0], along_u(1)), send(far[1], along_u(-1))]
    far_low, far_high = send(ahead[:half], along_w(1)), send(behind[half:], along_w(-1))
    far = [send(far[0], along_u(1)), send(far[1], along_u(-1))]
    first = [block, ahead, far_low, far_high, behind]
    dealt = [own, right, *far, left]
    first, dealt, later, factors = tie((first, dealt, later, factors))

    def reduce(parts, factor, early, late):
        parts = [parts[0]] + [send(parts[s], along_u(-s)) for s in range(1, RING)]
        total = parts[0]
        for part in parts[1:]:
            total = total + part.astype(F32)
        total, early = tie((total, early))
        total = total + send(total, other_core())
        rounded = total.astype(BF16)
        parts = [total] + [send(rounded, along_x(s)) for s in range(1, RING)]
        parts, late = tie((parts, late))
        coeffs = coefficients(factor, parts)
        return [coeffs] + [send(coeffs, along_u(s)) for s in range(1, RING)], early, late

    parts = sums(place, first, dealt)
    parts, later = tie((parts, later))
    ahead, behind = send(later, along_w(1)), send(later, along_w(-1))
    far_low, far_high = send(ahead[:half], along_w(1)), send(behind[half:], along_w(-1))
    second = [later, ahead, far_low, far_high, behind]
    w0, first_flat, _ = reduce(parts, factors[0], transpose(first), ())
    w1, second_flat, _ = reduce(sums(place, second, dealt, first_flat, w0), factors[1], transpose(second), ())

    def moved(shifts, halves):
        return update(place, first_flat, second_flat, [w0[s] for s in shifts], [w1[s] for s in shifts], halves)

    right, left = moved((1, 3), 1)
    right, left = send(right, along_u(-1)), send(left, along_u(1))
    far, own = moved((2, 0), 1)
    far = send(far, along_u(2))
    out = subtract(place, z_block, own, 0, 0, None)
    out = subtract(place, z_block, right, 1, 0, out)
    out = subtract(place, z_block, left, 3, 0, out)
    return subtract(place, z_block, far, 2, 0, out)


def solution(mesh):
    return jax.shard_map(
        local,
        mesh=mesh,
        in_specs=(P("prow", "pcol"), P(None, "prow", "pcol"), P()),
        out_specs=P("prow", "pcol"),
        check_vma=False,
    )
```

time: 196 us -> 185 us (0.944); the launches traced: 193 us -> 184 us
  waiting for transfers between devices: 92.4 us -> 86 us
  Pallas kernels: 37.6 us -> 35 us
    ppermute x36 -> x40, waiting for transfers between devices: 92.4 us -> 86 us  [send(): return lax.ppermute(value, AXES, pairs)]
    unnamed x15 -> x10, local copies, waits for them, and re-layouts: 4.13 us -> 1.01 us
    pallas_call x2, Pallas kernels: 13.7 us -> 10.7 us  [sums(): pl.pallas_call(functools.partial(first_sums_kernel if flat is None else s...]
    optimization_barrier x0 -> x1, local copies, waits for them, and re-layouts: none -> 2.88 us  [local(): z_in, t_in, mine = tie((z_block, t_panels, mine))]
    convert_element_type x1 -> x2, local copies, waits for them, and re-layouts: 5.38 us -> 6.4 us  [cut(): lax.dynamic_slice(z_in, (chunk(s) + start, 0), (size, z_block.shape[1]))]
    ppermute x36 -> x40, starting transfers between devices: 48.2 us -> 49 us  [send(): return lax.ppermute(value, AXES, pairs)]
  transfers between devices with their start and end apart: 36 -> 40, of which waited for: 27 -> 26; matrix products, arithmetic and copies ran while one was open for 5% -> 5% of each run, Pallas kernels for 13% -> 12%
where the time goes in v3:
time: 185 us; the launch traced here: 184 us
  waiting for transfers between devices  86 us (46%)
  starting transfers between devices  49 us (26%)
  Pallas kernels  35 us (19%)
  local copies, waits for them, and re-layouts  13.3 us (7%)
    ppermute x40, waiting for transfers between devices, send(): return lax.ppermute(value, AXES, pairs)  86 us
    ppermute x40, starting transfers between devices, send(): return lax.ppermute(value, AXES, pairs)  49 us
    pallas_call x2, Pallas kernels, sums(): pl.pallas_call(functools.partial(first_sums_kernel if flat is None else s...  10.7 us
    pallas_call x4, Pallas kernels, subtract(): pl.pallas_call(functools.partial(subtract_kernel, s), grid_spec=pltpu.Pre...  7.89 us
    convert_element_type x2, local copies, waits for them, and re-layouts, cut(): lax.dynamic_slice(z_in, (chunk(s) + start, 0), (size, z_block.shape[1]))  6.4 us
    pallas_call x2, Pallas kernels, transpose(): pl.pallas_call(transpose_kernel, grid=(rows // tile,), in_specs=[pl.Block...  6.18 us
    pallas_call x2, Pallas kernels, update(): pl.pallas_call(functools.partial(update_kernel, count, nb // (RING * RING...  5.82 us
  transfers between devices with their start and end apart: 40, of which 26 were waited for; matrix products, arithmetic and copies ran while one was open for 5% of the time, Pallas kernels for 12%

profile of v3, /device:TPU:0, one launch (start us, length us, event | category | flops | bytes accessed | tf_op | source)
XLA Modules:
  0.0 183.9 jit_solution(14279196117180751432)
XLA Ops:
  0.0 2.7 %constant_dynamic-slice_fusion = (bf16[64,4096]{1,0:T(8,128)(2,1)}, bf16[64,4096]{1,0:T(8,128)(2,1)}, bf16[64,4096]{1,0:T(8,128)(2,1)}, bf16[64,4096]{1,0:T(8,128)(2,1)S(1)}) fusion(bf16[64,16384]{1,0:T(8,128)(2,1)} %bitcast.14, s32[]{:T(128)S(6)} %select_n.78, s32[]{:T(128)S(6)} %select_n.76, s32[]{:T(128)S(6)} %select_n.74, s32[]{:T(128)S(6)} %select_n.72), kind=kLoop, calls=%fused_computation.9 | loop fusion | bytes 4194320 | tf_op jit(solution)/shard_map/dynamic_slice | solution.py:310
  4.4 2.9 %collective-permute-start.1 = (bf16[64,4096]{1,0:T(8,128)(2,1)}, bf16[64,4096]{1,0:T(8,128)(2,1)S(1)}, u32[]{:S(2)}, u32[]{:S(2)}) collective-permute-start(bf16[64,4096]{1,0:T(8,128)(2,1)} %get-tuple-element.66), channel_id=1, source_target_pairs={{0,8},{1,9},{2,10},{3,11},{4,12},{5,13},{6,14},{7,15},{8,0},{9,1},... | collective-permute-start | bytes 1572872 | tf_op jit(solution)/shard_map/ppermute | solution.py:46
  8.6 4.6 %dynamic-slice_convert_fusion = (bf16[4096,128]{1,0:T(8,128)(2,1)}, bf16[4096,128]{1,0:T(8,128)(2,1)}, bf16[4096,128]{1,0:T(8,128)(2,1)S(1)}) fusion(f32[16384,128]{1,0:T(8,128)} %z.7, s32[]{:T(128)S(6)} %select_n.78, s32[]{:T(128)S(6)} %select_n.74, s32[]{:T(128)S(6)} %select_n.72), kind=kLoop, calls=%fused_computation | loop fusion | bytes 6291468 | tf_op jit(solution)/shard_map/convert_element_type | solution.py:315
  15.3 2.9 %copy.7 = f32[2,512,512]{1,2,0:T(8,128)} copy(f32[2,512,512]{2,1,0:T(8,128)} %param.5) | data formatting | bytes 4194304 | tf_op jit(solution)/shard_map/optimization_barrier | solution.py:311
  20.4 2.3 %stack_reflectors.1 = (bf16[128,4096]{1,0:T(8,128)(2,1)}, bf16[128,4096]{1,0:T(8,128)(2,1)S(1)}) custom-call(s32[3]{0:T(128)S(1)} %pad_add_fusion.place, bf16[64,4096]{1,0:T(8,128)(2,1)S(1)} %get-tuple-element.70.refs_0_, bf16[64,4096]{1,0:T(8,128)(2,1)S(1)} %collective-permute-done.refs_1_, bf16[64,4096]{1,0:T(8,128)(2,1)S(1)} %collective-permute-done.1.refs_2_, ...), custom_call_target="tpu_custom_call" | custom-call | bytes 4194304 | tf_op jit(solution)/shard_map/stack_reflectors/pallas_call | solution.py:79
  23.7 4.0 %collective-permute-start.5 = (bf16[128,4096]{1,0:T(8,128)(2,1)}, bf16[128,4096]{1,0:T(8,128)(2,1)S(1)}, u32[]{:S(2)}, u32[]{:S(2)}) collective-permute-start(bf16[128,4096]{1,0:T(8,128)(2,1)} %get-tuple-element.82.refs_0_), channel_id=1, source_target_pairs={{0,3},{1,0},{2,1},{3,2},{4,7},{5,4},{6,5},{7,6},{8,11},{9,8},{10,9... | collective-permute-start | bytes 3145736 | tf_op jit(solution)/shard_map/ppermute | solution.py:46
  29.5 6.3 %collective-permute-done.8.refs_9_ = bf16[4096,128]{1,0:T(8,128)(2,1)} collective-permute-done((bf16[4096,128]{1,0:T(8,128)(2,1)}, bf16[4096,128]{1,0:T(8,128)(2,1)}, u32[]{:S(2)}, u32[]{:S(2)}) %collective-permute-start.8) | collective-permute-done | bytes 1048608 | tf_op jit(solution)/shard_map/ppermute | solution.py:46
  35.8 2.6 %collective-permute-start.9 = (bf16[2048,128]{1,0:T(8,128)(2,1)S(1)}, bf16[2048,128]{1,0:T(8,128)(2,1)S(1)}, u32[]{:S(2)}, u32[]{:S(2)}) collective-permute-start(bf16[2048,128]{1,0:T(8,128)(2,1)S(1)} %get-tuple-element.77), channel_id=1, source_target_pairs={{0,4},{1,5},{2,6},{3,7},{4,8},{5,9},{6,10},{7,11},{8,12},{9,13},{1... | collective-permute-start | bytes 1572872 | tf_op jit(solution)/shard_map/ppermute | solution.py:46
  39.0 6.9 %collective-permute-done.5.refs_4_ = bf16[128,4096]{1,0:T(8,128)(2,1)S(1)} collective-permute-done((bf16[128,4096]{1,0:T(8,128)(2,1)}, bf16[128,4096]{1,0:T(8,128)(2,1)S(1)}, u32[]{:S(2)}, u32[]{:S(2)}) %collective-permute-start.5) | collective-permute-done | bytes 1048608 | tf_op jit(solution)/shard_map/ppermute | solution.py:46
  45.9 2.4 %collective-permute-start.6 = (bf16[64,4096]{1,0:T(8,128)(2,1)S(1)}, bf16[64,4096]{1,0:T(8,128)(2,1)S(1)}, u32[]{:S(2)}, u32[]{:S(2)}) collective-permute-start(bf16[64,4096]{1,0:T(8,128)(2,1)S(1)} %slice.25), channel_id=1, source_target_pairs={{0,3},{1,0},{2,1},{3,2},{4,7},{5,4},{6,5},{7,6},{8,11},{9,8},{10,9... | collective-permute-start | bytes 1572872 | tf_op jit(solution)/shard_map/ppermute | solution.py:46
  53.0 7.3 %collective-permute-done.6.refs_3_ = bf16[64,4096]{1,0:T(8,128)(2,1)S(1)} collective-permute-done((bf16[64,4096]{1,0:T(8,128)(2,1)S(1)}, bf16[64,4096]{1,0:T(8,128)(2,1)S(1)}, u32[]{:S(2)}, u32[]{:S(2)}) %collective-permute-start.6) | collective-permute-done | bytes 524320 | tf_op jit(solution)/shard_map/ppermute | solution.py:46
  60.3 4.3 %collective-permute-done.4.refs_2_ = bf16[64,4096]{1,0:T(8,128)(2,1)S(1)} collective-permute-done((bf16[64,4096]{1,0:T(8,128)(2,1)S(1)}, bf16[64,4096]{1,0:T(8,128)(2,1)S(1)}, u32[]{:S(2)}, u32[]{:S(2)}) %collective-permute-start.4) | collective-permute-done | bytes 524320 | tf_op jit(solution)/shard_map/ppermute | solution.py:46
  64.6 4.4 %panel_sums.2 = (f32[512,128]{1,0:T(8,128)S(1)}, bf16[512,128]{1,0:T(8,128)(2,1)S(1)}, bf16[512,128]{1,0:T(8,128)(2,1)S(1)}, bf16[512,128]{1,0:T(8,128)(2,1)S(1)}) custom-call(s32[3]{0:T(128)S(1)} %pad_add_fusion.place, bf16[128,4096]{1,0:T(8,128)(2,1)} %get-tuple-element.82.refs_0_, bf16[128,4096]{1,0:T(8,128)(2,1)S(1)} %collective-permute-done.3.refs_1_, ...), custom_call_target="tpu_custom_call" | custom-call | flops 2147483648 | bytes 8388608 | tf_op jit(solution)/shard_map/panel_sums/pallas_call | solution.py:190
  69.0 2.8 %collective-permute-start.18 = (bf16[128,4096]{1,0:T(8,128)(2,1)S(1)}, bf16[128,4096]{1,0:T(8,128)(2,1)S(1)}, u32[]{:S(2)}, u32[]{:S(2)}) collective-permute-start(bf16[128,4096]{1,0:T(8,128)(2,1)S(1)} %copy-done.1), channel_id=1, source_target_pairs={{0,3},{1,0},{2,1},{3,2},{4,7},{5,4},{6,5},{7,6},{8,11},{9,8},{10,9... | collective-permute-start | bytes 3145736 | tf_op jit(solution)/shard_map/ppermute | solution.py:46
  75.1 3.6 %transpose_reflectors.2.refs_10_.first = bf16[4096,512]{1,0:T(8,128)(2,1)S(1)} custom-call(bf16[128,4096]{1,0:T(8,128)(2,1)} %get-tuple-element.82.refs_0_, bf16[128,4096]{1,0:T(8,128)(2,1)S(1)} %collective-permute-done.3.refs_1_, bf16[64,4096]{1,0:T(8,128)(2,1)S(1)} %collective-permute-done.4.refs_2_, bf16[64,4096]{1,0:T(8,128)(2,1)S(1)} %collective-permute-done.6.refs_3_, ...), custom_call_target="tpu_custom_call" | custom-call | bytes 8388608 | tf_op jit(solution)/shard_map/transpose_reflectors/pallas_call | solution.py:106
  83.3 3.4 %collective-permute-done.18.refs_4_ = bf16[128,4096]{1,0:T(8,128)(2,1)S(1)} collective-permute-done((bf16[128,4096]{1,0:T(8,128)(2,1)S(1)}, bf16[128,4096]{1,0:T(8,128)(2,1)S(1)}, u32[]{:S(2)}, u32[]{:S(2)}) %collective-permute-start.18) | collective-permute-done | bytes 1048608 | tf_op jit(solution)/shard_map/ppermute | solution.py:46
  86.7 2.6 %collective-permute-start.19 = (bf16[64,4096]{1,0:T(8,128)(2,1)S(1)}, bf16[64,4096]{1,0:T(8,128)(2,1)S(1)}, u32[]{:S(2)}, u32[]{:S(2)}) collective-permute-start(bf16[64,4096]{1,0:T(8,128)(2,1)S(1)} %slice.27), channel_id=1, source_target_pairs={{0,3},{1,0},{2,1},{3,2},{4,7},{5,4},{6,5},{7,6},{8,11},{9,8},{10,9... | collective-permute-start | bytes 1572872 | tf_op jit(solution)/shard_map/ppermute | solution.py:46
  89.6 2.7 %collective-permute-start.23 = (bf16[512,128]{1,0:T(8,128)(2,1)S(1)}, bf16[512,128]{1,0:T(8,128)(2,1)S(1)}, u32[]{:S(2)}, u32[]{:S(2)}) collective-permute-start(bf16[512,128]{1,0:T(8,128)(2,1)S(1)} %get-tuple-element.125), channel_id=1, source_target_pairs={{0,96},{1,97},{2,98},{3,99},{4,100},{5,101},{6,102},{7,103},{8,104... | collective-permute-start | bytes 393224 | tf_op jit(solution)/shard_map/ppermute | solution.py:46
  94.2 3.4 %collective-permute-done.23.d = bf16[512,128]{1,0:T(8,128)(2,1)S(1)} collective-permute-done((bf16[512,128]{1,0:T(8,128)(2,1)S(1)}, bf16[512,128]{1,0:T(8,128)(2,1)S(1)}, u32[]{:S(2)}, u32[]{:S(2)}) %collective-permute-start.23) | collective-permute-done | bytes 131104 | tf_op jit(solution)/shard_map/ppermute | solution.py:46
  97.6 2.3 %collective-permute-done.22.c = bf16[512,128]{1,0:T(8,128)(2,1)S(1)} collective-permute-done((bf16[512,128]{1,0:T(8,128)(2,1)S(1)}, bf16[512,128]{1,0:T(8,128)(2,1)S(1)}, u32[]{:S(2)}, u32[]{:S(2)}) %collective-permute-start.22) | collective-permute-done | bytes 131104 | tf_op jit(solution)/shard_map/ppermute | solution.py:46
  102.3 3.0 %collective-permute-start.26 = (bf16[512,128]{1,0:T(8,128)(2,1)S(1)}, bf16[512,128]{1,0:T(8,128)(2,1)S(1)}, u32[]{:S(2)}, u32[]{:S(2)}) collective-permute-start(bf16[512,128]{1,0:T(8,128)(2,1)S(1)} %coefficients.2.refs_11_.refs_1_), channel_id=1, source_target_pairs={{0,12},{1,13},{2,14},{3,15},{4,0},{5,1},{6,2},{7,3},{8,4},{9,5},{1... | collective-permute-start | bytes 393224 | tf_op jit(solution)/shard_map/ppermute | solution.py:46
  106.3 3.0 %collective-permute-done.26.refs_14_.refs_1_ = bf16[512,128]{1,0:T(8,128)(2,1)S(1)} collective-permute-done((bf16[512,128]{1,0:T(8,128)(2,1)S(1)}, bf16[512,128]{1,0:T(8,128)(2,1)S(1)}, u32[]{:S(2)}, u32[]{:S(2)}) %collective-permute-start.26) | collective-permute-done | bytes 131104 | tf_op jit(solution)/shard_map/ppermute | solution.py:46
  109.3 2.7 %collective-permute-done.25.refs_13_.refs_0_ = bf16[512,128]{1,0:T(8,128)(2,1)S(1)} collective-permute-done((bf16[512,128]{1,0:T(8,128)(2,1)S(1)}, bf16[512,128]{1,0:T(8,128)(2,1)S(1)}, u32[]{:S(2)}, u32[]{:S(2)}) %collective-permute-start.25) | collective-permute-done | bytes 131104 | tf_op jit(solution)/shard_map/ppermute | solution.py:46
  112.9 6.3 %panel_sums.3 = (f32[512,128]{1,0:T(8,128)S(1)}, bf16[512,128]{1,0:T(8,128)(2,1)S(1)}, bf16[512,128]{1,0:T(8,128)(2,1)S(1)}, bf16[512,128]{1,0:T(8,128)(2,1)S(1)}) custom-call(s32[3]{0:T(128)S(1)} %pad_add_fusion.place, bf16[128,4096]{1,0:T(8,128)(2,1)S(1)} %copy-done.1, bf16[128,4096]{1,0:T(8,128)(2,1)S(1)} %collective-permute-done.16.refs_1_, ...), custom_call_target="tpu_custom_call" | custom-call | flops 4294967296 | bytes 8388608 | tf_op jit(solution)/shard_map/panel_sums/pallas_call | solution.py:190
  121.6 2.5 %transpose_reflectors.3.second = bf16[4096,512]{1,0:T(8,128)(2,1)S(1)} custom-call(bf16[128,4096]{1,0:T(8,128)(2,1)S(1)} %copy-done.1, bf16[128,4096]{1,0:T(8,128)(2,1)S(1)} %collective-permute-done.16.refs_1_, bf16[64,4096]{1,0:T(8,128)(2,1)S(1)} %collective-permute-done.17.refs_2_, bf16[64,4096]{1,0:T(8,128)(2,1)S(1)} %collective-permute-done.19.refs_3_, ...), custom_call_target="tpu_custom_call" | custom-call | bytes 8388608 | tf_op jit(solution)/shard_map/transpose_reflectors/pallas_call | solution.py:106
  124.3 2.5 %collective-permute-done.28 = bf16[512,128]{1,0:T(8,128)(2,1)S(1)} collective-permute-done((bf16[512,128]{1,0:T(8,128)(2,1)S(1)}, bf16[512,128]{1,0:T(8,128)(2,1)S(1)}, u32[]{:S(2)}, u32[]{:S(2)}) %collective-permute-start.28) | collective-permute-done | bytes 131104 | tf_op jit(solution)/shard_map/ppermute | solution.py:46
  132.1 4.1 %collective-permute-done.33.d = bf16[512,128]{1,0:T(8,128)(2,1)S(1)} collective-permute-done((bf16[512,128]{1,0:T(8,128)(2,1)S(1)}, bf16[512,128]{1,0:T(8,128)(2,1)S(1)}, u32[]{:S(2)}, u32[]{:S(2)}) %collective-permute-start.33) | collective-permute-done | bytes 131104 | tf_op jit(solution)/shard_map/ppermute | solution.py:46
  143.8 2.3 %collective-permute-done.37.refs_3_ = bf16[512,128]{1,0:T(8,128)(2,1)S(1)} collective-permute-done((bf16[512,128]{1,0:T(8,128)(2,1)S(1)}, bf16[512,128]{1,0:T(8,128)(2,1)S(1)}, u32[]{:S(2)}, u32[]{:S(2)}) %collective-permute-start.37) | collective-permute-done | bytes 131104 | tf_op jit(solution)/shard_map/ppermute | solution.py:46
  148.2 2.9 %update.3 = (bf16[4096,128]{1,0:T(8,128)(2,1)S(1)}, bf16[4096,128]{1,0:T(8,128)(2,1)S(1)}) custom-call(s32[3]{0:T(128)S(1)} %pad_add_fusion.place, bf16[4096,512]{1,0:T(8,128)(2,1)S(1)} %transpose_reflectors.2.refs_10_.first, bf16[4096,512]{1,0:T(8,128)(2,1)S(1)} %transpose_reflectors.3.second, ...), custom_call_target="tpu_custom_call" | custom-call | flops 2147483648 | bytes 8388608 | tf_op jit(solution)/shard_map/update/pallas_call | solution.py:245
  151.2 3.2 %collective-permute-start.39 = (bf16[4096,128]{1,0:T(8,128)(2,1)S(1)}, bf16[4096,128]{1,0:T(8,128)(2,1)S(1)}, u32[]{:S(2)}, u32[]{:S(2)}) collective-permute-start(bf16[4096,128]{1,0:T(8,128)(2,1)S(1)} %get-tuple-element.121), channel_id=1, source_target_pairs={{0,12},{1,13},{2,14},{3,15},{4,0},{5,1},{6,2},{7,3},{8,4},{9,5},{1... | collective-permute-start | bytes 3145736 | tf_op jit(solution)/shard_map/ppermute | solution.py:46
  154.5 2.9 %update.2 = (bf16[4096,128]{1,0:T(8,128)(2,1)S(1)}, bf16[4096,128]{1,0:T(8,128)(2,1)S(1)}) custom-call(s32[3]{0:T(128)S(1)} %pad_add_fusion.place, bf16[4096,512]{1,0:T(8,128)(2,1)S(1)} %transpose_reflectors.2.refs_10_.first, bf16[4096,512]{1,0:T(8,128)(2,1)S(1)} %transpose_reflectors.3.second, ...), custom_call_target="tpu_custom_call" | custom-call | flops 2147483648 | bytes 8388608 | tf_op jit(solution)/shard_map/update/pallas_call | solution.py:245
  159.5 18.5 %collective-permute-done.39.moved = bf16[4096,128]{1,0:T(8,128)(2,1)S(1)} collective-permute-done((bf16[4096,128]{1,0:T(8,128)(2,1)S(1)}, bf16[4096,128]{1,0:T(8,128)(2,1)S(1)}, u32[]{:S(2)}, u32[]{:S(2)}) %collective-permute-start.39) | collective-permute-done | bytes 1048608 | tf_op jit(solution)/shard_map/ppermute | solution.py:46
  (86 shorter events, 55.2 us)
Async XLA Ops:
  2.7 15.5 %collective-permute-start = (bf16[64,4096]{1,0:T(8,128)(2,1)}, bf16[64,4096]{1,0:T(8,128)(2,1)S(1)}, u32[]{:S(2)}, u32[]{:S(2)}) collective-permute-start(bf16[64,4096]{1,0:T(8,128)(2,1)} %get-tuple-element.65), channel_id=1, source_target_pairs={{0,4},{1,5},{2,6},{3,7},{4,8},{5,9},{6,10},{7,11},{8,12},{9,13},{1... | collective-permute-start | bytes 1572872 | tf_op jit(solution)/shard_map/ppermute | solution.py:46
  4.4 16.0 %collective-permute-start.1 = (bf16[64,4096]{1,0:T(8,128)(2,1)}, bf16[64,4096]{1,0:T(8,128)(2,1)S(1)}, u32[]{:S(2)}, u32[]{:S(2)}) collective-permute-start(bf16[64,4096]{1,0:T(8,128)(2,1)} %get-tuple-element.66), channel_id=1, source_target_pairs={{0,8},{1,9},{2,10},{3,11},{4,12},{5,13},{6,14},{7,15},{8,0},{9,1},... | collective-permute-start | bytes 1572872 | tf_op jit(solution)/shard_map/ppermute | solution.py:46
  7.3 13.1 %collective-permute-start.2 = (bf16[64,4096]{1,0:T(8,128)(2,1)}, bf16[64,4096]{1,0:T(8,128)(2,1)S(1)}, u32[]{:S(2)}, u32[]{:S(2)}) collective-permute-start(bf16[64,4096]{1,0:T(8,128)(2,1)} %get-tuple-element.67), channel_id=1, source_target_pairs={{0,12},{1,13},{2,14},{3,15},{4,0},{5,1},{6,2},{7,3},{8,4},{9,5},{1... | collective-permute-start | bytes 1572872 | tf_op jit(solution)/shard_map/ppermute | solution.py:46
  13.3 22.5 %collective-permute-start.8 = (bf16[4096,128]{1,0:T(8,128)(2,1)}, bf16[4096,128]{1,0:T(8,128)(2,1)}, u32[]{:S(2)}, u32[]{:S(2)}) collective-permute-start(bf16[4096,128]{1,0:T(8,128)(2,1)} %get-tuple-element.129), channel_id=1, source_target_pairs={{0,12},{1,13},{2,14},{3,15},{4,0},{5,1},{6,2},{7,3},{8,4},{9,5},{1... | collective-permute-start | bytes 3145736 | tf_op jit(solution)/shard_map/ppermute | solution.py:46
  13.3 22.5 %collective-permute-start.7 = (bf16[4096,128]{1,0:T(8,128)(2,1)}, bf16[4096,128]{1,0:T(8,128)(2,1)}, u32[]{:S(2)}, u32[]{:S(2)}) collective-permute-start(bf16[4096,128]{1,0:T(8,128)(2,1)} %get-tuple-element.130), channel_id=1, source_target_pairs={{0,4},{1,5},{2,6},{3,7},{4,8},{5,9},{6,10},{7,11},{8,12},{9,13},{1... | collective-permute-start | bytes 3145736 | tf_op jit(solution)/shard_map/ppermute | solution.py:46
  23.7 22.2 %collective-permute-start.5 = (bf16[128,4096]{1,0:T(8,128)(2,1)}, bf16[128,4096]{1,0:T(8,128)(2,1)S(1)}, u32[]{:S(2)}, u32[]{:S(2)}) collective-permute-start(bf16[128,4096]{1,0:T(8,128)(2,1)} %get-tuple-element.82.refs_0_), channel_id=1, source_target_pairs={{0,3},{1,0},{2,1},{3,2},{4,7},{5,4},{6,5},{7,6},{8,11},{9,8},{10,9... | collective-permute-start | bytes 3145736 | tf_op jit(solution)/shard_map/ppermute | solution.py:46
  27.7 21.8 %collective-permute-start.3 = (bf16[128,4096]{1,0:T(8,128)(2,1)}, bf16[128,4096]{1,0:T(8,128)(2,1)S(1)}, u32[]{:S(2)}, u32[]{:S(2)}) collective-permute-start(bf16[128,4096]{1,0:T(8,128)(2,1)} %get-tuple-element.82.refs_0_), channel_id=1, source_target_pairs={{0,1},{1,2},{2,3},{3,0},{4,5},{5,6},{6,7},{7,4},{8,9},{9,10},{10,1... | collective-permute-start | bytes 3145736 | tf_op jit(solution)/shard_map/ppermute | solution.py:46
  35.8 13.9 %collective-permute-start.9 = (bf16[2048,128]{1,0:T(8,128)(2,1)S(1)}, bf16[2048,128]{1,0:T(8,128)(2,1)S(1)}, u32[]{:S(2)}, u32[]{:S(2)}) collective-permute-start(bf16[2048,128]{1,0:T(8,128)(2,1)S(1)} %get-tuple-element.77), channel_id=1, source_target_pairs={{0,4},{1,5},{2,6},{3,7},{4,8},{5,9},{6,10},{7,11},{8,12},{9,13},{1... | collective-permute-start | bytes 1572872 | tf_op jit(solution)/shard_map/ppermute | solution.py:46
  38.4 12.8 %collective-permute-start.11 = (bf16[2048,128]{1,0:T(8,128)(2,1)S(1)}, bf16[2048,128]{1,0:T(8,128)(2,1)S(1)}, u32[]{:S(2)}, u32[]{:S(2)}) collective-permute-start(bf16[2048,128]{1,0:T(8,128)(2,1)S(1)} %get-tuple-element.78), channel_id=1, source_target_pairs={{0,12},{1,13},{2,14},{3,15},{4,0},{5,1},{6,2},{7,3},{8,4},{9,5},{1... | collective-permute-start | bytes 1572872 | tf_op jit(solution)/shard_map/ppermute | solution.py:46
  45.9 14.4 %collective-permute-start.6 = (bf16[64,4096]{1,0:T(8,128)(2,1)S(1)}, bf16[64,4096]{1,0:T(8,128)(2,1)S(1)}, u32[]{:S(2)}, u32[]{:S(2)}) collective-permute-start(bf16[64,4096]{1,0:T(8,128)(2,1)S(1)} %slice.25), channel_id=1, source_target_pairs={{0,3},{1,0},{2,1},{3,2},{4,7},{5,4},{6,5},{7,6},{8,11},{9,8},{10,9... | collective-permute-start | bytes 1572872 | tf_op jit(solution)/shard_map/ppermute | solution.py:46
  49.6 15.0 %collective-permute-start.4 = (bf16[64,4096]{1,0:T(8,128)(2,1)S(1)}, bf16[64,4096]{1,0:T(8,128)(2,1)S(1)}, u32[]{:S(2)}, u32[]{:S(2)}) collective-permute-start(bf16[64,4096]{1,0:T(8,128)(2,1)S(1)} %slice.24), channel_id=1, source_target_pairs={{0,1},{1,2},{2,3},{3,0},{4,5},{5,6},{6,7},{7,4},{8,9},{9,10},{10,1... | collective-permute-start | bytes 1572872 | tf_op jit(solution)/shard_map/ppermute | solution.py:46
  49.7 14.9 %collective-permute-start.10 = (bf16[2048,128]{1,0:T(8,128)(2,1)S(1)}, bf16[2048,128]{1,0:T(8,128)(2,1)S(1)}, u32[]{:S(2)}, u32[]{:S(2)}) collective-permute-start(bf16[2048,128]{1,0:T(8,128)(2,1)S(1)} %collective-permute-done.9), channel_id=1, source_target_pairs={{0,4},{1,5},{2,6},{3,7},{4,8},{5,9},{6,10},{7,11},{8,12},{9,13},{1... | collective-permute-start | bytes 1572872 | tf_op jit(solution)/shard_map/ppermute | solution.py:46
  51.2 13.4 %collective-permute-start.12 = (bf16[2048,128]{1,0:T(8,128)(2,1)S(1)}, bf16[2048,128]{1,0:T(8,128)(2,1)S(1)}, u32[]{:S(2)}, u32[]{:S(2)}) collective-permute-start(bf16[2048,128]{1,0:T(8,128)(2,1)S(1)} %collective-permute-done.11), channel_id=1, source_target_pairs={{0,12},{1,13},{2,14},{3,15},{4,0},{5,1},{6,2},{7,3},{8,4},{9,5},{1... | collective-permute-start | bytes 1572872 | tf_op jit(solution)/shard_map/ppermute | solution.py:46
  69.0 17.7 %collective-permute-start.18 = (bf16[128,4096]{1,0:T(8,128)(2,1)S(1)}, bf16[128,4096]{1,0:T(8,128)(2,1)S(1)}, u32[]{:S(2)}, u32[]{:S(2)}) collective-permute-start(bf16[128,4096]{1,0:T(8,128)(2,1)S(1)} %copy-done.1), channel_id=1, source_target_pairs={{0,3},{1,0},{2,1},{3,2},{4,7},{5,4},{6,5},{7,6},{8,11},{9,8},{10,9... | collective-permute-start | bytes 3145736 | tf_op jit(solution)/shard_map/ppermute | solution.py:46
  71.8 17.6 %collective-permute-start.16 = (bf16[128,4096]{1,0:T(8,128)(2,1)S(1)}, bf16[128,4096]{1,0:T(8,128)(2,1)S(1)}, u32[]{:S(2)}, u32[]{:S(2)}) collective-permute-start(bf16[128,4096]{1,0:T(8,128)(2,1)S(1)} %copy-done.1), channel_id=1, source_target_pairs={{0,1},{1,2},{2,3},{3,0},{4,5},{5,6},{6,7},{7,4},{8,9},{9,10},{10,1... | collective-permute-start | bytes 3145736 | tf_op jit(solution)/shard_map/ppermute | solution.py:46
  71.8 6.9 %collective-permute-start.13 = (bf16[512,128]{1,0:T(8,128)(2,1)S(1)}, bf16[512,128]{1,0:T(8,128)(2,1)S(1)}, u32[]{:S(2)}, u32[]{:S(2)}) collective-permute-start(bf16[512,128]{1,0:T(8,128)(2,1)S(1)} %get-tuple-element.98), channel_id=1, source_target_pairs={{0,12},{1,13},{2,14},{3,15},{4,0},{5,1},{6,2},{7,3},{8,4},{9,5},{1... | collective-permute-start | bytes 393224 | tf_op jit(solution)/shard_map/ppermute | solution.py:46
  73.1 7.9 %collective-permute-start.14 = (bf16[512,128]{1,0:T(8,128)(2,1)S(1)}, bf16[512,128]{1,0:T(8,128)(2,1)S(1)}, u32[]{:S(2)}, u32[]{:S(2)}) collective-permute-start(bf16[512,128]{1,0:T(8,128)(2,1)S(1)} %get-tuple-element.99), channel_id=1, source_target_pairs={{0,8},{1,9},{2,10},{3,11},{4,12},{5,13},{6,14},{7,15},{8,0},{9,1},... | collective-permute-start | bytes 393224 | tf_op jit(solution)/shard_map/ppermute | solution.py:46
  74.7 8.4 %collective-permute-start.15 = (bf16[512,128]{1,0:T(8,128)(2,1)S(1)}, bf16[512,128]{1,0:T(8,128)(2,1)S(1)}, u32[]{:S(2)}, u32[]{:S(2)}) collective-permute-start(bf16[512,128]{1,0:T(8,128)(2,1)S(1)} %get-tuple-element.100), channel_id=1, source_target_pairs={{0,4},{1,5},{2,6},{3,7},{4,8},{5,9},{6,10},{7,11},{8,12},{9,13},{1... | collective-permute-start | bytes 393224 | tf_op jit(solution)/shard_map/ppermute | solution.py:46
  86.7 26.2 %collective-permute-start.19 = (bf16[64,4096]{1,0:T(8,128)(2,1)S(1)}, bf16[64,4096]{1,0:T(8,128)(2,1)S(1)}, u32[]{:S(2)}, u32[]{:S(2)}) collective-permute-start(bf16[64,4096]{1,0:T(8,128)(2,1)S(1)} %slice.27), channel_id=1, source_target_pairs={{0,3},{1,0},{2,1},{3,2},{4,7},{5,4},{6,5},{7,6},{8,11},{9,8},{10,9... | collective-permute-start | bytes 1572872 | tf_op jit(solution)/shard_map/ppermute | solution.py:46
  89.5 23.5 %collective-permute-start.17 = (bf16[64,4096]{1,0:T(8,128)(2,1)S(1)}, bf16[64,4096]{1,0:T(8,128)(2,1)S(1)}, u32[]{:S(2)}, u32[]{:S(2)}) collective-permute-start(bf16[64,4096]{1,0:T(8,128)(2,1)S(1)} %slice.26), channel_id=1, source_target_pairs={{0,1},{1,2},{2,3},{3,0},{4,5},{5,6},{6,7},{7,4},{8,9},{9,10},{10,1... | collective-permute-start | bytes 1572872 | tf_op jit(solution)/shard_map/ppermute | solution.py:46
  89.6 8.0 %collective-permute-start.23 = (bf16[512,128]{1,0:T(8,128)(2,1)S(1)}, bf16[512,128]{1,0:T(8,128)(2,1)S(1)}, u32[]{:S(2)}, u32[]{:S(2)}) collective-permute-start(bf16[512,128]{1,0:T(8,128)(2,1)S(1)} %get-tuple-element.125), channel_id=1, source_target_pairs={{0,96},{1,97},{2,98},{3,99},{4,100},{5,101},{6,102},{7,103},{8,104... | collective-permute-start | bytes 393224 | tf_op jit(solution)/shard_map/ppermute | solution.py:46
  92.3 7.6 %collective-permute-start.22 = (bf16[512,128]{1,0:T(8,128)(2,1)S(1)}, bf16[512,128]{1,0:T(8,128)(2,1)S(1)}, u32[]{:S(2)}, u32[]{:S(2)}) collective-permute-start(bf16[512,128]{1,0:T(8,128)(2,1)S(1)} %get-tuple-element.125), channel_id=1, source_target_pairs={{0,64},{1,65},{2,66},{3,67},{4,68},{5,69},{6,70},{7,71},{8,72},{9,... | collective-permute-start | bytes 393224 | tf_op jit(solution)/shard_map/ppermute | solution.py:46
  93.2 8.1 %collective-permute-start.21 = (bf16[512,128]{1,0:T(8,128)(2,1)S(1)}, bf16[512,128]{1,0:T(8,128)(2,1)S(1)}, u32[]{:S(2)}, u32[]{:S(2)}) collective-permute-start(bf16[512,128]{1,0:T(8,128)(2,1)S(1)} %get-tuple-element.125), channel_id=1, source_target_pairs={{0,32},{1,33},{2,34},{3,35},{4,36},{5,37},{6,38},{7,39},{8,40},{9,... | collective-permute-start | bytes 393224 | tf_op jit(solution)/shard_map/ppermute | solution.py:46
  102.3 6.9 %collective-permute-start.26 = (bf16[512,128]{1,0:T(8,128)(2,1)S(1)}, bf16[512,128]{1,0:T(8,128)(2,1)S(1)}, u32[]{:S(2)}, u32[]{:S(2)}) collective-permute-start(bf16[512,128]{1,0:T(8,128)(2,1)S(1)} %coefficients.2.refs_11_.refs_1_), channel_id=1, source_target_pairs={{0,12},{1,13},{2,14},{3,15},{4,0},{5,1},{6,2},{7,3},{8,4},{9,5},{1... | collective-permute-start | bytes 393224 | tf_op jit(solution)/shard_map/ppermute | solution.py:46
  105.4 7.6 %collective-permute-start.24 = (bf16[512,128]{1,0:T(8,128)(2,1)S(1)}, bf16[512,128]{1,0:T(8,128)(2,1)S(1)}, u32[]{:S(2)}, u32[]{:S(2)}) collective-permute-start(bf16[512,128]{1,0:T(8,128)(2,1)S(1)} %coefficients.2.refs_11_.refs_1_), channel_id=1, source_target_pairs={{0,4},{1,5},{2,6},{3,7},{4,8},{5,9},{6,10},{7,11},{8,12},{9,13},{1... | collective-permute-start | bytes 393224 | tf_op jit(solution)/shard_map/ppermute | solution.py:46
  120.3 7.8 %collective-permute-start.29 = (bf16[512,128]{1,0:T(8,128)(2,1)S(1)}, bf16[512,128]{1,0:T(8,128)(2,1)S(1)}, u32[]{:S(2)}, u32[]{:S(2)}) collective-permute-start(bf16[512,128]{1,0:T(8,128)(2,1)S(1)} %get-tuple-element.112), channel_id=1, source_target_pairs={{0,4},{1,5},{2,6},{3,7},{4,8},{5,9},{6,10},{7,11},{8,12},{9,13},{1... | collective-permute-start | bytes 393224 | tf_op jit(solution)/shard_map/ppermute | solution.py:46
  130.4 7.8 %collective-permute-start.32 = (bf16[512,128]{1,0:T(8,128)(2,1)S(1)}, bf16[512,128]{1,0:T(8,128)(2,1)S(1)}, u32[]{:S(2)}, u32[]{:S(2)}) collective-permute-start(bf16[512,128]{1,0:T(8,128)(2,1)S(1)} %get-tuple-element.123), channel_id=1, source_target_pairs={{0,64},{1,65},{2,66},{3,67},{4,68},{5,69},{6,70},{7,71},{8,72},{9,... | collective-permute-start | bytes 393224 | tf_op jit(solution)/shard_map/ppermute | solution.py:46
  131.2 8.8 %collective-permute-start.31 = (bf16[512,128]{1,0:T(8,128)(2,1)S(1)}, bf16[512,128]{1,0:T(8,128)(2,1)S(1)}, u32[]{:S(2)}, u32[]{:S(2)}) collective-permute-start(bf16[512,128]{1,0:T(8,128)(2,1)S(1)} %get-tuple-element.123), channel_id=1, source_target_pairs={{0,32},{1,33},{2,34},{3,35},{4,36},{5,37},{6,38},{7,39},{8,40},{9,... | collective-permute-start | bytes 393224 | tf_op jit(solution)/shard_map/ppermute | solution.py:46
  143.2 11.3 %collective-permute-start.34 = (bf16[512,128]{1,0:T(8,128)(2,1)S(1)}, bf16[512,128]{1,0:T(8,128)(2,1)S(1)}, u32[]{:S(2)}, u32[]{:S(2)}) collective-permute-start(bf16[512,128]{1,0:T(8,128)(2,1)S(1)} %coefficients.3.refs_3_), channel_id=1, source_target_pairs={{0,8},{1,9},{2,10},{3,11},{4,12},{5,13},{6,14},{7,15},{8,0},{9,1},... | collective-permute-start | bytes 393224 | tf_op jit(solution)/shard_map/ppermute | solution.py:46
  151.1 28.8 %collective-permute-start.38 = (bf16[4096,128]{1,0:T(8,128)(2,1)S(1)}, bf16[4096,128]{1,0:T(8,128)(2,1)S(1)}, u32[]{:S(2)}, u32[]{:S(2)}) collective-permute-start(bf16[4096,128]{1,0:T(8,128)(2,1)S(1)} %get-tuple-element.120), channel_id=1, source_target_pairs={{0,4},{1,5},{2,6},{3,7},{4,8},{5,9},{6,10},{7,11},{8,12},{9,13},{1... | collective-permute-start | bytes 3145736 | tf_op jit(solution)/shard_map/ppermute | solution.py:46
  151.2 26.8 %collective-permute-start.39 = (bf16[4096,128]{1,0:T(8,128)(2,1)S(1)}, bf16[4096,128]{1,0:T(8,128)(2,1)S(1)}, u32[]{:S(2)}, u32[]{:S(2)}) collective-permute-start(bf16[4096,128]{1,0:T(8,128)(2,1)S(1)} %get-tuple-element.121), channel_id=1, source_target_pairs={{0,12},{1,13},{2,14},{3,15},{4,0},{5,1},{6,2},{7,3},{8,4},{9,5},{1... | collective-permute-start | bytes 3145736 | tf_op jit(solution)/shard_map/ppermute | solution.py:46
  157.4 24.6 %collective-permute-start.35 = (bf16[4096,128]{1,0:T(8,128)(2,1)S(1)}, bf16[4096,128]{1,0:T(8,128)(2,1)S(1)}, u32[]{:S(2)}, u32[]{:S(2)}) collective-permute-start(bf16[4096,128]{1,0:T(8,128)(2,1)S(1)} %get-tuple-element.119), channel_id=1, source_target_pairs={{0,8},{1,9},{2,10},{3,11},{4,12},{5,13},{6,14},{7,15},{8,0},{9,1},... | collective-permute-start | bytes 3145736 | tf_op jit(solution)/shard_map/ppermute | solution.py:46
  (13 other events, 138.2 us)

commit v4 on v3

--- a/solution.py
+++ b/solution.py
@@ -134,6 +134,7 @@
 
 
 TILE = 1024
+NEAR_FIRST = (0, 1, 3, 2)
 
 
 def tiles_of(z, tile):
@@ -163,7 +164,7 @@
     v, z, flat = refs[:count], refs[count:count + RING + 1], refs[count + RING + 1]
     coeffs = refs[count + RING + 2:count + 2 * RING + 2]
     outs, total, w = refs[count + 2 * RING + 2:-2], refs[-2], refs[-1]
-    take_home(place, coeffs, width, w)
+    take_home(place, [coeffs[NEAR_FIRST.index(s)] for s in range(RING)], width, w)
     for rows, parts in tiles_of(z, TILE):
         left = jnp.concatenate([r[:, rows] for r in v], axis=0)
         old = jnp.concatenate(parts, axis=1).astype(F32)
@@ -185,7 +186,7 @@
     args = list(v) + list(z)
     scratch = [pltpu.VMEM((nb, RING * columns), F32)]
     if flat is not None:
-        args += [flat, *coeffs]
+        args += [flat, *(coeffs[s] for s in NEAR_FIRST)]
         scratch += [pltpu.VMEM((nb, RING * columns), BF16)]
     return pl.pallas_call(
         functools.partial(first_sums_kernel if flat is None else second_sums_kernel, len(v), width),
@@ -332,17 +333,19 @@
     first, dealt, later, factors = tie((first, dealt, later, factors))
 
     def reduce(parts, factor, early, late):
-        parts = [parts[0]] + [send(parts[s], along_u(-s)) for s in range(1, RING)]
+        moved = {s: send(parts[s], along_u(-s)) for s in (2, 1, 3)}
+        parts = [parts[0]] + [moved[s] for s in (2, 1, 3)]
         total = parts[0]
         for part in parts[1:]:
             total = total + part.astype(F32)
         total, early = tie((total, early))
         total = total + send(total, other_core())
         rounded = total.astype(BF16)
-        parts = [total] + [send(rounded, along_x(s)) for s in range(1, RING)]
+        parts = [total] + [send(rounded, along_x(s)) for s in (1, 3, 2)]
         parts, late = tie((parts, late))
         coeffs = coefficients(factor, parts)
-        return [coeffs] + [send(coeffs, along_u(s)) for s in range(1, RING)], early, late
+        moved = {s: send(coeffs, along_u(s)) for s in (1, 3, 2)}
+        return [coeffs, moved[1], moved[2], moved[3]], early, late
 
     parts = sums(place, first, dealt)
     parts, later = tie((parts, later))

time: 185 us -> 182 us (0.984)
  waiting for transfers between devices: 86 us -> 78.3 us
  starting transfers between devices: 49 us -> 53.6 us
    ppermute x40, waiting for transfers between devices: 86 us -> 78.3 us  [send(): return lax.ppermute(value, AXES, pairs)]
    ppermute x40, starting transfers between devices: 49 us -> 53.6 us  [send(): return lax.ppermute(value, AXES, pairs)]
  transfers between devices with their start and end apart: 40 -> 40, of which waited for: 26 -> 25; matrix products, arithmetic and copies ran while one was open for 5% -> 5% of each run, Pallas kernels for 12% -> 12%
where the time goes in v4:
time: 182 us; the launch traced here: 181 us
  waiting for transfers between devices  78.3 us (43%)
  starting transfers between devices  53.6 us (29%)
  Pallas kernels  35 us (19%)
  local copies, waits for them, and re-layouts  13.3 us (7%)
    ppermute x40, waiting for transfers between devices, send(): return lax.ppermute(value, AXES, pairs)  78.3 us
    ppermute x40, starting transfers between devices, send(): return lax.ppermute(value, AXES, pairs)  53.6 us
    pallas_call x2, Pallas kernels, sums(): pl.pallas_call(functools.partial(first_sums_kernel if flat is None else s...  10.7 us
    pallas_call x4, Pallas kernels, subtract(): pl.pallas_call(functools.partial(subtract_kernel, s), grid_spec=pltpu.Pre...  7.89 us
    convert_element_type x2, local copies, waits for them, and re-layouts, cut(): lax.dynamic_slice(z_in, (chunk(s) + start, 0), (size, z_block.shape[1]))  6.4 us
    pallas_call x2, Pallas kernels, transpose(): pl.pallas_call(transpose_kernel, grid=(rows // tile,), in_specs=[pl.Block...  6.18 us
    pallas_call x2, Pallas kernels, update(): pl.pallas_call(functools.partial(update_kernel, count, nb // (RING * RING...  5.82 us
  transfers between devices with their start and end apart: 40, of which 25 were waited for; matrix products, arithmetic and copies ran while one was open for 5% of the time, Pallas kernels for 12%

profile of v4, /device:TPU:0, one launch (start us, length us, event | category | flops | bytes accessed | tf_op | source)
XLA Modules:
  0.0 180.8 jit_solution(9136507788356176676)
XLA Ops:
  0.0 2.7 %constant_dynamic-slice_fusion = (bf16[64,4096]{1,0:T(8,128)(2,1)}, bf16[64,4096]{1,0:T(8,128)(2,1)}, bf16[64,4096]{1,0:T(8,128)(2,1)}, bf16[64,4096]{1,0:T(8,128)(2,1)S(1)}) fusion(bf16[64,16384]{1,0:T(8,128)(2,1)} %bitcast.14, s32[]{:T(128)S(6)} %select_n.78, s32[]{:T(128)S(6)} %select_n.76, s32[]{:T(128)S(6)} %select_n.74, s32[]{:T(128)S(6)} %select_n.72), kind=kLoop, calls=%fused_computation.9 | loop fusion | bytes 4194320 | tf_op jit(solution)/shard_map/dynamic_slice | solution.py:311
  4.4 2.9 %collective-permute-start.1 = (bf16[64,4096]{1,0:T(8,128)(2,1)}, bf16[64,4096]{1,0:T(8,128)(2,1)S(1)}, u32[]{:S(2)}, u32[]{:S(2)}) collective-permute-start(bf16[64,4096]{1,0:T(8,128)(2,1)} %get-tuple-element.66), channel_id=1, source_target_pairs={{0,8},{1,9},{2,10},{3,11},{4,12},{5,13},{6,14},{7,15},{8,0},{9,1},... | collective-permute-start | bytes 1572872 | tf_op jit(solution)/shard_map/ppermute | solution.py:46
  8.6 4.6 %dynamic-slice_convert_fusion = (bf16[4096,128]{1,0:T(8,128)(2,1)}, bf16[4096,128]{1,0:T(8,128)(2,1)}, bf16[4096,128]{1,0:T(8,128)(2,1)S(1)}) fusion(f32[16384,128]{1,0:T(8,128)} %z.7, s32[]{:T(128)S(6)} %select_n.78, s32[]{:T(128)S(6)} %select_n.74, s32[]{:T(128)S(6)} %select_n.72), kind=kLoop, calls=%fused_computation | loop fusion | bytes 6291468 | tf_op jit(solution)/shard_map/convert_element_type | solution.py:316
  13.3 2.0 %collective-permute-start.7 = (bf16[4096,128]{1,0:T(8,128)(2,1)}, bf16[4096,128]{1,0:T(8,128)(2,1)}, u32[]{:S(2)}, u32[]{:S(2)}) collective-permute-start(bf16[4096,128]{1,0:T(8,128)(2,1)} %get-tuple-element.130), channel_id=1, source_target_pairs={{0,4},{1,5},{2,6},{3,7},{4,8},{5,9},{6,10},{7,11},{8,12},{9,13},{1... | collective-permute-start | bytes 3145736 | tf_op jit(solution)/shard_map/ppermute | solution.py:46
  15.3 2.9 %copy.7 = f32[2,512,512]{1,2,0:T(8,128)} copy(f32[2,512,512]{2,1,0:T(8,128)} %param.5) | data formatting | bytes 4194304 | tf_op jit(solution)/shard_map/optimization_barrier | solution.py:312
  18.2 2.1 %collective-permute-done.1.refs_2_ = bf16[64,4096]{1,0:T(8,128)(2,1)S(1)} collective-permute-done((bf16[64,4096]{1,0:T(8,128)(2,1)}, bf16[64,4096]{1,0:T(8,128)(2,1)S(1)}, u32[]{:S(2)}, u32[]{:S(2)}) %collective-permute-start.1) | collective-permute-done | bytes 524320 | tf_op jit(solution)/shard_map/ppermute | solution.py:46
  20.4 2.3 %stack_reflectors.1 = (bf16[128,4096]{1,0:T(8,128)(2,1)}, bf16[128,4096]{1,0:T(8,128)(2,1)S(1)}) custom-call(s32[3]{0:T(128)S(1)} %pad_add_fusion.place, bf16[64,4096]{1,0:T(8,128)(2,1)S(1)} %get-tuple-element.70.refs_0_, bf16[64,4096]{1,0:T(8,128)(2,1)S(1)} %collective-permute-done.refs_1_, bf16[64,4096]{1,0:T(8,128)(2,1)S(1)} %collective-permute-done.1.refs_2_, ...), custom_call_target="tpu_custom_call" | custom-call | bytes 4194304 | tf_op jit(solution)/shard_map/stack_reflectors/pallas_call | solution.py:79
  23.7 4.0 %collective-permute-start.5 = (bf16[128,4096]{1,0:T(8,128)(2,1)}, bf16[128,4096]{1,0:T(8,128)(2,1)S(1)}, u32[]{:S(2)}, u32[]{:S(2)}) collective-permute-start(bf16[128,4096]{1,0:T(8,128)(2,1)} %get-tuple-element.82.refs_0_), channel_id=1, source_target_pairs={{0,3},{1,0},{2,1},{3,2},{4,7},{5,4},{6,5},{7,6},{8,11},{9,8},{10,9... | collective-permute-start | bytes 3145736 | tf_op jit(solution)/shard_map/ppermute | solution.py:46
  29.5 6.3 %collective-permute-done.8.refs_9_ = bf16[4096,128]{1,0:T(8,128)(2,1)} collective-permute-done((bf16[4096,128]{1,0:T(8,128)(2,1)}, bf16[4096,128]{1,0:T(8,128)(2,1)}, u32[]{:S(2)}, u32[]{:S(2)}) %collective-permute-start.8) | collective-permute-done | bytes 1048608 | tf_op jit(solution)/shard_map/ppermute | solution.py:46
  35.8 2.6 %collective-permute-start.9 = (bf16[2048,128]{1,0:T(8,128)(2,1)S(1)}, bf16[2048,128]{1,0:T(8,128)(2,1)S(1)}, u32[]{:S(2)}, u32[]{:S(2)}) collective-permute-start(bf16[2048,128]{1,0:T(8,128)(2,1)S(1)} %get-tuple-element.77), channel_id=1, source_target_pairs={{0,4},{1,5},{2,6},{3,7},{4,8},{5,9},{6,10},{7,11},{8,12},{9,13},{1... | collective-permute-start | bytes 1572872 | tf_op jit(solution)/shard_map/ppermute | solution.py:46
  39.0 6.9 %collective-permute-done.5.refs_4_ = bf16[128,4096]{1,0:T(8,128)(2,1)S(1)} collective-permute-done((bf16[128,4096]{1,0:T(8,128)(2,1)}, bf16[128,4096]{1,0:T(8,128)(2,1)S(1)}, u32[]{:S(2)}, u32[]{:S(2)}) %collective-permute-start.5) | collective-permute-done | bytes 1048608 | tf_op jit(solution)/shard_map/ppermute | solution.py:46
  45.9 2.4 %collective-permute-start.6 = (bf16[64,4096]{1,0:T(8,128)(2,1)S(1)}, bf16[64,4096]{1,0:T(8,128)(2,1)S(1)}, u32[]{:S(2)}, u32[]{:S(2)}) collective-permute-start(bf16[64,4096]{1,0:T(8,128)(2,1)S(1)} %slice.25), channel_id=1, source_target_pairs={{0,3},{1,0},{2,1},{3,2},{4,7},{5,4},{6,5},{7,6},{8,11},{9,8},{10,9... | collective-permute-start | bytes 1572872 | tf_op jit(solution)/shard_map/ppermute | solution.py:46
  53.0 7.3 %collective-permute-done.6.refs_3_ = bf16[64,4096]{1,0:T(8,128)(2,1)S(1)} collective-permute-done((bf16[64,4096]{1,0:T(8,128)(2,1)S(1)}, bf16[64,4096]{1,0:T(8,128)(2,1)S(1)}, u32[]{:S(2)}, u32[]{:S(2)}) %collective-permute-start.6) | collective-permute-done | bytes 524320 | tf_op jit(solution)/shard_map/ppermute | solution.py:46
  60.3 4.3 %collective-permute-done.4.refs_2_ = bf16[64,4096]{1,0:T(8,128)(2,1)S(1)} collective-permute-done((bf16[64,4096]{1,0:T(8,128)(2,1)S(1)}, bf16[64,4096]{1,0:T(8,128)(2,1)S(1)}, u32[]{:S(2)}, u32[]{:S(2)}) %collective-permute-start.4) | collective-permute-done | bytes 524320 | tf_op jit(solution)/shard_map/ppermute | solution.py:46
  64.6 4.4 %panel_sums.2 = (f32[512,128]{1,0:T(8,128)S(1)}, bf16[512,128]{1,0:T(8,128)(2,1)S(1)}, bf16[512,128]{1,0:T(8,128)(2,1)S(1)}, bf16[512,128]{1,0:T(8,128)(2,1)S(1)}) custom-call(s32[3]{0:T(128)S(1)} %pad_add_fusion.place, bf16[128,4096]{1,0:T(8,128)(2,1)} %get-tuple-element.82.refs_0_, bf16[128,4096]{1,0:T(8,128)(2,1)S(1)} %collective-permute-done.3.refs_1_, ...), custom_call_target="tpu_custom_call" | custom-call | flops 2147483648 | bytes 8388608 | tf_op jit(solution)/shard_map/panel_sums/pallas_call | solution.py:191
  69.0 2.8 %collective-permute-start.18 = (bf16[128,4096]{1,0:T(8,128)(2,1)S(1)}, bf16[128,4096]{1,0:T(8,128)(2,1)S(1)}, u32[]{:S(2)}, u32[]{:S(2)}) collective-permute-start(bf16[128,4096]{1,0:T(8,128)(2,1)S(1)} %copy-done.1), channel_id=1, source_target_pairs={{0,3},{1,0},{2,1},{3,2},{4,7},{5,4},{6,5},{7,6},{8,11},{9,8},{10,9... | collective-permute-start | bytes 3145736 | tf_op jit(solution)/shard_map/ppermute | solution.py:46
  75.7 3.6 %transpose_reflectors.2.refs_10_.first = bf16[4096,512]{1,0:T(8,128)(2,1)S(1)} custom-call(bf16[128,4096]{1,0:T(8,128)(2,1)} %get-tuple-element.82.refs_0_, bf16[128,4096]{1,0:T(8,128)(2,1)S(1)} %collective-permute-done.3.refs_1_, bf16[64,4096]{1,0:T(8,128)(2,1)S(1)} %collective-permute-done.4.refs_2_, bf16[64,4096]{1,0:T(8,128)(2,1)S(1)} %collective-permute-done.6.refs_3_, ...), custom_call_target="tpu_custom_call" | custom-call | bytes 8388608 | tf_op jit(solution)/shard_map/transpose_reflectors/pallas_call | solution.py:106
  83.1 3.2 %collective-permute-done.18.refs_4_ = bf16[128,4096]{1,0:T(8,128)(2,1)S(1)} collective-permute-done((bf16[128,4096]{1,0:T(8,128)(2,1)S(1)}, bf16[128,4096]{1,0:T(8,128)(2,1)S(1)}, u32[]{:S(2)}, u32[]{:S(2)}) %collective-permute-start.18) | collective-permute-done | bytes 1048608 | tf_op jit(solution)/shard_map/ppermute | solution.py:46
  86.3 3.3 %collective-permute-start.19 = (bf16[64,4096]{1,0:T(8,128)(2,1)S(1)}, bf16[64,4096]{1,0:T(8,128)(2,1)S(1)}, u32[]{:S(2)}, u32[]{:S(2)}) collective-permute-start(bf16[64,4096]{1,0:T(8,128)(2,1)S(1)} %slice.27), channel_id=1, source_target_pairs={{0,3},{1,0},{2,1},{3,2},{4,7},{5,4},{6,5},{7,6},{8,11},{9,8},{10,9... | collective-permute-start | bytes 1572872 | tf_op jit(solution)/shard_map/ppermute | solution.py:46
  89.8 3.1 %collective-permute-start.23 = (bf16[512,128]{1,0:T(8,128)(2,1)S(1)}, bf16[512,128]{1,0:T(8,128)(2,1)S(1)}, u32[]{:S(2)}, u32[]{:S(2)}) collective-permute-start(bf16[512,128]{1,0:T(8,128)(2,1)S(1)} %get-tuple-element.125), channel_id=1, source_target_pairs={{0,64},{1,65},{2,66},{3,67},{4,68},{5,69},{6,70},{7,71},{8,72},{9,... | collective-permute-start | bytes 393224 | tf_op jit(solution)/shard_map/ppermute | solution.py:46
  95.2 2.5 %collective-permute-done.23.d = bf16[512,128]{1,0:T(8,128)(2,1)S(1)} collective-permute-done((bf16[512,128]{1,0:T(8,128)(2,1)S(1)}, bf16[512,128]{1,0:T(8,128)(2,1)S(1)}, u32[]{:S(2)}, u32[]{:S(2)}) %collective-permute-start.23) | collective-permute-done | bytes 131104 | tf_op jit(solution)/shard_map/ppermute | solution.py:46
  102.3 2.0 %collective-permute-start.25 = (bf16[512,128]{1,0:T(8,128)(2,1)S(1)}, bf16[512,128]{1,0:T(8,128)(2,1)S(1)}, u32[]{:S(2)}, u32[]{:S(2)}) collective-permute-start(bf16[512,128]{1,0:T(8,128)(2,1)S(1)} %coefficients.2.refs_11_.refs_1_), channel_id=1, source_target_pairs={{0,12},{1,13},{2,14},{3,15},{4,0},{5,1},{6,2},{7,3},{8,4},{9,5},{1... | collective-permute-start | bytes 393224 | tf_op jit(solution)/shard_map/ppermute | solution.py:46
  104.6 3.3 %collective-permute-done.26.refs_14_.refs_0_ = bf16[512,128]{1,0:T(8,128)(2,1)S(1)} collective-permute-done((bf16[512,128]{1,0:T(8,128)(2,1)S(1)}, bf16[512,128]{1,0:T(8,128)(2,1)S(1)}, u32[]{:S(2)}, u32[]{:S(2)}) %collective-permute-start.26) | collective-permute-done | bytes 131104 | tf_op jit(solution)/shard_map/ppermute | solution.py:46
  110.5 6.3 %panel_sums.3 = (f32[512,128]{1,0:T(8,128)S(1)}, bf16[512,128]{1,0:T(8,128)(2,1)S(1)}, bf16[512,128]{1,0:T(8,128)(2,1)S(1)}, bf16[512,128]{1,0:T(8,128)(2,1)S(1)}) custom-call(s32[3]{0:T(128)S(1)} %pad_add_fusion.place, bf16[128,4096]{1,0:T(8,128)(2,1)S(1)} %copy-done.1, bf16[128,4096]{1,0:T(8,128)(2,1)S(1)} %collective-permute-done.16.refs_1_, ...), custom_call_target="tpu_custom_call" | custom-call | flops 4294967296 | bytes 8388608 | tf_op jit(solution)/shard_map/panel_sums/pallas_call | solution.py:191
  120.0 2.5 %transpose_reflectors.3.second = bf16[4096,512]{1,0:T(8,128)(2,1)S(1)} custom-call(bf16[128,4096]{1,0:T(8,128)(2,1)S(1)} %copy-done.1, bf16[128,4096]{1,0:T(8,128)(2,1)S(1)} %collective-permute-done.16.refs_1_, bf16[64,4096]{1,0:T(8,128)(2,1)S(1)} %collective-permute-done.17.refs_2_, bf16[64,4096]{1,0:T(8,128)(2,1)S(1)} %collective-permute-done.19.refs_3_, ...), custom_call_target="tpu_custom_call" | custom-call | bytes 8388608 | tf_op jit(solution)/shard_map/transpose_reflectors/pallas_call | solution.py:106
  126.5 2.3 %collective-permute-start.33 = (bf16[512,128]{1,0:T(8,128)(2,1)S(1)}, bf16[512,128]{1,0:T(8,128)(2,1)S(1)}, u32[]{:S(2)}, u32[]{:S(2)}) collective-permute-start(bf16[512,128]{1,0:T(8,128)(2,1)S(1)} %get-tuple-element.123), channel_id=1, source_target_pairs={{0,64},{1,65},{2,66},{3,67},{4,68},{5,69},{6,70},{7,71},{8,72},{9,... | collective-permute-start | bytes 393224 | tf_op jit(solution)/shard_map/ppermute | solution.py:46
  130.8 3.6 %collective-permute-done.33.d = bf16[512,128]{1,0:T(8,128)(2,1)S(1)} collective-permute-done((bf16[512,128]{1,0:T(8,128)(2,1)S(1)}, bf16[512,128]{1,0:T(8,128)(2,1)S(1)}, u32[]{:S(2)}, u32[]{:S(2)}) %collective-permute-start.33) | collective-permute-done | bytes 131104 | tf_op jit(solution)/shard_map/ppermute | solution.py:46
  142.8 2.2 %collective-permute-done.36.refs_2_ = bf16[512,128]{1,0:T(8,128)(2,1)S(1)} collective-permute-done((bf16[512,128]{1,0:T(8,128)(2,1)S(1)}, bf16[512,128]{1,0:T(8,128)(2,1)S(1)}, u32[]{:S(2)}, u32[]{:S(2)}) %collective-permute-start.36) | collective-permute-done | bytes 131104 | tf_op jit(solution)/shard_map/ppermute | solution.py:46
  145.1 2.9 %update.3 = (bf16[4096,128]{1,0:T(8,128)(2,1)S(1)}, bf16[4096,128]{1,0:T(8,128)(2,1)S(1)}) custom-call(s32[3]{0:T(128)S(1)} %pad_add_fusion.place, bf16[4096,512]{1,0:T(8,128)(2,1)S(1)} %transpose_reflectors.2.refs_10_.first, bf16[4096,512]{1,0:T(8,128)(2,1)S(1)} %transpose_reflectors.3.second, ...), custom_call_target="tpu_custom_call" | custom-call | flops 2147483648 | bytes 8388608 | tf_op jit(solution)/shard_map/update/pallas_call | solution.py:246
  148.1 3.2 %collective-permute-start.39 = (bf16[4096,128]{1,0:T(8,128)(2,1)S(1)}, bf16[4096,128]{1,0:T(8,128)(2,1)S(1)}, u32[]{:S(2)}, u32[]{:S(2)}) collective-permute-start(bf16[4096,128]{1,0:T(8,128)(2,1)S(1)} %get-tuple-element.121), channel_id=1, source_target_pairs={{0,12},{1,13},{2,14},{3,15},{4,0},{5,1},{6,2},{7,3},{8,4},{9,5},{1... | collective-permute-start | bytes 3145736 | tf_op jit(solution)/shard_map/ppermute | solution.py:46
  151.3 2.9 %update.2 = (bf16[4096,128]{1,0:T(8,128)(2,1)S(1)}, bf16[4096,128]{1,0:T(8,128)(2,1)S(1)}) custom-call(s32[3]{0:T(128)S(1)} %pad_add_fusion.place, bf16[4096,512]{1,0:T(8,128)(2,1)S(1)} %transpose_reflectors.2.refs_10_.first, bf16[4096,512]{1,0:T(8,128)(2,1)S(1)} %transpose_reflectors.3.second, ...), custom_call_target="tpu_custom_call" | custom-call | flops 2147483648 | bytes 8388608 | tf_op jit(solution)/shard_map/update/pallas_call | solution.py:246
  156.3 18.5 %collective-permute-done.39.moved = bf16[4096,128]{1,0:T(8,128)(2,1)S(1)} collective-permute-done((bf16[4096,128]{1,0:T(8,128)(2,1)S(1)}, bf16[4096,128]{1,0:T(8,128)(2,1)S(1)}, u32[]{:S(2)}, u32[]{:S(2)}) %collective-permute-start.39) | collective-permute-done | bytes 1048608 | tf_op jit(solution)/shard_map/ppermute | solution.py:46
  (86 shorter events, 54.3 us)
Async XLA Ops:
  2.7 15.5 %collective-permute-start = (bf16[64,4096]{1,0:T(8,128)(2,1)}, bf16[64,4096]{1,0:T(8,128)(2,1)S(1)}, u32[]{:S(2)}, u32[]{:S(2)}) collective-permute-start(bf16[64,4096]{1,0:T(8,128)(2,1)} %get-tuple-element.65), channel_id=1, source_target_pairs={{0,4},{1,5},{2,6},{3,7},{4,8},{5,9},{6,10},{7,11},{8,12},{9,13},{1... | collective-permute-start | bytes 1572872 | tf_op jit(solution)/shard_map/ppermute | solution.py:46
  4.4 16.0 %collective-permute-start.1 = (bf16[64,4096]{1,0:T(8,128)(2,1)}, bf16[64,4096]{1,0:T(8,128)(2,1)S(1)}, u32[]{:S(2)}, u32[]{:S(2)}) collective-permute-start(bf16[64,4096]{1,0:T(8,128)(2,1)} %get-tuple-element.66), channel_id=1, source_target_pairs={{0,8},{1,9},{2,10},{3,11},{4,12},{5,13},{6,14},{7,15},{8,0},{9,1},... | collective-permute-start | bytes 1572872 | tf_op jit(solution)/shard_map/ppermute | solution.py:46
  7.3 13.1 %collective-permute-start.2 = (bf16[64,4096]{1,0:T(8,128)(2,1)}, bf16[64,4096]{1,0:T(8,128)(2,1)S(1)}, u32[]{:S(2)}, u32[]{:S(2)}) collective-permute-start(bf16[64,4096]{1,0:T(8,128)(2,1)} %get-tuple-element.67), channel_id=1, source_target_pairs={{0,12},{1,13},{2,14},{3,15},{4,0},{5,1},{6,2},{7,3},{8,4},{9,5},{1... | collective-permute-start | bytes 1572872 | tf_op jit(solution)/shard_map/ppermute | solution.py:46
  13.3 22.5 %collective-permute-start.8 = (bf16[4096,128]{1,0:T(8,128)(2,1)}, bf16[4096,128]{1,0:T(8,128)(2,1)}, u32[]{:S(2)}, u32[]{:S(2)}) collective-permute-start(bf16[4096,128]{1,0:T(8,128)(2,1)} %get-tuple-element.129), channel_id=1, source_target_pairs={{0,12},{1,13},{2,14},{3,15},{4,0},{5,1},{6,2},{7,3},{8,4},{9,5},{1... | collective-permute-start | bytes 3145736 | tf_op jit(solution)/shard_map/ppermute | solution.py:46
  13.3 22.5 %collective-permute-start.7 = (bf16[4096,128]{1,0:T(8,128)(2,1)}, bf16[4096,128]{1,0:T(8,128)(2,1)}, u32[]{:S(2)}, u32[]{:S(2)}) collective-permute-start(bf16[4096,128]{1,0:T(8,128)(2,1)} %get-tuple-element.130), channel_id=1, source_target_pairs={{0,4},{1,5},{2,6},{3,7},{4,8},{5,9},{6,10},{7,11},{8,12},{9,13},{1... | collective-permute-start | bytes 3145736 | tf_op jit(solution)/shard_map/ppermute | solution.py:46
  23.7 22.2 %collective-permute-start.5 = (bf16[128,4096]{1,0:T(8,128)(2,1)}, bf16[128,4096]{1,0:T(8,128)(2,1)S(1)}, u32[]{:S(2)}, u32[]{:S(2)}) collective-permute-start(bf16[128,4096]{1,0:T(8,128)(2,1)} %get-tuple-element.82.refs_0_), channel_id=1, source_target_pairs={{0,3},{1,0},{2,1},{3,2},{4,7},{5,4},{6,5},{7,6},{8,11},{9,8},{10,9... | collective-permute-start | bytes 3145736 | tf_op jit(solution)/shard_map/ppermute | solution.py:46
  27.7 21.8 %collective-permute-start.3 = (bf16[128,4096]{1,0:T(8,128)(2,1)}, bf16[128,4096]{1,0:T(8,128)(2,1)S(1)}, u32[]{:S(2)}, u32[]{:S(2)}) collective-permute-start(bf16[128,4096]{1,0:T(8,128)(2,1)} %get-tuple-element.82.refs_0_), channel_id=1, source_target_pairs={{0,1},{1,2},{2,3},{3,0},{4,5},{5,6},{6,7},{7,4},{8,9},{9,10},{10,1... | collective-permute-start | bytes 3145736 | tf_op jit(solution)/shard_map/ppermute | solution.py:46
  35.8 13.9 %collective-permute-start.9 = (bf16[2048,128]{1,0:T(8,128)(2,1)S(1)}, bf16[2048,128]{1,0:T(8,128)(2,1)S(1)}, u32[]{:S(2)}, u32[]{:S(2)}) collective-permute-start(bf16[2048,128]{1,0:T(8,128)(2,1)S(1)} %get-tuple-element.77), channel_id=1, source_target_pairs={{0,4},{1,5},{2,6},{3,7},{4,8},{5,9},{6,10},{7,11},{8,12},{9,13},{1... | collective-permute-start | bytes 1572872 | tf_op jit(solution)/shard_map/ppermute | solution.py:46
  38.4 12.8 %collective-permute-start.11 = (bf16[2048,128]{1,0:T(8,128)(2,1)S(1)}, bf16[2048,128]{1,0:T(8,128)(2,1)S(1)}, u32[]{:S(2)}, u32[]{:S(2)}) collective-permute-start(bf16[2048,128]{1,0:T(8,128)(2,1)S(1)} %get-tuple-element.78), channel_id=1, source_target_pairs={{0,12},{1,13},{2,14},{3,15},{4,0},{5,1},{6,2},{7,3},{8,4},{9,5},{1... | collective-permute-start | bytes 1572872 | tf_op jit(solution)/shard_map/ppermute | solution.py:46
  45.9 14.4 %collective-permute-start.6 = (bf16[64,4096]{1,0:T(8,128)(2,1)S(1)}, bf16[64,4096]{1,0:T(8,128)(2,1)S(1)}, u32[]{:S(2)}, u32[]{:S(2)}) collective-permute-start(bf16[64,4096]{1,0:T(8,128)(2,1)S(1)} %slice.25), channel_id=1, source_target_pairs={{0,3},{1,0},{2,1},{3,2},{4,7},{5,4},{6,5},{7,6},{8,11},{9,8},{10,9... | collective-permute-start | bytes 1572872 | tf_op jit(solution)/shard_map/ppermute | solution.py:46
  49.6 15.0 %collective-permute-start.4 = (bf16[64,4096]{1,0:T(8,128)(2,1)S(1)}, bf16[64,4096]{1,0:T(8,128)(2,1)S(1)}, u32[]{:S(2)}, u32[]{:S(2)}) collective-permute-start(bf16[64,4096]{1,0:T(8,128)(2,1)S(1)} %slice.24), channel_id=1, source_target_pairs={{0,1},{1,2},{2,3},{3,0},{4,5},{5,6},{6,7},{7,4},{8,9},{9,10},{10,1... | collective-permute-start | bytes 1572872 | tf_op jit(solution)/shard_map/ppermute | solution.py:46
  49.7 14.9 %collective-permute-start.10 = (bf16[2048,128]{1,0:T(8,128)(2,1)S(1)}, bf16[2048,128]{1,0:T(8,128)(2,1)S(1)}, u32[]{:S(2)}, u32[]{:S(2)}) collective-permute-start(bf16[2048,128]{1,0:T(8,128)(2,1)S(1)} %collective-permute-done.9), channel_id=1, source_target_pairs={{0,4},{1,5},{2,6},{3,7},{4,8},{5,9},{6,10},{7,11},{8,12},{9,13},{1... | collective-permute-start | bytes 1572872 | tf_op jit(solution)/shard_map/ppermute | solution.py:46
  51.2 13.4 %collective-permute-start.12 = (bf16[2048,128]{1,0:T(8,128)(2,1)S(1)}, bf16[2048,128]{1,0:T(8,128)(2,1)S(1)}, u32[]{:S(2)}, u32[]{:S(2)}) collective-permute-start(bf16[2048,128]{1,0:T(8,128)(2,1)S(1)} %collective-permute-done.11), channel_id=1, source_target_pairs={{0,12},{1,13},{2,14},{3,15},{4,0},{5,1},{6,2},{7,3},{8,4},{9,5},{1... | collective-permute-start | bytes 1572872 | tf_op jit(solution)/shard_map/ppermute | solution.py:46
  69.0 17.3 %collective-permute-start.18 = (bf16[128,4096]{1,0:T(8,128)(2,1)S(1)}, bf16[128,4096]{1,0:T(8,128)(2,1)S(1)}, u32[]{:S(2)}, u32[]{:S(2)}) collective-permute-start(bf16[128,4096]{1,0:T(8,128)(2,1)S(1)} %copy-done.1), channel_id=1, source_target_pairs={{0,3},{1,0},{2,1},{3,2},{4,7},{5,4},{6,5},{7,6},{8,11},{9,8},{10,9... | collective-permute-start | bytes 3145736 | tf_op jit(solution)/shard_map/ppermute | solution.py:46
  71.8 17.8 %collective-permute-start.16 = (bf16[128,4096]{1,0:T(8,128)(2,1)S(1)}, bf16[128,4096]{1,0:T(8,128)(2,1)S(1)}, u32[]{:S(2)}, u32[]{:S(2)}) collective-permute-start(bf16[128,4096]{1,0:T(8,128)(2,1)S(1)} %copy-done.1), channel_id=1, source_target_pairs={{0,1},{1,2},{2,3},{3,0},{4,5},{5,6},{6,7},{7,4},{8,9},{9,10},{10,1... | collective-permute-start | bytes 3145736 | tf_op jit(solution)/shard_map/ppermute | solution.py:46
  71.8 7.9 %collective-permute-start.13 = (bf16[512,128]{1,0:T(8,128)(2,1)S(1)}, bf16[512,128]{1,0:T(8,128)(2,1)S(1)}, u32[]{:S(2)}, u32[]{:S(2)}) collective-permute-start(bf16[512,128]{1,0:T(8,128)(2,1)S(1)} %get-tuple-element.98), channel_id=1, source_target_pairs={{0,8},{1,9},{2,10},{3,11},{4,12},{5,13},{6,14},{7,15},{8,0},{9,1},... | collective-permute-start | bytes 393224 | tf_op jit(solution)/shard_map/ppermute | solution.py:46
  73.6 7.5 %collective-permute-start.14 = (bf16[512,128]{1,0:T(8,128)(2,1)S(1)}, bf16[512,128]{1,0:T(8,128)(2,1)S(1)}, u32[]{:S(2)}, u32[]{:S(2)}) collective-permute-start(bf16[512,128]{1,0:T(8,128)(2,1)S(1)} %get-tuple-element.99), channel_id=1, source_target_pairs={{0,12},{1,13},{2,14},{3,15},{4,0},{5,1},{6,2},{7,3},{8,4},{9,5},{1... | collective-permute-start | bytes 393224 | tf_op jit(solution)/shard_map/ppermute | solution.py:46
  75.3 7.6 %collective-permute-start.15 = (bf16[512,128]{1,0:T(8,128)(2,1)S(1)}, bf16[512,128]{1,0:T(8,128)(2,1)S(1)}, u32[]{:S(2)}, u32[]{:S(2)}) collective-permute-start(bf16[512,128]{1,0:T(8,128)(2,1)S(1)} %get-tuple-element.100), channel_id=1, source_target_pairs={{0,4},{1,5},{2,6},{3,7},{4,8},{5,9},{6,10},{7,11},{8,12},{9,13},{1... | collective-permute-start | bytes 393224 | tf_op jit(solution)/shard_map/ppermute | solution.py:46
  83.0 6.7 %collective-permute-start.20 = (f32[512,128]{1,0:T(8,128)S(1)}, f32[512,128]{1,0:T(8,128)S(1)}, u32[]{:S(2)}, u32[]{:S(2)}) collective-permute-start(f32[512,128]{1,0:T(8,128)S(1)} %convert_add_fusion.1), channel_id=1, source_target_pairs={{0,16},{1,17},{2,18},{3,19},{4,20},{5,21},{6,22},{7,23},{8,24},{9,... | collective-permute-start | bytes 786440 | tf_op jit(solution)/shard_map/ppermute | solution.py:46
  86.3 24.2 %collective-permute-start.19 = (bf16[64,4096]{1,0:T(8,128)(2,1)S(1)}, bf16[64,4096]{1,0:T(8,128)(2,1)S(1)}, u32[]{:S(2)}, u32[]{:S(2)}) collective-permute-start(bf16[64,4096]{1,0:T(8,128)(2,1)S(1)} %slice.27), channel_id=1, source_target_pairs={{0,3},{1,0},{2,1},{3,2},{4,7},{5,4},{6,5},{7,6},{8,11},{9,8},{10,9... | collective-permute-start | bytes 1572872 | tf_op jit(solution)/shard_map/ppermute | solution.py:46
  89.7 20.9 %collective-permute-start.17 = (bf16[64,4096]{1,0:T(8,128)(2,1)S(1)}, bf16[64,4096]{1,0:T(8,128)(2,1)S(1)}, u32[]{:S(2)}, u32[]{:S(2)}) collective-permute-start(bf16[64,4096]{1,0:T(8,128)(2,1)S(1)} %slice.26), channel_id=1, source_target_pairs={{0,1},{1,2},{2,3},{3,0},{4,5},{5,6},{6,7},{7,4},{8,9},{9,10},{10,1... | collective-permute-start | bytes 1572872 | tf_op jit(solution)/shard_map/ppermute | solution.py:46
  89.8 7.8 %collective-permute-start.23 = (bf16[512,128]{1,0:T(8,128)(2,1)S(1)}, bf16[512,128]{1,0:T(8,128)(2,1)S(1)}, u32[]{:S(2)}, u32[]{:S(2)}) collective-permute-start(bf16[512,128]{1,0:T(8,128)(2,1)S(1)} %get-tuple-element.125), channel_id=1, source_target_pairs={{0,64},{1,65},{2,66},{3,67},{4,68},{5,69},{6,70},{7,71},{8,72},{9,... | collective-permute-start | bytes 393224 | tf_op jit(solution)/shard_map/ppermute | solution.py:46
  101.3 6.6 %collective-permute-start.26 = (bf16[512,128]{1,0:T(8,128)(2,1)S(1)}, bf16[512,128]{1,0:T(8,128)(2,1)S(1)}, u32[]{:S(2)}, u32[]{:S(2)}) collective-permute-start(bf16[512,128]{1,0:T(8,128)(2,1)S(1)} %coefficients.2.refs_11_.refs_1_), channel_id=1, source_target_pairs={{0,8},{1,9},{2,10},{3,11},{4,12},{5,13},{6,14},{7,15},{8,0},{9,1},... | collective-permute-start | bytes 393224 | tf_op jit(solution)/shard_map/ppermute | solution.py:46
  102.3 6.6 %collective-permute-start.25 = (bf16[512,128]{1,0:T(8,128)(2,1)S(1)}, bf16[512,128]{1,0:T(8,128)(2,1)S(1)}, u32[]{:S(2)}, u32[]{:S(2)}) collective-permute-start(bf16[512,128]{1,0:T(8,128)(2,1)S(1)} %coefficients.2.refs_11_.refs_1_), channel_id=1, source_target_pairs={{0,12},{1,13},{2,14},{3,15},{4,0},{5,1},{6,2},{7,3},{8,4},{9,5},{1... | collective-permute-start | bytes 393224 | tf_op jit(solution)/shard_map/ppermute | solution.py:46
  116.8 6.6 %collective-permute-start.27 = (bf16[512,128]{1,0:T(8,128)(2,1)S(1)}, bf16[512,128]{1,0:T(8,128)(2,1)S(1)}, u32[]{:S(2)}, u32[]{:S(2)}) collective-permute-start(bf16[512,128]{1,0:T(8,128)(2,1)S(1)} %get-tuple-element.110), channel_id=1, source_target_pairs={{0,8},{1,9},{2,10},{3,11},{4,12},{5,13},{6,14},{7,15},{8,0},{9,1},... | collective-permute-start | bytes 393224 | tf_op jit(solution)/shard_map/ppermute | solution.py:46
  126.5 7.9 %collective-permute-start.33 = (bf16[512,128]{1,0:T(8,128)(2,1)S(1)}, bf16[512,128]{1,0:T(8,128)(2,1)S(1)}, u32[]{:S(2)}, u32[]{:S(2)}) collective-permute-start(bf16[512,128]{1,0:T(8,128)(2,1)S(1)} %get-tuple-element.123), channel_id=1, source_target_pairs={{0,64},{1,65},{2,66},{3,67},{4,68},{5,69},{6,70},{7,71},{8,72},{9,... | collective-permute-start | bytes 393224 | tf_op jit(solution)/shard_map/ppermute | solution.py:46
  128.8 6.9 %collective-permute-start.32 = (bf16[512,128]{1,0:T(8,128)(2,1)S(1)}, bf16[512,128]{1,0:T(8,128)(2,1)S(1)}, u32[]{:S(2)}, u32[]{:S(2)}) collective-permute-start(bf16[512,128]{1,0:T(8,128)(2,1)S(1)} %get-tuple-element.123), channel_id=1, source_target_pairs={{0,96},{1,97},{2,98},{3,99},{4,100},{5,101},{6,102},{7,103},{8,104... | collective-permute-start | bytes 393224 | tf_op jit(solution)/shard_map/ppermute | solution.py:46
  129.9 6.7 %collective-permute-start.31 = (bf16[512,128]{1,0:T(8,128)(2,1)S(1)}, bf16[512,128]{1,0:T(8,128)(2,1)S(1)}, u32[]{:S(2)}, u32[]{:S(2)}) collective-permute-start(bf16[512,128]{1,0:T(8,128)(2,1)S(1)} %get-tuple-element.123), channel_id=1, source_target_pairs={{0,32},{1,33},{2,34},{3,35},{4,36},{5,37},{6,38},{7,39},{8,40},{9,... | collective-permute-start | bytes 393224 | tf_op jit(solution)/shard_map/ppermute | solution.py:46
  139.9 11.4 %collective-permute-start.34 = (bf16[512,128]{1,0:T(8,128)(2,1)S(1)}, bf16[512,128]{1,0:T(8,128)(2,1)S(1)}, u32[]{:S(2)}, u32[]{:S(2)}) collective-permute-start(bf16[512,128]{1,0:T(8,128)(2,1)S(1)} %coefficients.3.refs_3_), channel_id=1, source_target_pairs={{0,8},{1,9},{2,10},{3,11},{4,12},{5,13},{6,14},{7,15},{8,0},{9,1},... | collective-permute-start | bytes 393224 | tf_op jit(solution)/shard_map/ppermute | solution.py:46
  148.0 28.8 %collective-permute-start.38 = (bf16[4096,128]{1,0:T(8,128)(2,1)S(1)}, bf16[4096,128]{1,0:T(8,128)(2,1)S(1)}, u32[]{:S(2)}, u32[]{:S(2)}) collective-permute-start(bf16[4096,128]{1,0:T(8,128)(2,1)S(1)} %get-tuple-element.120), channel_id=1, source_target_pairs={{0,4},{1,5},{2,6},{3,7},{4,8},{5,9},{6,10},{7,11},{8,12},{9,13},{1... | collective-permute-start | bytes 3145736 | tf_op jit(solution)/shard_map/ppermute | solution.py:46
  148.1 26.8 %collective-permute-start.39 = (bf16[4096,128]{1,0:T(8,128)(2,1)S(1)}, bf16[4096,128]{1,0:T(8,128)(2,1)S(1)}, u32[]{:S(2)}, u32[]{:S(2)}) collective-permute-start(bf16[4096,128]{1,0:T(8,128)(2,1)S(1)} %get-tuple-element.121), channel_id=1, source_target_pairs={{0,12},{1,13},{2,14},{3,15},{4,0},{5,1},{6,2},{7,3},{8,4},{9,5},{1... | collective-permute-start | bytes 3145736 | tf_op jit(solution)/shard_map/ppermute | solution.py:46
  154.2 24.6 %collective-permute-start.35 = (bf16[4096,128]{1,0:T(8,128)(2,1)S(1)}, bf16[4096,128]{1,0:T(8,128)(2,1)S(1)}, u32[]{:S(2)}, u32[]{:S(2)}) collective-permute-start(bf16[4096,128]{1,0:T(8,128)(2,1)S(1)} %get-tuple-element.119), channel_id=1, source_target_pairs={{0,8},{1,9},{2,10},{3,11},{4,12},{5,13},{6,14},{7,15},{8,0},{9,1},... | collective-permute-start | bytes 3145736 | tf_op jit(solution)/shard_map/ppermute | solution.py:46
  (13 other events, 138.1 us)

commit v5 on v4

--- a/solution.py
+++ b/solution.py
@@ -358,9 +358,10 @@
     def moved(shifts, halves):
         return update(place, first_flat, second_flat, [w0[s] for s in shifts], [w1[s] for s in shifts], halves)
 
+    own, = moved((0,), 1)
     right, left = moved((1, 3), 1)
     right, left = send(right, along_u(-1)), send(left, along_u(1))
-    far, own = moved((2, 0), 1)
+    far, = moved((2,), 1)
     far = send(far, along_u(2))
     out = subtract(place, z_block, own, 0, 0, None)
     out = subtract(place, z_block, right, 1, 0, out)

time: 182 us -> 182 us (level)
  Pallas kernels: 35 us -> 37.9 us
  waiting for transfers between devices: 78.3 us -> 75.4 us
    ppermute x40, waiting for transfers between devices: 78.3 us -> 75.4 us  [send(): return lax.ppermute(value, AXES, pairs)]
    pallas_call x2 -> x3, Pallas kernels: 5.82 us -> 8.72 us  [update(): pl.pallas_call(functools.partial(update_kernel, count, nb // (RING * RING...]
  transfers between devices with their start and end apart: 40 -> 40, of which waited for: 25 -> 25; matrix products, arithmetic and copies ran while one was open for 5% -> 5% of each run, Pallas kernels for 12% -> 13%
where the time goes in v5:
time: 182 us; the launch traced here: 181 us
  waiting for transfers between devices  75.4 us (41%)
  starting transfers between devices  53.7 us (30%)
  Pallas kernels  37.9 us (21%)
  local copies, waits for them, and re-layouts  13.3 us (7%)
    ppermute x40, waiting for transfers between devices, send(): return lax.ppermute(value, AXES, pairs)  75.4 us
    ppermute x40, starting transfers between devices, send(): return lax.ppermute(value, AXES, pairs)  53.7 us
    pallas_call x2, Pallas kernels, sums(): pl.pallas_call(functools.partial(first_sums_kernel if flat is None else s...  10.7 us
    pallas_call x3, Pallas kernels, update(): pl.pallas_call(functools.partial(update_kernel, count, nb // (RING * RING...  8.72 us
    pallas_call x4, Pallas kernels, subtract(): pl.pallas_call(functools.partial(subtract_kernel, s), grid_spec=pltpu.Pre...  7.89 us
    convert_element_type x2, local copies, waits for them, and re-layouts, cut(): lax.dynamic_slice(z_in, (chunk(s) + start, 0), (size, z_block.shape[1]))  6.38 us
    pallas_call x2, Pallas kernels, transpose(): pl.pallas_call(transpose_kernel, grid=(rows // tile,), in_specs=[pl.Block...  6.18 us
  transfers between devices with their start and end apart: 40, of which 25 were waited for; matrix products, arithmetic and copies ran while one was open for 5% of the time, Pallas kernels for 13%

profile of v5, /device:TPU:0, one launch (start us, length us, event | category | flops | bytes accessed | tf_op | source)
XLA Modules:
  0.0 180.7 jit_solution(9104731385312244651)
XLA Ops:
  0.0 2.7 %constant_dynamic-slice_fusion = (bf16[64,4096]{1,0:T(8,128)(2,1)}, bf16[64,4096]{1,0:T(8,128)(2,1)}, bf16[64,4096]{1,0:T(8,128)(2,1)}, bf16[64,4096]{1,0:T(8,128)(2,1)S(1)}) fusion(bf16[64,16384]{1,0:T(8,128)(2,1)} %bitcast.14, s32[]{:T(128)S(6)} %select_n.78, s32[]{:T(128)S(6)} %select_n.76, s32[]{:T(128)S(6)} %select_n.74, s32[]{:T(128)S(6)} %select_n.72), kind=kLoop, calls=%fused_computation.9 | loop fusion | bytes 4194320 | tf_op jit(solution)/shard_map/dynamic_slice | solution.py:311
  4.4 2.9 %collective-permute-start.1 = (bf16[64,4096]{1,0:T(8,128)(2,1)}, bf16[64,4096]{1,0:T(8,128)(2,1)S(1)}, u32[]{:S(2)}, u32[]{:S(2)}) collective-permute-start(bf16[64,4096]{1,0:T(8,128)(2,1)} %get-tuple-element.64), channel_id=1, source_target_pairs={{0,8},{1,9},{2,10},{3,11},{4,12},{5,13},{6,14},{7,15},{8,0},{9,1},... | collective-permute-start | bytes 1572872 | tf_op jit(solution)/shard_map/ppermute | solution.py:46
  8.6 4.6 %dynamic-slice_convert_fusion = (bf16[4096,128]{1,0:T(8,128)(2,1)}, bf16[4096,128]{1,0:T(8,128)(2,1)}, bf16[4096,128]{1,0:T(8,128)(2,1)S(1)}) fusion(f32[16384,128]{1,0:T(8,128)} %z.7, s32[]{:T(128)S(6)} %select_n.78, s32[]{:T(128)S(6)} %select_n.74, s32[]{:T(128)S(6)} %select_n.72), kind=kLoop, calls=%fused_computation | loop fusion | bytes 6291468 | tf_op jit(solution)/shard_map/convert_element_type | solution.py:316
  15.3 2.9 %copy.7 = f32[2,512,512]{1,2,0:T(8,128)} copy(f32[2,512,512]{2,1,0:T(8,128)} %param.5) | data formatting | bytes 4194304 | tf_op jit(solution)/shard_map/optimization_barrier | solution.py:312
  18.2 2.1 %collective-permute-done.1.refs_2_ = bf16[64,4096]{1,0:T(8,128)(2,1)S(1)} collective-permute-done((bf16[64,4096]{1,0:T(8,128)(2,1)}, bf16[64,4096]{1,0:T(8,128)(2,1)S(1)}, u32[]{:S(2)}, u32[]{:S(2)}) %collective-permute-start.1) | collective-permute-done | bytes 524320 | tf_op jit(solution)/shard_map/ppermute | solution.py:46
  20.4 2.3 %stack_reflectors.1 = (bf16[128,4096]{1,0:T(8,128)(2,1)}, bf16[128,4096]{1,0:T(8,128)(2,1)S(1)}) custom-call(s32[3]{0:T(128)S(1)} %pad_add_fusion.place, bf16[64,4096]{1,0:T(8,128)(2,1)S(1)} %get-tuple-element.68.refs_0_, bf16[64,4096]{1,0:T(8,128)(2,1)S(1)} %collective-permute-done.refs_1_, bf16[64,4096]{1,0:T(8,128)(2,1)S(1)} %collective-permute-done.1.refs_2_, ...), custom_call_target="tpu_custom_call" | custom-call | bytes 4194304 | tf_op jit(solution)/shard_map/stack_reflectors/pallas_call | solution.py:79
  23.6 4.0 %collective-permute-start.5 = (bf16[128,4096]{1,0:T(8,128)(2,1)}, bf16[128,4096]{1,0:T(8,128)(2,1)S(1)}, u32[]{:S(2)}, u32[]{:S(2)}) collective-permute-start(bf16[128,4096]{1,0:T(8,128)(2,1)} %get-tuple-element.80.refs_0_), channel_id=1, source_target_pairs={{0,3},{1,0},{2,1},{3,2},{4,7},{5,4},{6,5},{7,6},{8,11},{9,8},{10,9... | collective-permute-start | bytes 3145736 | tf_op jit(solution)/shard_map/ppermute | solution.py:46
  29.4 6.3 %collective-permute-done.8.refs_9_ = bf16[4096,128]{1,0:T(8,128)(2,1)} collective-permute-done((bf16[4096,128]{1,0:T(8,128)(2,1)}, bf16[4096,128]{1,0:T(8,128)(2,1)}, u32[]{:S(2)}, u32[]{:S(2)}) %collective-permute-start.8) | collective-permute-done | bytes 1048608 | tf_op jit(solution)/shard_map/ppermute | solution.py:46
  35.8 2.6 %collective-permute-start.9 = (bf16[2048,128]{1,0:T(8,128)(2,1)S(1)}, bf16[2048,128]{1,0:T(8,128)(2,1)S(1)}, u32[]{:S(2)}, u32[]{:S(2)}) collective-permute-start(bf16[2048,128]{1,0:T(8,128)(2,1)S(1)} %get-tuple-element.75), channel_id=1, source_target_pairs={{0,4},{1,5},{2,6},{3,7},{4,8},{5,9},{6,10},{7,11},{8,12},{9,13},{1... | collective-permute-start | bytes 1572872 | tf_op jit(solution)/shard_map/ppermute | solution.py:46
  39.0 6.8 %collective-permute-done.5.refs_4_ = bf16[128,4096]{1,0:T(8,128)(2,1)S(1)} collective-permute-done((bf16[128,4096]{1,0:T(8,128)(2,1)}, bf16[128,4096]{1,0:T(8,128)(2,1)S(1)}, u32[]{:S(2)}, u32[]{:S(2)}) %collective-permute-start.5) | collective-permute-done | bytes 1048608 | tf_op jit(solution)/shard_map/ppermute | solution.py:46
  45.9 2.4 %collective-permute-start.6 = (bf16[64,4096]{1,0:T(8,128)(2,1)S(1)}, bf16[64,4096]{1,0:T(8,128)(2,1)S(1)}, u32[]{:S(2)}, u32[]{:S(2)}) collective-permute-start(bf16[64,4096]{1,0:T(8,128)(2,1)S(1)} %slice.25), channel_id=1, source_target_pairs={{0,3},{1,0},{2,1},{3,2},{4,7},{5,4},{6,5},{7,6},{8,11},{9,8},{10,9... | collective-permute-start | bytes 1572872 | tf_op jit(solution)/shard_map/ppermute | solution.py:46
  53.0 7.3 %collective-permute-done.6.refs_3_ = bf16[64,4096]{1,0:T(8,128)(2,1)S(1)} collective-permute-done((bf16[64,4096]{1,0:T(8,128)(2,1)S(1)}, bf16[64,4096]{1,0:T(8,128)(2,1)S(1)}, u32[]{:S(2)}, u32[]{:S(2)}) %collective-permute-start.6) | collective-permute-done | bytes 524320 | tf_op jit(solution)/shard_map/ppermute | solution.py:46
  60.2 4.4 %collective-permute-done.4.refs_2_ = bf16[64,4096]{1,0:T(8,128)(2,1)S(1)} collective-permute-done((bf16[64,4096]{1,0:T(8,128)(2,1)S(1)}, bf16[64,4096]{1,0:T(8,128)(2,1)S(1)}, u32[]{:S(2)}, u32[]{:S(2)}) %collective-permute-start.4) | collective-permute-done | bytes 524320 | tf_op jit(solution)/shard_map/ppermute | solution.py:46
  64.6 4.4 %panel_sums.2 = (f32[512,128]{1,0:T(8,128)S(1)}, bf16[512,128]{1,0:T(8,128)(2,1)S(1)}, bf16[512,128]{1,0:T(8,128)(2,1)S(1)}, bf16[512,128]{1,0:T(8,128)(2,1)S(1)}) custom-call(s32[3]{0:T(128)S(1)} %pad_add_fusion.place, bf16[128,4096]{1,0:T(8,128)(2,1)} %get-tuple-element.80.refs_0_, bf16[128,4096]{1,0:T(8,128)(2,1)S(1)} %collective-permute-done.3.refs_1_, ...), custom_call_target="tpu_custom_call" | custom-call | flops 2147483648 | bytes 8388608 | tf_op jit(solution)/shard_map/panel_sums/pallas_call | solution.py:191
  69.0 2.8 %collective-permute-start.18 = (bf16[128,4096]{1,0:T(8,128)(2,1)S(1)}, bf16[128,4096]{1,0:T(8,128)(2,1)S(1)}, u32[]{:S(2)}, u32[]{:S(2)}) collective-permute-start(bf16[128,4096]{1,0:T(8,128)(2,1)S(1)} %copy-done.1), channel_id=1, source_target_pairs={{0,3},{1,0},{2,1},{3,2},{4,7},{5,4},{6,5},{7,6},{8,11},{9,8},{10,9... | collective-permute-start | bytes 3145736 | tf_op jit(solution)/shard_map/ppermute | solution.py:46
  75.6 3.6 %transpose_reflectors.2.refs_10_.first = bf16[4096,512]{1,0:T(8,128)(2,1)S(1)} custom-call(bf16[128,4096]{1,0:T(8,128)(2,1)} %get-tuple-element.80.refs_0_, bf16[128,4096]{1,0:T(8,128)(2,1)S(1)} %collective-permute-done.3.refs_1_, bf16[64,4096]{1,0:T(8,128)(2,1)S(1)} %collective-permute-done.4.refs_2_, bf16[64,4096]{1,0:T(8,128)(2,1)S(1)} %collective-permute-done.6.refs_3_, ...), custom_call_target="tpu_custom_call" | custom-call | bytes 8388608 | tf_op jit(solution)/shard_map/transpose_reflectors/pallas_call | solution.py:106
  83.0 3.2 %collective-permute-done.18.refs_4_ = bf16[128,4096]{1,0:T(8,128)(2,1)S(1)} collective-permute-done((bf16[128,4096]{1,0:T(8,128)(2,1)S(1)}, bf16[128,4096]{1,0:T(8,128)(2,1)S(1)}, u32[]{:S(2)}, u32[]{:S(2)}) %collective-permute-start.18) | collective-permute-done | bytes 1048608 | tf_op jit(solution)/shard_map/ppermute | solution.py:46
  86.3 3.3 %collective-permute-start.19 = (bf16[64,4096]{1,0:T(8,128)(2,1)S(1)}, bf16[64,4096]{1,0:T(8,128)(2,1)S(1)}, u32[]{:S(2)}, u32[]{:S(2)}) collective-permute-start(bf16[64,4096]{1,0:T(8,128)(2,1)S(1)} %slice.27), channel_id=1, source_target_pairs={{0,3},{1,0},{2,1},{3,2},{4,7},{5,4},{6,5},{7,6},{8,11},{9,8},{10,9... | collective-permute-start | bytes 1572872 | tf_op jit(solution)/shard_map/ppermute | solution.py:46
  89.7 3.2 %collective-permute-start.23 = (bf16[512,128]{1,0:T(8,128)(2,1)S(1)}, bf16[512,128]{1,0:T(8,128)(2,1)S(1)}, u32[]{:S(2)}, u32[]{:S(2)}) collective-permute-start(bf16[512,128]{1,0:T(8,128)(2,1)S(1)} %get-tuple-element.121), channel_id=1, source_target_pairs={{0,64},{1,65},{2,66},{3,67},{4,68},{5,69},{6,70},{7,71},{8,72},{9,... | collective-permute-start | bytes 393224 | tf_op jit(solution)/shard_map/ppermute | solution.py:46
  95.1 2.4 %collective-permute-done.23.d = bf16[512,128]{1,0:T(8,128)(2,1)S(1)} collective-permute-done((bf16[512,128]{1,0:T(8,128)(2,1)S(1)}, bf16[512,128]{1,0:T(8,128)(2,1)S(1)}, u32[]{:S(2)}, u32[]{:S(2)}) %collective-permute-start.23) | collective-permute-done | bytes 131104 | tf_op jit(solution)/shard_map/ppermute | solution.py:46
  102.3 2.0 %collective-permute-start.25 = (bf16[512,128]{1,0:T(8,128)(2,1)S(1)}, bf16[512,128]{1,0:T(8,128)(2,1)S(1)}, u32[]{:S(2)}, u32[]{:S(2)}) collective-permute-start(bf16[512,128]{1,0:T(8,128)(2,1)S(1)} %coefficients.2.refs_11_.refs_0_), channel_id=1, source_target_pairs={{0,12},{1,13},{2,14},{3,15},{4,0},{5,1},{6,2},{7,3},{8,4},{9,5},{1... | collective-permute-start | bytes 393224 | tf_op jit(solution)/shard_map/ppermute | solution.py:46
  104.6 3.2 %collective-permute-done.26.refs_14_.refs_0_ = bf16[512,128]{1,0:T(8,128)(2,1)S(1)} collective-permute-done((bf16[512,128]{1,0:T(8,128)(2,1)S(1)}, bf16[512,128]{1,0:T(8,128)(2,1)S(1)}, u32[]{:S(2)}, u32[]{:S(2)}) %collective-permute-start.26) | collective-permute-done | bytes 131104 | tf_op jit(solution)/shard_map/ppermute | solution.py:46
  110.5 6.3 %panel_sums.3 = (f32[512,128]{1,0:T(8,128)S(1)}, bf16[512,128]{1,0:T(8,128)(2,1)S(1)}, bf16[512,128]{1,0:T(8,128)(2,1)S(1)}, bf16[512,128]{1,0:T(8,128)(2,1)S(1)}) custom-call(s32[3]{0:T(128)S(1)} %pad_add_fusion.place, bf16[128,4096]{1,0:T(8,128)(2,1)S(1)} %copy-done.1, bf16[128,4096]{1,0:T(8,128)(2,1)S(1)} %collective-permute-done.16.refs_1_, ...), custom_call_target="tpu_custom_call" | custom-call | flops 4294967296 | bytes 8388608 | tf_op jit(solution)/shard_map/panel_sums/pallas_call | solution.py:191
  120.1 2.5 %transpose_reflectors.3.second = bf16[4096,512]{1,0:T(8,128)(2,1)S(1)} custom-call(bf16[128,4096]{1,0:T(8,128)(2,1)S(1)} %copy-done.1, bf16[128,4096]{1,0:T(8,128)(2,1)S(1)} %collective-permute-done.16.refs_1_, bf16[64,4096]{1,0:T(8,128)(2,1)S(1)} %collective-permute-done.17.refs_2_, bf16[64,4096]{1,0:T(8,128)(2,1)S(1)} %collective-permute-done.19.refs_3_, ...), custom_call_target="tpu_custom_call" | custom-call | bytes 8388608 | tf_op jit(solution)/shard_map/transpose_reflectors/pallas_call | solution.py:106
  126.6 2.2 %collective-permute-start.33 = (bf16[512,128]{1,0:T(8,128)(2,1)S(1)}, bf16[512,128]{1,0:T(8,128)(2,1)S(1)}, u32[]{:S(2)}, u32[]{:S(2)}) collective-permute-start(bf16[512,128]{1,0:T(8,128)(2,1)S(1)} %get-tuple-element.119), channel_id=1, source_target_pairs={{0,64},{1,65},{2,66},{3,67},{4,68},{5,69},{6,70},{7,71},{8,72},{9,... | collective-permute-start | bytes 393224 | tf_op jit(solution)/shard_map/ppermute | solution.py:46
  130.8 3.7 %collective-permute-done.33.d = bf16[512,128]{1,0:T(8,128)(2,1)S(1)} collective-permute-done((bf16[512,128]{1,0:T(8,128)(2,1)S(1)}, bf16[512,128]{1,0:T(8,128)(2,1)S(1)}, u32[]{:S(2)}, u32[]{:S(2)}) %collective-permute-start.33) | collective-permute-done | bytes 131104 | tf_op jit(solution)/shard_map/ppermute | solution.py:46
  142.8 2.2 %collective-permute-done.36.refs_2_ = bf16[512,128]{1,0:T(8,128)(2,1)S(1)} collective-permute-done((bf16[512,128]{1,0:T(8,128)(2,1)S(1)}, bf16[512,128]{1,0:T(8,128)(2,1)S(1)}, u32[]{:S(2)}, u32[]{:S(2)}) %collective-permute-start.36) | collective-permute-done | bytes 131104 | tf_op jit(solution)/shard_map/ppermute | solution.py:46
  145.0 2.9 %update.4 = (bf16[4096,128]{1,0:T(8,128)(2,1)S(1)}, bf16[4096,128]{1,0:T(8,128)(2,1)S(1)}) custom-call(s32[3]{0:T(128)S(1)} %pad_add_fusion.place, bf16[4096,512]{1,0:T(8,128)(2,1)S(1)} %transpose_reflectors.2.refs_10_.first, bf16[4096,512]{1,0:T(8,128)(2,1)S(1)} %transpose_reflectors.3.second, ...), custom_call_target="tpu_custom_call" | custom-call | flops 2147483648 | bytes 8388608 | tf_op jit(solution)/shard_map/update/pallas_call | solution.py:246
  148.0 3.2 %collective-permute-start.39 = (bf16[4096,128]{1,0:T(8,128)(2,1)S(1)}, bf16[4096,128]{1,0:T(8,128)(2,1)S(1)}, u32[]{:S(2)}, u32[]{:S(2)}) collective-permute-start(bf16[4096,128]{1,0:T(8,128)(2,1)S(1)} %get-tuple-element.118), channel_id=1, source_target_pairs={{0,12},{1,13},{2,14},{3,15},{4,0},{5,1},{6,2},{7,3},{8,4},{9,5},{1... | collective-permute-start | bytes 3145736 | tf_op jit(solution)/shard_map/ppermute | solution.py:46
  151.2 2.9 %update.3 = bf16[4096,128]{1,0:T(8,128)(2,1)S(1)} custom-call(s32[3]{0:T(128)S(1)} %pad_add_fusion.place, bf16[4096,512]{1,0:T(8,128)(2,1)S(1)} %transpose_reflectors.2.refs_10_.first, bf16[4096,512]{1,0:T(8,128)(2,1)S(1)} %transpose_reflectors.3.second, bf16[512,128]{1,0:T(8,128)(2,1)S(1)} %collective-permute-done.26.refs_14_.refs_0_, ...), custom_call_target="tpu_custom_call" | custom-call | flops 1073741824 | bytes 8388608 | tf_op jit(solution)/shard_map/update/pallas_call | solution.py:246
  154.3 2.9 %update.5.moved = bf16[4096,128]{1,0:T(8,128)(2,1)S(1)} custom-call(s32[3]{0:T(128)S(1)} %pad_add_fusion.place, bf16[4096,512]{1,0:T(8,128)(2,1)S(1)} %transpose_reflectors.2.refs_10_.first, bf16[4096,512]{1,0:T(8,128)(2,1)S(1)} %transpose_reflectors.3.second, bf16[512,128]{1,0:T(8,128)(2,1)S(1)} %coefficients.2.refs_11_.refs_0_, ...), custom_call_target="tpu_custom_call" | custom-call | flops 1073741824 | bytes 8388608 | tf_op jit(solution)/shard_map/update/pallas_call | solution.py:246
  159.2 15.6 %collective-permute-done.39.moved = bf16[4096,128]{1,0:T(8,128)(2,1)S(1)} collective-permute-done((bf16[4096,128]{1,0:T(8,128)(2,1)S(1)}, bf16[4096,128]{1,0:T(8,128)(2,1)S(1)}, u32[]{:S(2)}, u32[]{:S(2)}) %collective-permute-start.39) | collective-permute-done | bytes 1048608 | tf_op jit(solution)/shard_map/ppermute | solution.py:46
  (87 shorter events, 56.4 us)
Async XLA Ops:
  2.7 15.5 %collective-permute-start = (bf16[64,4096]{1,0:T(8,128)(2,1)}, bf16[64,4096]{1,0:T(8,128)(2,1)S(1)}, u32[]{:S(2)}, u32[]{:S(2)}) collective-permute-start(bf16[64,4096]{1,0:T(8,128)(2,1)} %get-tuple-element.63), channel_id=1, source_target_pairs={{0,4},{1,5},{2,6},{3,7},{4,8},{5,9},{6,10},{7,11},{8,12},{9,13},{1... | collective-permute-start | bytes 1572872 | tf_op jit(solution)/shard_map/ppermute | solution.py:46
  4.4 16.0 %collective-permute-start.1 = (bf16[64,4096]{1,0:T(8,128)(2,1)}, bf16[64,4096]{1,0:T(8,128)(2,1)S(1)}, u32[]{:S(2)}, u32[]{:S(2)}) collective-permute-start(bf16[64,4096]{1,0:T(8,128)(2,1)} %get-tuple-element.64), channel_id=1, source_target_pairs={{0,8},{1,9},{2,10},{3,11},{4,12},{5,13},{6,14},{7,15},{8,0},{9,1},... | collective-permute-start | bytes 1572872 | tf_op jit(solution)/shard_map/ppermute | solution.py:46
  7.3 13.1 %collective-permute-start.2 = (bf16[64,4096]{1,0:T(8,128)(2,1)}, bf16[64,4096]{1,0:T(8,128)(2,1)S(1)}, u32[]{:S(2)}, u32[]{:S(2)}) collective-permute-start(bf16[64,4096]{1,0:T(8,128)(2,1)} %get-tuple-element.65), channel_id=1, source_target_pairs={{0,12},{1,13},{2,14},{3,15},{4,0},{5,1},{6,2},{7,3},{8,4},{9,5},{1... | collective-permute-start | bytes 1572872 | tf_op jit(solution)/shard_map/ppermute | solution.py:46
  13.2 22.5 %collective-permute-start.8 = (bf16[4096,128]{1,0:T(8,128)(2,1)}, bf16[4096,128]{1,0:T(8,128)(2,1)}, u32[]{:S(2)}, u32[]{:S(2)}) collective-permute-start(bf16[4096,128]{1,0:T(8,128)(2,1)} %get-tuple-element.125), channel_id=1, source_target_pairs={{0,12},{1,13},{2,14},{3,15},{4,0},{5,1},{6,2},{7,3},{8,4},{9,5},{1... | collective-permute-start | bytes 3145736 | tf_op jit(solution)/shard_map/ppermute | solution.py:46
  13.2 22.5 %collective-permute-start.7 = (bf16[4096,128]{1,0:T(8,128)(2,1)}, bf16[4096,128]{1,0:T(8,128)(2,1)}, u32[]{:S(2)}, u32[]{:S(2)}) collective-permute-start(bf16[4096,128]{1,0:T(8,128)(2,1)} %get-tuple-element.126), channel_id=1, source_target_pairs={{0,4},{1,5},{2,6},{3,7},{4,8},{5,9},{6,10},{7,11},{8,12},{9,13},{1... | collective-permute-start | bytes 3145736 | tf_op jit(solution)/shard_map/ppermute | solution.py:46
  23.6 22.2 %collective-permute-start.5 = (bf16[128,4096]{1,0:T(8,128)(2,1)}, bf16[128,4096]{1,0:T(8,128)(2,1)S(1)}, u32[]{:S(2)}, u32[]{:S(2)}) collective-permute-start(bf16[128,4096]{1,0:T(8,128)(2,1)} %get-tuple-element.80.refs_0_), channel_id=1, source_target_pairs={{0,3},{1,0},{2,1},{3,2},{4,7},{5,4},{6,5},{7,6},{8,11},{9,8},{10,9... | collective-permute-start | bytes 3145736 | tf_op jit(solution)/shard_map/ppermute | solution.py:46
  27.7 21.8 %collective-permute-start.3 = (bf16[128,4096]{1,0:T(8,128)(2,1)}, bf16[128,4096]{1,0:T(8,128)(2,1)S(1)}, u32[]{:S(2)}, u32[]{:S(2)}) collective-permute-start(bf16[128,4096]{1,0:T(8,128)(2,1)} %get-tuple-element.80.refs_0_), channel_id=1, source_target_pairs={{0,1},{1,2},{2,3},{3,0},{4,5},{5,6},{6,7},{7,4},{8,9},{9,10},{10,1... | collective-permute-start | bytes 3145736 | tf_op jit(solution)/shard_map/ppermute | solution.py:46
  35.8 13.8 %collective-permute-start.9 = (bf16[2048,128]{1,0:T(8,128)(2,1)S(1)}, bf16[2048,128]{1,0:T(8,128)(2,1)S(1)}, u32[]{:S(2)}, u32[]{:S(2)}) collective-permute-start(bf16[2048,128]{1,0:T(8,128)(2,1)S(1)} %get-tuple-element.75), channel_id=1, source_target_pairs={{0,4},{1,5},{2,6},{3,7},{4,8},{5,9},{6,10},{7,11},{8,12},{9,13},{1... | collective-permute-start | bytes 1572872 | tf_op jit(solution)/shard_map/ppermute | solution.py:46
  38.4 12.7 %collective-permute-start.11 = (bf16[2048,128]{1,0:T(8,128)(2,1)S(1)}, bf16[2048,128]{1,0:T(8,128)(2,1)S(1)}, u32[]{:S(2)}, u32[]{:S(2)}) collective-permute-start(bf16[2048,128]{1,0:T(8,128)(2,1)S(1)} %get-tuple-element.76), channel_id=1, source_target_pairs={{0,12},{1,13},{2,14},{3,15},{4,0},{5,1},{6,2},{7,3},{8,4},{9,5},{1... | collective-permute-start | bytes 1572872 | tf_op jit(solution)/shard_map/ppermute | solution.py:46
  45.9 14.3 %collective-permute-start.6 = (bf16[64,4096]{1,0:T(8,128)(2,1)S(1)}, bf16[64,4096]{1,0:T(8,128)(2,1)S(1)}, u32[]{:S(2)}, u32[]{:S(2)}) collective-permute-start(bf16[64,4096]{1,0:T(8,128)(2,1)S(1)} %slice.25), channel_id=1, source_target_pairs={{0,3},{1,0},{2,1},{3,2},{4,7},{5,4},{6,5},{7,6},{8,11},{9,8},{10,9... | collective-permute-start | bytes 1572872 | tf_op jit(solution)/shard_map/ppermute | solution.py:46
  49.5 15.1 %collective-permute-start.4 = (bf16[64,4096]{1,0:T(8,128)(2,1)S(1)}, bf16[64,4096]{1,0:T(8,128)(2,1)S(1)}, u32[]{:S(2)}, u32[]{:S(2)}) collective-permute-start(bf16[64,4096]{1,0:T(8,128)(2,1)S(1)} %slice.24), channel_id=1, source_target_pairs={{0,1},{1,2},{2,3},{3,0},{4,5},{5,6},{6,7},{7,4},{8,9},{9,10},{10,1... | collective-permute-start | bytes 1572872 | tf_op jit(solution)/shard_map/ppermute | solution.py:46
  49.6 15.0 %collective-permute-start.10 = (bf16[2048,128]{1,0:T(8,128)(2,1)S(1)}, bf16[2048,128]{1,0:T(8,128)(2,1)S(1)}, u32[]{:S(2)}, u32[]{:S(2)}) collective-permute-start(bf16[2048,128]{1,0:T(8,128)(2,1)S(1)} %collective-permute-done.9), channel_id=1, source_target_pairs={{0,4},{1,5},{2,6},{3,7},{4,8},{5,9},{6,10},{7,11},{8,12},{9,13},{1... | collective-permute-start | bytes 1572872 | tf_op jit(solution)/shard_map/ppermute | solution.py:46
  51.1 13.5 %collective-permute-start.12 = (bf16[2048,128]{1,0:T(8,128)(2,1)S(1)}, bf16[2048,128]{1,0:T(8,128)(2,1)S(1)}, u32[]{:S(2)}, u32[]{:S(2)}) collective-permute-start(bf16[2048,128]{1,0:T(8,128)(2,1)S(1)} %collective-permute-done.11), channel_id=1, source_target_pairs={{0,12},{1,13},{2,14},{3,15},{4,0},{5,1},{6,2},{7,3},{8,4},{9,5},{1... | collective-permute-start | bytes 1572872 | tf_op jit(solution)/shard_map/ppermute | solution.py:46
  69.0 17.2 %collective-permute-start.18 = (bf16[128,4096]{1,0:T(8,128)(2,1)S(1)}, bf16[128,4096]{1,0:T(8,128)(2,1)S(1)}, u32[]{:S(2)}, u32[]{:S(2)}) collective-permute-start(bf16[128,4096]{1,0:T(8,128)(2,1)S(1)} %copy-done.1), channel_id=1, source_target_pairs={{0,3},{1,0},{2,1},{3,2},{4,7},{5,4},{6,5},{7,6},{8,11},{9,8},{10,9... | collective-permute-start | bytes 3145736 | tf_op jit(solution)/shard_map/ppermute | solution.py:46
  71.9 17.7 %collective-permute-start.16 = (bf16[128,4096]{1,0:T(8,128)(2,1)S(1)}, bf16[128,4096]{1,0:T(8,128)(2,1)S(1)}, u32[]{:S(2)}, u32[]{:S(2)}) collective-permute-start(bf16[128,4096]{1,0:T(8,128)(2,1)S(1)} %copy-done.1), channel_id=1, source_target_pairs={{0,1},{1,2},{2,3},{3,0},{4,5},{5,6},{6,7},{7,4},{8,9},{9,10},{10,1... | collective-permute-start | bytes 3145736 | tf_op jit(solution)/shard_map/ppermute | solution.py:46
  71.9 7.9 %collective-permute-start.13 = (bf16[512,128]{1,0:T(8,128)(2,1)S(1)}, bf16[512,128]{1,0:T(8,128)(2,1)S(1)}, u32[]{:S(2)}, u32[]{:S(2)}) collective-permute-start(bf16[512,128]{1,0:T(8,128)(2,1)S(1)} %get-tuple-element.96), channel_id=1, source_target_pairs={{0,8},{1,9},{2,10},{3,11},{4,12},{5,13},{6,14},{7,15},{8,0},{9,1},... | collective-permute-start | bytes 393224 | tf_op jit(solution)/shard_map/ppermute | solution.py:46
  73.6 7.5 %collective-permute-start.14 = (bf16[512,128]{1,0:T(8,128)(2,1)S(1)}, bf16[512,128]{1,0:T(8,128)(2,1)S(1)}, u32[]{:S(2)}, u32[]{:S(2)}) collective-permute-start(bf16[512,128]{1,0:T(8,128)(2,1)S(1)} %get-tuple-element.97), channel_id=1, source_target_pairs={{0,12},{1,13},{2,14},{3,15},{4,0},{5,1},{6,2},{7,3},{8,4},{9,5},{1... | collective-permute-start | bytes 393224 | tf_op jit(solution)/shard_map/ppermute | solution.py:46
  75.2 7.6 %collective-permute-start.15 = (bf16[512,128]{1,0:T(8,128)(2,1)S(1)}, bf16[512,128]{1,0:T(8,128)(2,1)S(1)}, u32[]{:S(2)}, u32[]{:S(2)}) collective-permute-start(bf16[512,128]{1,0:T(8,128)(2,1)S(1)} %get-tuple-element.98), channel_id=1, source_target_pairs={{0,4},{1,5},{2,6},{3,7},{4,8},{5,9},{6,10},{7,11},{8,12},{9,13},{1... | collective-permute-start | bytes 393224 | tf_op jit(solution)/shard_map/ppermute | solution.py:46
  82.9 6.7 %collective-permute-start.20 = (f32[512,128]{1,0:T(8,128)S(1)}, f32[512,128]{1,0:T(8,128)S(1)}, u32[]{:S(2)}, u32[]{:S(2)}) collective-permute-start(f32[512,128]{1,0:T(8,128)S(1)} %convert_add_fusion.1), channel_id=1, source_target_pairs={{0,16},{1,17},{2,18},{3,19},{4,20},{5,21},{6,22},{7,23},{8,24},{9,... | collective-permute-start | bytes 786440 | tf_op jit(solution)/shard_map/ppermute | solution.py:46
  86.3 24.2 %collective-permute-start.19 = (bf16[64,4096]{1,0:T(8,128)(2,1)S(1)}, bf16[64,4096]{1,0:T(8,128)(2,1)S(1)}, u32[]{:S(2)}, u32[]{:S(2)}) collective-permute-start(bf16[64,4096]{1,0:T(8,128)(2,1)S(1)} %slice.27), channel_id=1, source_target_pairs={{0,3},{1,0},{2,1},{3,2},{4,7},{5,4},{6,5},{7,6},{8,11},{9,8},{10,9... | collective-permute-start | bytes 1572872 | tf_op jit(solution)/shard_map/ppermute | solution.py:46
  89.6 20.9 %collective-permute-start.17 = (bf16[64,4096]{1,0:T(8,128)(2,1)S(1)}, bf16[64,4096]{1,0:T(8,128)(2,1)S(1)}, u32[]{:S(2)}, u32[]{:S(2)}) collective-permute-start(bf16[64,4096]{1,0:T(8,128)(2,1)S(1)} %slice.26), channel_id=1, source_target_pairs={{0,1},{1,2},{2,3},{3,0},{4,5},{5,6},{6,7},{7,4},{8,9},{9,10},{10,1... | collective-permute-start | bytes 1572872 | tf_op jit(solution)/shard_map/ppermute | solution.py:46
  89.7 7.8 %collective-permute-start.23 = (bf16[512,128]{1,0:T(8,128)(2,1)S(1)}, bf16[512,128]{1,0:T(8,128)(2,1)S(1)}, u32[]{:S(2)}, u32[]{:S(2)}) collective-permute-start(bf16[512,128]{1,0:T(8,128)(2,1)S(1)} %get-tuple-element.121), channel_id=1, source_target_pairs={{0,64},{1,65},{2,66},{3,67},{4,68},{5,69},{6,70},{7,71},{8,72},{9,... | collective-permute-start | bytes 393224 | tf_op jit(solution)/shard_map/ppermute | solution.py:46
  101.3 6.6 %collective-permute-start.26 = (bf16[512,128]{1,0:T(8,128)(2,1)S(1)}, bf16[512,128]{1,0:T(8,128)(2,1)S(1)}, u32[]{:S(2)}, u32[]{:S(2)}) collective-permute-start(bf16[512,128]{1,0:T(8,128)(2,1)S(1)} %coefficients.2.refs_11_.refs_0_), channel_id=1, source_target_pairs={{0,8},{1,9},{2,10},{3,11},{4,12},{5,13},{6,14},{7,15},{8,0},{9,1},... | collective-permute-start | bytes 393224 | tf_op jit(solution)/shard_map/ppermute | solution.py:46
  102.3 6.7 %collective-permute-start.25 = (bf16[512,128]{1,0:T(8,128)(2,1)S(1)}, bf16[512,128]{1,0:T(8,128)(2,1)S(1)}, u32[]{:S(2)}, u32[]{:S(2)}) collective-permute-start(bf16[512,128]{1,0:T(8,128)(2,1)S(1)} %coefficients.2.refs_11_.refs_0_), channel_id=1, source_target_pairs={{0,12},{1,13},{2,14},{3,15},{4,0},{5,1},{6,2},{7,3},{8,4},{9,5},{1... | collective-permute-start | bytes 393224 | tf_op jit(solution)/shard_map/ppermute | solution.py:46
  116.8 6.6 %collective-permute-start.27 = (bf16[512,128]{1,0:T(8,128)(2,1)S(1)}, bf16[512,128]{1,0:T(8,128)(2,1)S(1)}, u32[]{:S(2)}, u32[]{:S(2)}) collective-permute-start(bf16[512,128]{1,0:T(8,128)(2,1)S(1)} %get-tuple-element.108), channel_id=1, source_target_pairs={{0,8},{1,9},{2,10},{3,11},{4,12},{5,13},{6,14},{7,15},{8,0},{9,1},... | collective-permute-start | bytes 393224 | tf_op jit(solution)/shard_map/ppermute | solution.py:46
  126.6 7.9 %collective-permute-start.33 = (bf16[512,128]{1,0:T(8,128)(2,1)S(1)}, bf16[512,128]{1,0:T(8,128)(2,1)S(1)}, u32[]{:S(2)}, u32[]{:S(2)}) collective-permute-start(bf16[512,128]{1,0:T(8,128)(2,1)S(1)} %get-tuple-element.119), channel_id=1, source_target_pairs={{0,64},{1,65},{2,66},{3,67},{4,68},{5,69},{6,70},{7,71},{8,72},{9,... | collective-permute-start | bytes 393224 | tf_op jit(solution)/shard_map/ppermute | solution.py:46
  128.7 6.9 %collective-permute-start.32 = (bf16[512,128]{1,0:T(8,128)(2,1)S(1)}, bf16[512,128]{1,0:T(8,128)(2,1)S(1)}, u32[]{:S(2)}, u32[]{:S(2)}) collective-permute-start(bf16[512,128]{1,0:T(8,128)(2,1)S(1)} %get-tuple-element.119), channel_id=1, source_target_pairs={{0,96},{1,97},{2,98},{3,99},{4,100},{5,101},{6,102},{7,103},{8,104... | collective-permute-start | bytes 393224 | tf_op jit(solution)/shard_map/ppermute | solution.py:46
  129.9 6.8 %collective-permute-start.31 = (bf16[512,128]{1,0:T(8,128)(2,1)S(1)}, bf16[512,128]{1,0:T(8,128)(2,1)S(1)}, u32[]{:S(2)}, u32[]{:S(2)}) collective-permute-start(bf16[512,128]{1,0:T(8,128)(2,1)S(1)} %get-tuple-element.119), channel_id=1, source_target_pairs={{0,32},{1,33},{2,34},{3,35},{4,36},{5,37},{6,38},{7,39},{8,40},{9,... | collective-permute-start | bytes 393224 | tf_op jit(solution)/shard_map/ppermute | solution.py:46
  139.9 11.4 %collective-permute-start.34 = (bf16[512,128]{1,0:T(8,128)(2,1)S(1)}, bf16[512,128]{1,0:T(8,128)(2,1)S(1)}, u32[]{:S(2)}, u32[]{:S(2)}) collective-permute-start(bf16[512,128]{1,0:T(8,128)(2,1)S(1)} %coefficients.3.refs_1_), channel_id=1, source_target_pairs={{0,8},{1,9},{2,10},{3,11},{4,12},{5,13},{6,14},{7,15},{8,0},{9,1},... | collective-permute-start | bytes 393224 | tf_op jit(solution)/shard_map/ppermute | solution.py:46
  147.9 28.8 %collective-permute-start.38 = (bf16[4096,128]{1,0:T(8,128)(2,1)S(1)}, bf16[4096,128]{1,0:T(8,128)(2,1)S(1)}, u32[]{:S(2)}, u32[]{:S(2)}) collective-permute-start(bf16[4096,128]{1,0:T(8,128)(2,1)S(1)} %get-tuple-element.117), channel_id=1, source_target_pairs={{0,4},{1,5},{2,6},{3,7},{4,8},{5,9},{6,10},{7,11},{8,12},{9,13},{1... | collective-permute-start | bytes 3145736 | tf_op jit(solution)/shard_map/ppermute | solution.py:46
  148.0 26.8 %collective-permute-start.39 = (bf16[4096,128]{1,0:T(8,128)(2,1)S(1)}, bf16[4096,128]{1,0:T(8,128)(2,1)S(1)}, u32[]{:S(2)}, u32[]{:S(2)}) collective-permute-start(bf16[4096,128]{1,0:T(8,128)(2,1)S(1)} %get-tuple-element.118), channel_id=1, source_target_pairs={{0,12},{1,13},{2,14},{3,15},{4,0},{5,1},{6,2},{7,3},{8,4},{9,5},{1... | collective-permute-start | bytes 3145736 | tf_op jit(solution)/shard_map/ppermute | solution.py:46
  154.2 24.6 %collective-permute-start.35 = (bf16[4096,128]{1,0:T(8,128)(2,1)S(1)}, bf16[4096,128]{1,0:T(8,128)(2,1)S(1)}, u32[]{:S(2)}, u32[]{:S(2)}) collective-permute-start(bf16[4096,128]{1,0:T(8,128)(2,1)S(1)} %update.3), channel_id=1, source_target_pairs={{0,8},{1,9},{2,10},{3,11},{4,12},{5,13},{6,14},{7,15},{8,0},{9,1},... | collective-permute-start | bytes 3145736 | tf_op jit(solution)/shard_map/ppermute | solution.py:46
  (13 other events, 127.4 us)
